TPU v7x, 32 devices: a whole 2x2x4 slice. The times are simulated.
32 devices in a mesh: row: 4 (over z), col: 8 (over y, x, core).
Axes of the slice: x: 2, y: 2, z: 4, core: 2. Of those that a mesh axis runs over, the one named last changes fastest.
Arguments:
- positions: float32 [3, 16, 16, 16, 128], P(None, 'row', 'col'), may hold values from 0.5 to 7.5
- torques: float32 [3, 16, 16, 16, 128], P(None, 'row', 'col'), may hold values from -6 to 6
- counts: int32 [16, 16, 16], P('row', 'col'), may hold values from 42 to 128
- neighbour_flags: int32 [6, 16, 16, 16], P(None, 'row', 'col'), may hold values 0 or 1
Outputs:
- moved_positions: float32 [3, 16, 16, 16, 128], P(None, 'row', 'col')
- spin: float32 [3, 16, 16, 16, 128], P(None, 'row', 'col')
Inputs may be any that keep to these rules, and one draw needn't show every extreme that they name: `counts`: number of occupied slots of each cell block; slots at or past it hold no particle. `neighbour_flags`: entry f of a block is 1 where its neighbour at the f-th face offset (+x, -x, +y, -y, +z, -z) acts on it, else 0.
All inputs are finite; a program needn't handle non-finite values.
Results may differ from a plain program's by a relative error of at most 0.0003.
Values sent between devices are 32-bit elements; how exact they have to be, the bound alone decides.
No kernel may reach another device: no remote copies, remote signals or barrier semaphores. Data moves between devices by JAX's collectives and lax.ppermute only.
A program may use at most 192 MiB of HBM per device.

v0:
```python
import math

import jax
import jax.numpy as jnp
from jax import lax
from jax.sharding import PartitionSpec as P

GRID = 128
CELL = 8
STEPS = 3


highest = lax.Precision.HIGHEST
step_pace = 0.06
drift_gain = 1.0
couple_gain = 0.5
bin_rate = 1.0
face_moves = ((0, 1.0), (0, -1.0), (1, 1.0), (1, -1.0), (2, 1.0), (2, -1.0))


def with_halo(block, sides, width):
    for axis, dim in sides:
        count = lax.axis_size(axis)
        forward = [(i, i + 1) for i in range(count - 1)]
        forward.append((count - 1, 0))
        backward = [(target, source) for source, target in forward]
        low = lax.ppermute(
            lax.slice_in_dim(block, block.shape[dim] - width, None, axis=dim), axis, forward
        )
        high = lax.ppermute(lax.slice_in_dim(block, 0, width, axis=dim), axis, backward)
        block = jnp.concatenate([low, block, high], axis=dim)
    return block


def cross_product(left_vec, right_vec):
    return jnp.stack(
        [
            left_vec[1] * right_vec[2] - left_vec[2] * right_vec[1],
            left_vec[2] * right_vec[0] - left_vec[0] * right_vec[2],
            left_vec[0] * right_vec[1] - left_vec[1] * right_vec[0],
        ]
    )


def make_loads(places, torque, filled):
    return jnp.concatenate(
        [torque * filled, cross_product(torque, places) * filled, filled[None]], 0
    )


def pair_totals(near_places, far_places, far_loads, offset_vec):
    separation = (
        near_places[:, :, :, None] - far_places[:, :, None, :] - offset_vec[:, None, None, None]
    )
    weights = jnp.exp(-jnp.sum(separation * separation, axis=0) * (2.0 / (CELL * CELL)))
    return jnp.einsum("nij,qnj->qni", weights, far_loads, precision=highest)


def neighbours(extended):
    centre = extended[:, 1:-1, 1:-1]
    return [
        centre,
        extended[:, 2:, 1:-1],
        extended[:, :-2, 1:-1],
        extended[:, 1:-1, 2:],
        extended[:, 1:-1, :-2],
        jnp.roll(centre, -1, axis=3),
        jnp.roll(centre, 1, axis=3),
    ]


def near_field(places, torque, filled, face_flags, far_place_list, far_load_list):
    layout = places.shape
    cell_count = layout[1] * layout[2] * layout[3]

    def flatten(values):
        return values.reshape(values.shape[0], cell_count, layout[4])

    drives = jnp.zeros(layout, jnp.float32)
    twists = jnp.zeros(layout, jnp.float32)
    weight_total = jnp.zeros(layout[1:], jnp.float32)
    for face_id in range(7):
        if face_id == 0:
            offset_vec = jnp.zeros((3,), jnp.float32)
            face_gate = jnp.ones(layout[1:4] + (1,), jnp.float32)
        else:
            axis_id, face_sign = face_moves[face_id - 1]
            offset_vec = jnp.zeros((3,), jnp.float32).at[axis_id].set(face_sign * CELL)
            face_gate = face_flags[face_id - 1].astype(jnp.float32)[..., None]
        totals = pair_totals(
            flatten(places),
            flatten(far_place_list[face_id]),
            flatten(far_load_list[face_id]),
            offset_vec,
        )
        totals = totals.reshape((7,) + layout[1:])
        lever = places - offset_vec[:, None, None, None, None]
        drives = drives + face_gate * (cross_product(totals[0:3], lever) - totals[3:6])
        twists = twists + face_gate * totals[0:3]
        weight_total = weight_total + face_gate * totals[6]
    velocity = drift_gain / layout[4] * drives * filled
    spin_near = (torque + couple_gain / layout[4] * (twists - weight_total * torque)) * filled
    return (velocity, spin_near)


def bin_weights(coordinate):
    centres = jnp.arange(CELL, dtype=jnp.float32) + 0.5
    separation = coordinate[..., None] - centres
    return jnp.exp(-separation * separation * bin_rate)


def signed_wave(values):
    return jnp.where(values < GRID // 2, values, values - GRID).astype(jnp.float32)


def stokes(spectrum, wave_x, wave_y, wave_z):
    wave_square = wave_x * wave_x + wave_y * wave_y + wave_z * wave_z
    damping = 0.25 * jnp.exp(-wave_square * (math.pi / GRID) ** 2)
    along = (wave_x * spectrum[0] + wave_y * spectrum[1] + wave_z * spectrum[2]) / jnp.maximum(
        wave_square, 1.0
    )
    return jnp.stack(
        [
            damping * (spectrum[0] - wave_x * along),
            damping * (spectrum[1] - wave_y * along),
            damping * (spectrum[2] - wave_z * along),
        ]
    )


def dft_tables(length):
    counter = jnp.arange(length, dtype=jnp.int32)
    phase = counter[:, None] * counter[None, :] % length
    angle = phase.astype(jnp.float32) * (2.0 * math.pi / length)
    return (jnp.cos(angle), jnp.sin(angle))


def half_tables(length):
    counter = jnp.arange(length, dtype=jnp.int32)
    half_index = jnp.arange(length // 2, dtype=jnp.int32)
    phase = counter[:, None] * half_index[None, :] % length
    angle = phase.astype(jnp.float32) * (2.0 * math.pi / length)
    alternate = 1.0 - 2.0 * (counter % 2).astype(jnp.float32)
    cos_half = jnp.cos(angle)
    sin_half = jnp.where(half_index[None, :] == 0, -alternate[:, None], jnp.sin(angle))
    folding = jnp.where(half_index == 0, 1.0, 2.0).astype(jnp.float32)[:, None]
    return (cos_half, sin_half, folding * cos_half.T, folding * sin_half.T)


def spectral_forward(pieces, form, cosine, sine_tab):
    real_out = jnp.einsum(form, pieces[0], cosine, precision=highest) + jnp.einsum(
        form, pieces[1], sine_tab, precision=highest
    )
    imag_out = jnp.einsum(form, pieces[1], cosine, precision=highest) - jnp.einsum(
        form, pieces[0], sine_tab, precision=highest
    )
    return jnp.stack([real_out, imag_out])


def spectral_inverse(pieces, form, cosine, sine_tab):
    real_out = jnp.einsum(form, pieces[0], cosine, precision=highest) - jnp.einsum(
        form, pieces[1], sine_tab, precision=highest
    )
    imag_out = jnp.einsum(form, pieces[1], cosine, precision=highest) + jnp.einsum(
        form, pieces[0], sine_tab, precision=highest
    )
    return jnp.stack([real_out, imag_out])


def apply_stokes(spectrum, wave_x, wave_y, wave_z):
    return jnp.stack(
        [stokes(spectrum[0], wave_x, wave_y, wave_z), stokes(spectrum[1], wave_x, wave_y, wave_z)]
    )


def solve_half(grid_field):
    cosine, sine_tab = dft_tables(GRID)
    cos_half, sin_half, cos_back, sin_back = half_tables(GRID)
    real_part = jnp.einsum("cxyz,zk->ckxy", grid_field, cos_half, precision=highest)
    imag_part = -jnp.einsum("cxyz,zk->ckxy", grid_field, sin_half, precision=highest)
    spectrum = jnp.stack([real_part, imag_part])
    pencil = spectral_forward(
        lax.all_to_all(spectrum, "col", split_axis=2, concat_axis=4, tiled=True),
        "ckxy,yl->clkx",
        cosine,
        sine_tab,
    )
    pencil = spectral_forward(
        lax.all_to_all(pencil, "row", split_axis=2, concat_axis=4, tiled=True),
        "clkx,xm->clkm",
        cosine,
        sine_tab,
    )
    ky_count = pencil.shape[2]
    kz_count = pencil.shape[3]
    row_place = lax.axis_index("row")
    col_place = lax.axis_index("col")
    wave_ky = signed_wave(row_place * ky_count + jnp.arange(ky_count, dtype=jnp.int32))
    wave_kz = signed_wave(col_place * kz_count + jnp.arange(kz_count, dtype=jnp.int32))
    wave_kx = signed_wave(jnp.arange(GRID, dtype=jnp.int32))
    regular = apply_stokes(
        pencil, wave_kx[None, None, :], wave_ky[:, None, None], wave_kz[None, :, None]
    )
    edge_plane = pencil[:, :, :, 0, :]
    whole_plane = lax.all_gather(edge_plane, "row", axis=2, tiled=True)
    mirrored = jnp.roll(jnp.flip(whole_plane, (2, 3)), 1, (2, 3))
    partner = lax.dynamic_slice_in_dim(mirrored, row_place * ky_count, ky_count, 2)
    even_part = jnp.stack([(edge_plane[0] + partner[0]) * 0.5, (edge_plane[1] - partner[1]) * 0.5])
    odd_part = jnp.stack([(edge_plane[1] + partner[1]) * 0.5, (partner[0] - edge_plane[0]) * 0.5])
    plane_x = wave_kx[None, :]
    plane_y = wave_ky[:, None]
    zero_wave = jnp.zeros((1, 1), wave_kx.dtype)
    nyquist_wave = zero_wave + GRID // 2
    even_out = apply_stokes(even_part, plane_x, plane_y, zero_wave)
    odd_out = 0.5 * (
        apply_stokes(odd_part, plane_x, plane_y, nyquist_wave)
        + apply_stokes(odd_part, plane_x, plane_y, -nyquist_wave)
    )
    packed = jnp.stack([even_out[0] - odd_out[1], even_out[1] + odd_out[0]])
    first_slot = jnp.where(col_place == 0, packed, regular[:, :, :, 0, :])
    pencil = jnp.concatenate([first_slot[:, :, :, None], regular[:, :, :, 1:]], 3)
    pencil = spectral_inverse(pencil, "clkm,mx->clkx", cosine, sine_tab)
    pencil = spectral_inverse(
        lax.all_to_all(pencil, "row", split_axis=4, concat_axis=2, tiled=True),
        "clkx,ly->ckxy",
        cosine,
        sine_tab,
    )
    pieces = lax.all_to_all(pencil, "col", split_axis=4, concat_axis=2, tiled=True)
    summed = jnp.einsum("ckxy,kz->cxyz", pieces[0], cos_back, precision=highest) - jnp.einsum(
        "ckxy,kz->cxyz", pieces[1], sin_back, precision=highest
    )
    return summed * (1.0 / GRID) ** 3


def solve_far(grid_field):
    return solve_half(grid_field)


def far_field(places, torque, filled):
    cells_x, cells_y, cells_z, slot_count = (
        places.shape[1],
        places.shape[2],
        places.shape[3],
        places.shape[4],
    )
    cell_count = cells_x * cells_y * cells_z
    flat_places = places.reshape(3, cell_count, slot_count)
    weight_x = bin_weights(flat_places[0])
    weight_y = bin_weights(flat_places[1])
    weight_z = bin_weights(flat_places[2])
    planar = weight_x[:, :, :, None] * weight_y[:, :, None, :]
    lifted = (torque * filled).reshape(3, cell_count, slot_count)[:, :, :, None] * weight_z[None]
    cubes = jnp.einsum("niab,qnic->qnabc", planar, lifted, precision=highest)
    grid_field = (
        cubes.reshape(3, cells_x, cells_y, cells_z, CELL, CELL, CELL)
        .transpose(0, 1, 4, 2, 5, 3, 6)
        .reshape(3, cells_x * CELL, cells_y * CELL, cells_z * CELL)
    )
    far_grid = solve_far(grid_field)
    cubes = (
        far_grid.reshape(3, cells_x, CELL, cells_y, CELL, cells_z, CELL)
        .transpose(0, 1, 3, 5, 2, 4, 6)
        .reshape(3, cell_count, CELL, CELL, CELL)
    )
    partial_sum = jnp.einsum("qnabc,niab->qnic", cubes, planar, precision=highest)
    return jnp.sum(partial_sum * weight_z[None], axis=3).reshape(
        3, cells_x, cells_y, cells_z, slot_count
    )


def shards(positions, torques, counts, neighbour_flags):
    slot_count = positions.shape[4]
    filled = (jnp.arange(slot_count, dtype=jnp.int32) < counts[..., None]).astype(jnp.float32)
    places = positions
    spin_near = jnp.zeros(positions.shape, jnp.float32)
    for step_id in range(STEPS):
        loads = make_loads(places, torques, filled)
        state_rim = with_halo(jnp.concatenate([places, loads], 0), (("row", 1), ("col", 2)), 1)
        place_rim = state_rim[0:3]
        load_rim = state_rim[3:10]
        velocity, spin_near = near_field(
            places, torques, filled, neighbour_flags, neighbours(place_rim), neighbours(load_rim)
        )
        places = places + step_pace * CELL * velocity
    far_spin = far_field(places, torques, filled)
    return (places, spin_near + far_spin * filled)


def solution(mesh):
    in_specs = (
        P(None, "row", "col", None, None),
        P(None, "row", "col", None, None),
        P("row", "col", None),
        P(None, "row", "col", None),
    )
    out_specs = (P(None, "row", "col", None, None), P(None, "row", "col", None, None))
    return jax.shard_map(shards, mesh=mesh, in_specs=in_specs, out_specs=out_specs, check_vma=False)
```

profile of v0, /device:TPU:0, one launch (start us, length us, event | category | flops | bytes accessed | tf_op | source)
XLA Modules:
  0.0 1028.8 jit_solution(7356824172075767537)
XLA Ops:
  5.4 5.1 collective-permute-start
  23.9 2.8 collective-permute-start.2
  27.0 11.4 %multiply_reduce_fusion.19 = f32[128,128,128]{2,1,0:T(8,128)} fusion(f32[3]{0:T(128)S(1)} %copy-done.79, f32[3,128,128]{2,1,0:T(8,128)S(1)} %bitcast.562, f32[3,128,128]{2,1,0:T(8,128)S(1)} %bitcast.450), kind=kLoop, calls=%fused_computation.19 | loop fusion | flops 23068672 | bytes 8781836 | tf_op jit(solution)/shard_map/reduce_sum | solution.py:55
  38.4 15.4 %fusion.149 = f32[7,128,128]{2,0,1:T(8,128)S(1)} fusion(f32[7,128,128]{2,0,1:T(8,128)S(1)} %bitcast.507, f32[128,128,128]{2,1,0:T(8,128)} %multiply_reduce_fusion.19), kind=kOutput, calls=%fused_computation.203 | convolution fusion | flops 180355072 | bytes 9306112 | tf_op jit(solution)/shard_map/nij,qnj->qni/dot_general | solution.py:56
  58.6 57.2 %multiply_reduce_fusion.14 = (f32[128,128,128]{2,1,0:T(8,128)}, f32[128,128,128]{2,1,0:T(8,128)}, f32[128,128,128]{2,1,0:T(8,128)}, f32[128,128,128]{2,1,0:T(8,1...) fusion(f32[3]{0:T(128)S(1)} %copy-done.81, f32[3,128,128]{2,1,0:T(8,128)} %bitcast.560, ...), kind=kLoop, calls=%fused_computation.14 | loop fusion | flops 132120576 | bytes 51511356 | tf_op jit(solution)/shard_map/reduce_sum | solution.py:55
  115.9 16.0 %fusion.152 = f32[7,128,128]{2,0,1:T(8,128)S(1)} fusion(f32[7,128,128]{2,0,1:T(8,128)S(1)} %bitcast.504, f32[128,128,128]{2,1,0:T(8,128)} %get-tuple-element.183), kind=kOutput, calls=%fused_computation.204 | convolution fusion | flops 180355072 | bytes 9306112 | tf_op jit(solution)/shard_map/nij,qnj->qni/dot_general | solution.py:56
  132.2 13.1 %fusion.164 = f32[7,128,128]{2,0,1:T(8,128)S(1)} fusion(f32[7,128,128]{2,0,1:T(8,128)S(1)} %bitcast.501, f32[128,128,128]{2,1,0:T(8,128)S(1)} %copy-done.4), kind=kOutput, calls=%fused_computation.208 | convolution fusion | flops 180355072 | bytes 9306112 | tf_op jit(solution)/shard_map/nij,qnj->qni/dot_general | solution.py:56
  145.8 13.3 %fusion.155 = f32[7,128,128]{2,0,1:T(8,128)S(1)} fusion(f32[7,128,128]{2,0,1:T(8,128)S(1)} %bitcast.509, f32[128,128,128]{2,1,0:T(8,128)S(1)} %copy-done.1), kind=kOutput, calls=%fused_computation.205 | convolution fusion | flops 180355072 | bytes 9306112 | tf_op jit(solution)/shard_map/nij,qnj->qni/dot_general | solution.py:56
  159.6 13.3 %fusion.158 = f32[7,128,128]{2,0,1:T(8,128)S(1)} fusion(f32[7,128,128]{2,0,1:T(8,128)S(1)} %bitcast.510, f32[128,128,128]{2,1,0:T(8,128)S(1)} %bitcast.469), kind=kOutput, calls=%fused_computation.206 | convolution fusion | flops 180355072 | bytes 9306112 | tf_op jit(solution)/shard_map/nij,qnj->qni/dot_general | solution.py:56
  173.2 13.5 %fusion.161 = f32[7,128,128]{2,0,1:T(8,128)S(1)} fusion(f32[7,128,128]{2,0,1:T(8,128)S(1)} %bitcast.498, f32[128,128,128]{2,1,0:T(8,128)S(1)} %bitcast.463), kind=kOutput, calls=%fused_computation.207 | convolution fusion | flops 180355072 | bytes 9306112 | tf_op jit(solution)/shard_map/nij,qnj->qni/dot_general | solution.py:56
  187.1 13.3 %fusion.146 = f32[7,128,128]{2,0,1:T(8,128)S(1)} fusion(f32[128,128,128]{2,1,0:T(8,128)S(1)} %bitcast.457, f32[1,128,128]{2,0,1:T(1,128)S(1)} %copy-done.26, f32[3,128,128]{2,0,1:T(4,128)S(1)} %bitcast.488, f32[3,128,128]{2,0,1:T(4,128)S(1)} %copy-done.30), kind=kOutput, calls=%fused_computation.202 | convolution fusion | flops 180584448 | bytes 9306112 | tf_op jit(solution)/shard_map/nij,qnj->qni/dot_general | solution.py:56
  203.6 3.9 collective-permute-start.4
  219.5 12.9 %multiply_reduce_fusion.12 = f32[128,128,128]{2,1,0:T(8,128)} fusion(f32[3,128,128]{2,1,0:T(8,128)} %bitcast.563, f32[3,128,128]{2,1,0:T(8,128)S(1)} %bitcast.448, f32[3]{0:T(128)S(1)} %copy-done.80), kind=kLoop, calls=%fused_computation.12 | loop fusion | flops 23068672 | bytes 8781836 | tf_op jit(solution)/shard_map/reduce_sum | solution.py:55
  232.4 15.4 %fusion.170 = f32[7,128,128]{2,0,1:T(8,128)S(1)} fusion(f32[7,128,128]{2,0,1:T(8,128)S(1)} %bitcast.508, f32[128,128,128]{2,1,0:T(8,128)} %multiply_reduce_fusion.12), kind=kOutput, calls=%fused_computation.210 | convolution fusion | flops 180355072 | bytes 9306112 | tf_op jit(solution)/shard_map/nij,qnj->qni/dot_general | solution.py:56
  254.4 57.5 %multiply_reduce_fusion.7 = (f32[128,128,128]{2,1,0:T(8,128)}, f32[128,128,128]{2,1,0:T(8,128)}, f32[128,128,128]{2,1,0:T(8,128)}, f32[128,128,128]{2,1,0:T(8,12...) fusion(f32[3,128,128]{2,1,0:T(8,128)} %bitcast.549, f32[3,128,128]{2,1,0:T(8,128)S(1)} %bitcast.449, ...), kind=kLoop, calls=%fused_computation.7 | loop fusion | flops 132120576 | bytes 51511356 | tf_op jit(solution)/shard_map/reduce_sum | solution.py:55
  311.9 16.0 %fusion.173 = f32[7,128,128]{2,0,1:T(8,128)S(1)} fusion(f32[7,128,128]{2,0,1:T(8,128)S(1)} %bitcast.505, f32[128,128,128]{2,1,0:T(8,128)} %get-tuple-element.177), kind=kOutput, calls=%fused_computation.211 | convolution fusion | flops 180355072 | bytes 9306112 | tf_op jit(solution)/shard_map/nij,qnj->qni/dot_general | solution.py:56
  328.2 13.1 %fusion.185 = f32[7,128,128]{2,0,1:T(8,128)S(1)} fusion(f32[7,128,128]{2,0,1:T(8,128)S(1)} %bitcast.502, f32[128,128,128]{2,1,0:T(8,128)S(1)} %copy-done.5), kind=kOutput, calls=%fused_computation.215 | convolution fusion | flops 180355072 | bytes 9306112 | tf_op jit(solution)/shard_map/nij,qnj->qni/dot_general | solution.py:56
  341.8 13.3 %fusion.176 = f32[7,128,128]{2,0,1:T(8,128)S(1)} fusion(f32[7,128,128]{2,0,1:T(8,128)S(1)} %bitcast.511, f32[128,128,128]{2,1,0:T(8,128)S(1)} %copy-done.2), kind=kOutput, calls=%fused_computation.212 | convolution fusion | flops 180355072 | bytes 9306112 | tf_op jit(solution)/shard_map/nij,qnj->qni/dot_general | solution.py:56
  355.7 13.3 %fusion.179 = f32[7,128,128]{2,0,1:T(8,128)S(1)} fusion(f32[7,128,128]{2,0,1:T(8,128)S(1)} %bitcast.512, f32[128,128,128]{2,1,0:T(8,128)S(1)} %bitcast.471), kind=kOutput, calls=%fused_computation.213 | convolution fusion | flops 180355072 | bytes 9306112 | tf_op jit(solution)/shard_map/nij,qnj->qni/dot_general | solution.py:56
  369.3 13.5 %fusion.182 = f32[7,128,128]{2,0,1:T(8,128)S(1)} fusion(f32[7,128,128]{2,0,1:T(8,128)S(1)} %bitcast.499, f32[128,128,128]{2,1,0:T(8,128)S(1)} %bitcast.465), kind=kOutput, calls=%fused_computation.214 | convolution fusion | flops 180355072 | bytes 9306112 | tf_op jit(solution)/shard_map/nij,qnj->qni/dot_general | solution.py:56
  383.1 13.3 %fusion.167 = f32[7,128,128]{2,0,1:T(8,128)S(1)} fusion(f32[128,128,128]{2,1,0:T(8,128)S(1)} %bitcast.459, f32[1,128,128]{2,0,1:T(1,128)S(1)} %copy-done.27, f32[3,128,128]{2,0,1:T(4,128)S(1)} %bitcast.489, f32[3,128,128]{2,0,1:T(4,128)S(1)} %copy-done.33), kind=kOutput, calls=%fused_computation.209 | convolution fusion | flops 180584448 | bytes 9306112 | tf_op jit(solution)/shard_map/nij,qnj->qni/dot_general | solution.py:56
  413.5 12.9 %multiply_reduce_fusion.5 = f32[128,128,128]{2,1,0:T(8,128)} fusion(f32[3,128,128]{2,1,0:T(8,128)} %bitcast.561, f32[3,128,128]{2,1,0:T(8,128)S(1)} %bitcast.446, f32[3]{0:T(128)S(1)} %copy-done.80), kind=kLoop, calls=%fused_computation.5 | loop fusion | flops 23068672 | bytes 8781836 | tf_op jit(solution)/shard_map/reduce_sum | solution.py:55
  426.3 15.5 %fusion.191 = f32[7,128,128]{2,0,1:T(8,128)S(1)} fusion(f32[7,128,128]{2,0,1:T(8,128)S(1)} %bitcast.506, f32[128,128,128]{2,1,0:T(8,128)} %multiply_reduce_fusion.5), kind=kOutput, calls=%fused_computation.217 | convolution fusion | flops 180355072 | bytes 9306112 | tf_op jit(solution)/shard_map/nij,qnj->qni/dot_general | solution.py:56
  450.7 57.2 %multiply_reduce_fusion = (f32[128,128,128]{2,1,0:T(8,128)}, f32[128,128,128]{2,1,0:T(8,128)}, f32[128,128,128]{2,1,0:T(8,128)}, f32[128,128,128]{2,1,0:T(8,128)...) fusion(f32[3,128,128]{2,1,0:T(8,128)} %bitcast.547, f32[3,128,128]{2,1,0:T(8,128)S(1)} %bitcast.447, ...), kind=kLoop, calls=%fused_computation | loop fusion | flops 132120576 | bytes 51511356 | tf_op jit(solution)/shard_map/reduce_sum | solution.py:55
  507.9 16.1 %fusion.188 = f32[7,128,128]{2,0,1:T(8,128)S(1)} fusion(f32[128,128,128]{2,1,0:T(8,128)} %get-tuple-element.175, f32[1,128,128]{2,0,1:T(1,128)S(1)} %copy-done.28, f32[3,128,128]{2,0,1:T(4,128)S(1)} %bitcast.490, f32[3,128,128]{2,0,1:T(4,128)S(1)} %copy-done.34), kind=kOutput, calls=%fused_computation.216 | convolution fusion | flops 180584448 | bytes 9306112 | tf_op jit(solution)/shard_map/nij,qnj->qni/dot_general | solution.py:56
  525.7 13.1 %fusion.194 = f32[7,128,128]{2,0,1:T(8,128)S(1)} fusion(f32[7,128,128]{2,0,1:T(8,128)S(1)} %bitcast.503, f32[128,128,128]{2,1,0:T(8,128)S(1)} %copy-done.3), kind=kOutput, calls=%fused_computation.218 | convolution fusion | flops 180355072 | bytes 9306112 | tf_op jit(solution)/shard_map/nij,qnj->qni/dot_general | solution.py:56
  540.4 13.3 %fusion.206 = f32[7,128,128]{2,0,1:T(8,128)S(1)} fusion(f32[7,128,128]{2,0,1:T(8,128)S(1)} %bitcast.500, f32[128,128,128]{2,1,0:T(8,128)S(1)} %bitcast.467), kind=kOutput, calls=%fused_computation.222 | convolution fusion | flops 180355072 | bytes 9306112 | tf_op jit(solution)/shard_map/nij,qnj->qni/dot_general | solution.py:56
  555.7 13.3 %fusion.197 = f32[7,128,128]{2,0,1:T(8,128)S(1)} fusion(f32[7,128,128]{2,0,1:T(8,128)S(1)} %bitcast.513, f32[128,128,128]{2,1,0:T(8,128)S(1)} %bitcast.461), kind=kOutput, calls=%fused_computation.219 | convolution fusion | flops 180355072 | bytes 9306112 | tf_op jit(solution)/shard_map/nij,qnj->qni/dot_general | solution.py:56
  570.9 13.5 %fusion.200 = f32[7,128,128]{2,0,1:T(8,128)S(1)} fusion(f32[7,128,128]{2,0,1:T(8,128)S(1)} %bitcast.514, f32[128,128,128]{2,1,0:T(8,128)S(1)} %bitcast.455), kind=kOutput, calls=%fused_computation.220 | convolution fusion | flops 180355072 | bytes 9306112 | tf_op jit(solution)/shard_map/nij,qnj->qni/dot_general | solution.py:56
  586.1 13.3 %fusion.203 = f32[7,128,128]{2,0,1:T(8,128)S(1)} fusion(f32[7,128,128]{2,0,1:T(8,128)S(1)} %bitcast.497, f32[128,128,128]{2,1,0:T(8,128)S(1)} %bitcast.453), kind=kOutput, calls=%fused_computation.221 | convolution fusion | flops 180355072 | bytes 9306112 | tf_op jit(solution)/shard_map/nij,qnj->qni/dot_general | solution.py:56
  602.0 173.9 %fusion.86 = f32[128,3,8,8,8]{4,2,3,1,0:T(8,128)} fusion(f32[128,128,8]{1,2,0:T(8,128)S(1)} %get-tuple-element.506, f32[128,128,8]{1,2,0:T(8,128)S(1)} %get-tuple-element.507, f32[128,128,8]{1,2,0:T(8,128)S(1)} %get-tuple-element.505, f32[3,128,128]{2,0,1:T(4,128)S(1)} %bitcast.491), kind=kOutput, calls=%fused_computation.107 | convolution fusion | flops 303431680 | bytes 2555904 | tf_op jit(solution)/shard_map/niab,qnic->qnabc/dot_general | solution.py:254
  775.9 13.0 %copy.449 = f32[3,4,2,16,8,8,8]{6,3,5,2,4,1,0:T(8,128)} copy(f32[3,4,2,16,8,8,8]{5,6,4,0,3,2,1:T(8,128)} %bitcast.443) | data formatting | bytes 1572864 | tf_op jit(solution)/shard_map/reshape | solution.py:256
  789.0 9.1 reshape.1728
  801.3 2.8 copy.452
  806.2 16.0 %all_to_all.60 = f32[8,1,24576]{2,1,0:T(1,128)S(1)} all-to-all(f32[8,1,24576]{2,1,0:T(1,128)} %reshape.1742), channel_id=1, replica_groups=mesh['row'=4,'col'=8] {'col'}, dimensions={0} | all-to-all | bytes 1572864 | tf_op jit(solution)/shard_map/all_to_all | solution.py:183
  822.8 3.7 reduce.25
  846.3 3.5 all-to-all-start.1
  852.2 17.4 %all-to-all-done.1 = f32[4,1,49152]{2,1,0:T(1,128)S(1)} async-done(((f32[4,1,49152]{2,1,0:T(1,128)}), f32[4,1,49152]{2,1,0:T(1,128)S(1)}, u32[]{:S(2)}, u32[]{:S(2)}) %all-to-all-start.1) | async-done | bytes 786464 | tf_op jit(solution)/shard_map/all_to_all | solution.py:189
  869.5 3.8 reduce.26
  885.4 15.3 %all-gather = f32[2,3,128,1,128]{4,2,1,3,0:T(8,128)S(1)} all-gather(f32[2,3,32,1,128]{4,2,1,3,0:T(8,128)S(1)} %pad_maximum_fusion.67), channel_id=2, replica_groups=mesh['row'=4,'col'=8] {'row'}, dimensions={2}, use_global_device_ids=true | all-gather | bytes 491520 | tf_op jit(solution)/shard_map/all_gather | solution.py:205
  913.5 20.0 %all_to_all.61 = f32[4,1,49152]{2,1,0:T(1,128)S(1)} all-to-all(f32[4,1,49152]{2,1,0:T(1,128)} %reshape.1746), channel_id=1, replica_groups=mesh['row'=4,'col'=8] {'row'}, dimensions={0} | all-to-all | bytes 1572864 | tf_op jit(solution)/shard_map/all_to_all | solution.py:224
  933.5 3.8 reduce.27
  954.0 3.8 all-to-all-start.3
  959.5 10.8 %all-to-all-done.3 = f32[8,1,24576]{2,1,0:T(1,128)S(1)} async-done(((f32[8,1,24576]{2,1,0:T(1,128)}), f32[8,1,24576]{2,1,0:T(1,128)S(1)}, u32[]{:S(2)}, u32[]{:S(2)}) %all-to-all-start.3) | async-done | bytes 786464 | tf_op jit(solution)/shard_map/all_to_all | solution.py:229
  970.3 3.7 reduce.28
  983.4 8.6 reshape.1729
  992.0 14.1 %copy.503 = f32[3,4,2,16,8,8,8]{5,6,4,0,3,2,1:T(8,128)} copy(f32[3,4,2,16,8,8,8]{6,3,5,2,4,1,0:T(8,128)} %bitcast.445) | data formatting | bytes 1572864 | tf_op jit(solution)/shard_map/reshape | solution.py:264
  1006.2 21.2 %fusion.116 = f32[128,128,3]{1,2,0:T(4,128)S(1)} fusion(f32[3,128,8,8,8]{3,4,2,0,1:T(8,128)} %bitcast.442, f32[128,128,8]{1,2,0:T(8,128)S(1)} %copy-done.10, f32[128,128,8]{1,2,0:T(8,128)S(1)} %copy-done.12, f32[128,128,8]{1,2,0:T(8,128)S(1)} %copy-done.8), kind=kOutput, calls=%fused_computation.159 | convolution fusion | flops 303775744 | bytes 2555904 | tf_op jit(solution)/shard_map/qnabc,niab->qnic/dot_general | solution.py:266
  (564 shorter events, 165.7 us)
Async XLA Ops:
  5.4 17.2 %collective-permute-start = (f32[10,1,2,16,128]{4,3,2,1,0:T(8,128)S(1)}, f32[10,1,2,16,128]{4,3,2,1,0:T(8,128)S(1)}, u32[]{:S(2)}, u32[]{:S(2)}) collective-permute-start(f32[10,1,2,16,128]{4,3,2,1,0:T(8,128)S(1)} %get-tuple-element.238), channel_id=1, source_target_pairs={{8,0},{16,8},{24,16},{0,24},{9,1},{17,9},{25,17},{1,25},{10,2},{18... | collective-permute-start | bytes 491528 | tf_op jit(solution)/shard_map/ppermute | solution.py:30
  10.5 12.1 %collective-permute-start.1 = (f32[10,1,2,16,128]{4,3,2,1,0:T(8,128)S(1)}, f32[10,1,2,16,128]{4,3,2,1,0:T(8,128)S(1)}, u32[]{:S(2)}, u32[]{:S(2)}) collective-permute-start(f32[10,1,2,16,128]{4,3,2,1,0:T(8,128)S(1)} %get-tuple-element.239), channel_id=1, source_target_pairs={{0,8},{8,16},{16,24},{24,0},{1,9},{9,17},{17,25},{25,1},{2,10},{10... | collective-permute-start | bytes 491528 | tf_op jit(solution)/shard_map/ppermute | solution.py:27
  23.9 32.5 %collective-permute-start.3 = (f32[10,6,1,16,128]{4,3,2,1,0:T(8,128)}, f32[10,6,1,16,128]{4,3,2,1,0:T(8,128)S(1)}, u32[]{:S(2)}, u32[]{:S(2)}) collective-permute-start(f32[10,6,1,16,128]{4,3,2,1,0:T(8,128)} %get-tuple-element.226), channel_id=1, source_target_pairs={{0,1},{1,2},{2,3},{3,4},{4,5},{5,6},{6,7},{7,0},{8,9},{9,10},{10,1... | collective-permute-start | bytes 1474568 | tf_op jit(solution)/shard_map/ppermute | solution.py:27
  23.9 32.5 %collective-permute-start.2 = (f32[10,6,1,16,128]{4,3,2,1,0:T(8,128)}, f32[10,6,1,16,128]{4,3,2,1,0:T(8,128)}, u32[]{:S(2)}, u32[]{:S(2)}) collective-permute-start(f32[10,6,1,16,128]{4,3,2,1,0:T(8,128)} %get-tuple-element.227), channel_id=1, source_target_pairs={{1,0},{2,1},{3,2},{4,3},{5,4},{6,5},{7,6},{0,7},{9,8},{10,9},{11,1... | collective-permute-start | bytes 1474568 | tf_op jit(solution)/shard_map/ppermute | solution.py:30
  132.1 27.5 %slice-start.16 = ((s8[8388608]{0:T(1024)(128)(4,1)}), s8[4194304]{0:T(1024)(128)(4,1)S(1)}, s32[]{:S(2)}) async-start(s8[8388608]{0:T(1024)(128)(4,1)} %bitcast.468), calls=%async_computation.20 | async-start | bytes 8388608
  145.8 27.4 %slice-start.10 = ((s8[8388608]{0:T(1024)(128)(4,1)}), s8[4194304]{0:T(1024)(128)(4,1)S(1)}, s32[]{:S(2)}) async-start(s8[8388608]{0:T(1024)(128)(4,1)} %bitcast.462), calls=%async_computation.14 | async-start | bytes 8388608
  159.6 27.5 %slice-start.4 = ((s8[8388608]{0:T(1024)(128)(4,1)}), s8[4194304]{0:T(1024)(128)(4,1)S(1)}, s32[]{:S(2)}) async-start(s8[8388608]{0:T(1024)(128)(4,1)} %bitcast.456), calls=%async_computation.8 | async-start | bytes 8388608
  159.6 27.5 %copy-start.26 = (f32[1,128,128]{2,0,1:T(1,128)S(1)}, f32[1,128,128]{2,0,1:T(1,128)}, u32[]{:S(2)}) copy-start(f32[1,128,128]{2,0,1:T(1,128)} %compare_convert_fusion) | copy-start | bytes 196612
  159.6 27.5 %copy-start.30 = (f32[3,128,128]{2,0,1:T(4,128)S(1)}, f32[3,128,128]{2,0,1:T(4,128)}, u32[]{:S(2)}) copy-start(f32[3,128,128]{2,0,1:T(4,128)} %maximum_multiply_fusion) | copy-start | bytes 589828
  173.2 27.5 %copy-start.53 = (f32[3,4,2,16,128]{4,3,2,1,0:T(8,128)S(1)}, f32[3,4,2,16,128]{4,3,2,1,0:T(8,128)}, u32[]{:S(2)}) copy-start(f32[3,4,2,16,128]{4,3,2,1,0:T(8,128)} %get-tuple-element.442) | copy-start | bytes 589828
  203.6 8.3 collective-permute-start.4
  207.5 7.1 collective-permute-start.5
  216.6 34.7 %collective-permute-start.7 = (f32[10,6,1,16,128]{4,3,2,1,0:T(8,128)}, f32[10,6,1,16,128]{4,3,2,1,0:T(8,128)}, u32[]{:S(2)}, u32[]{:S(2)}) collective-permute-start(f32[10,6,1,16,128]{4,3,2,1,0:T(8,128)} %get-tuple-element.222), channel_id=1, source_target_pairs={{0,1},{1,2},{2,3},{3,4},{4,5},{5,6},{6,7},{7,0},{8,9},{9,10},{10,1... | collective-permute-start | bytes 1474568 | tf_op jit(solution)/shard_map/ppermute | solution.py:27
  216.6 34.7 %collective-permute-start.6 = (f32[10,6,1,16,128]{4,3,2,1,0:T(8,128)}, f32[10,6,1,16,128]{4,3,2,1,0:T(8,128)}, u32[]{:S(2)}, u32[]{:S(2)}) collective-permute-start(f32[10,6,1,16,128]{4,3,2,1,0:T(8,128)} %get-tuple-element.223), channel_id=1, source_target_pairs={{1,0},{2,1},{3,2},{4,3},{5,4},{6,5},{7,6},{0,7},{9,8},{10,9},{11,1... | collective-permute-start | bytes 1474568 | tf_op jit(solution)/shard_map/ppermute | solution.py:30
  254.4 57.5 %copy-start.16 = (f32[7,4,2,16,128]{4,0,3,2,1:T(8,128)S(1)}, f32[7,4,2,16,128]{4,0,3,2,1:T(8,128)}, u32[]{:S(2)}) copy-start(f32[7,4,2,16,128]{4,0,3,2,1:T(8,128)} %copy.419) | copy-start | bytes 1376260
  311.9 29.6 %copy-start.20 = (f32[7,4,2,16,128]{4,3,2,1,0:T(8,128)S(1)}, f32[7,4,2,16,128]{4,3,2,1,0:T(8,128)}, u32[]{:S(2)}) copy-start(f32[7,4,2,16,128]{4,3,2,1,0:T(8,128)} %slice.1956) | copy-start | bytes 1376260
  328.2 27.5 %slice-start.18 = ((s8[8388608]{0:T(1024)(128)(4,1)}), s8[4194304]{0:T(1024)(128)(4,1)S(1)}, s32[]{:S(2)}) async-start(s8[8388608]{0:T(1024)(128)(4,1)} %bitcast.470), calls=%async_computation.22 | async-start | bytes 8388608
  341.8 27.4 %slice-start.12 = ((s8[8388608]{0:T(1024)(128)(4,1)}), s8[4194304]{0:T(1024)(128)(4,1)S(1)}, s32[]{:S(2)}) async-start(s8[8388608]{0:T(1024)(128)(4,1)} %bitcast.464), calls=%async_computation.16 | async-start | bytes 8388608
  355.7 27.4 %slice-start.6 = ((s8[8388608]{0:T(1024)(128)(4,1)}), s8[4194304]{0:T(1024)(128)(4,1)S(1)}, s32[]{:S(2)}) async-start(s8[8388608]{0:T(1024)(128)(4,1)} %bitcast.458), calls=%async_computation.10 | async-start | bytes 8388608
  355.7 27.4 %copy-start.27 = (f32[1,128,128]{2,0,1:T(1,128)S(1)}, f32[1,128,128]{2,0,1:T(1,128)}, u32[]{:S(2)}) copy-start(f32[1,128,128]{2,0,1:T(1,128)} %compare_convert_fusion) | copy-start | bytes 196612
  355.7 27.4 %copy-start.33 = (f32[3,128,128]{2,0,1:T(4,128)S(1)}, f32[3,128,128]{2,0,1:T(4,128)}, u32[]{:S(2)}) copy-start(f32[3,128,128]{2,0,1:T(4,128)} %maximum_multiply_fusion.1) | copy-start | bytes 589828
  369.3 27.4 %copy-start.61 = (f32[3,4,2,16,128]{4,3,2,1,0:T(8,128)S(1)}, f32[3,4,2,16,128]{4,3,2,1,0:T(8,128)}, u32[]{:S(2)}) copy-start(f32[3,4,2,16,128]{4,3,2,1,0:T(8,128)} %get-tuple-element.433) | copy-start | bytes 589828
  399.5 7.9 collective-permute-start.8
  401.2 7.2 collective-permute-start.9
  410.5 35.5 %collective-permute-start.11 = (f32[10,6,1,16,128]{4,3,2,1,0:T(8,128)}, f32[10,6,1,16,128]{4,3,2,1,0:T(8,128)}, u32[]{:S(2)}, u32[]{:S(2)}) collective-permute-start(f32[10,6,1,16,128]{4,3,2,1,0:T(8,128)} %get-tuple-element.218), channel_id=1, source_target_pairs={{0,1},{1,2},{2,3},{3,4},{4,5},{5,6},{6,7},{7,0},{8,9},{9,10},{10,1... | collective-permute-start | bytes 1474568 | tf_op jit(solution)/shard_map/ppermute | solution.py:27
  410.5 35.5 %collective-permute-start.10 = (f32[10,6,1,16,128]{4,3,2,1,0:T(8,128)}, f32[10,6,1,16,128]{4,3,2,1,0:T(8,128)}, u32[]{:S(2)}, u32[]{:S(2)}) collective-permute-start(f32[10,6,1,16,128]{4,3,2,1,0:T(8,128)} %get-tuple-element.219), channel_id=1, source_target_pairs={{1,0},{2,1},{3,2},{4,3},{5,4},{6,5},{7,6},{0,7},{9,8},{10,9},{11,1... | collective-permute-start | bytes 1474568 | tf_op jit(solution)/shard_map/ppermute | solution.py:30
  413.5 31.0 %copy-start.63 = (f32[3,4,2,16,128]{4,3,2,1,0:T(8,128)S(1)}, f32[3,4,2,16,128]{4,3,2,1,0:T(8,128)}, u32[]{:S(2)}) copy-start(f32[3,4,2,16,128]{4,3,2,1,0:T(8,128)} %get-tuple-element.424) | copy-start | bytes 589828
  426.3 24.3 %copy-start.89 = (f32[3]{0:T(128)S(1)}, f32[3]{0:T(128)}, u32[]{:S(2)}) copy-start(f32[3]{0:T(128)} %constant.414.clone.1) | copy-start | bytes 40
  426.3 24.3 %copy-start.94 = (f32[3]{0:T(128)S(1)}, f32[3]{0:T(128)}, u32[]{:S(2)}) copy-start(f32[3]{0:T(128)} %constant.413.clone.1) | copy-start | bytes 40
  426.3 24.3 %copy-start.99 = (f32[3]{0:T(128)S(1)}, f32[3]{0:T(128)}, u32[]{:S(2)}) copy-start(f32[3]{0:T(128)} %constant.412.clone.1) | copy-start | bytes 40
  450.7 57.3 %copy-start.28 = (f32[1,128,128]{2,0,1:T(1,128)S(1)}, f32[1,128,128]{2,0,1:T(1,128)}, u32[]{:S(2)}) copy-start(f32[1,128,128]{2,0,1:T(1,128)} %compare_convert_fusion) | copy-start | bytes 196612
  450.7 57.3 %copy-start.34 = (f32[3,128,128]{2,0,1:T(4,128)S(1)}, f32[3,128,128]{2,0,1:T(4,128)}, u32[]{:S(2)}) copy-start(f32[3,128,128]{2,0,1:T(4,128)} %maximum_multiply_fusion.2) | copy-start | bytes 589828
  507.9 32.5 %slice-start.14 = ((s8[8388608]{0:T(1024)(128)(4,1)}), s8[4194304]{0:T(1024)(128)(4,1)S(1)}, s32[]{:S(2)}) async-start(s8[8388608]{0:T(1024)(128)(4,1)} %bitcast.466), calls=%async_computation.18 | async-start | bytes 8388608
  525.7 29.9 %slice-start.8 = ((s8[8388608]{0:T(1024)(128)(4,1)}), s8[4194304]{0:T(1024)(128)(4,1)S(1)}, s32[]{:S(2)}) async-start(s8[8388608]{0:T(1024)(128)(4,1)} %bitcast.460), calls=%async_computation.12 | async-start | bytes 8388608
  540.4 30.4 %slice-start.2 = ((s8[8388608]{0:T(1024)(128)(4,1)}), s8[4194304]{0:T(1024)(128)(4,1)S(1)}, s32[]{:S(2)}) async-start(s8[8388608]{0:T(1024)(128)(4,1)} %bitcast.454), calls=%async_computation.6 | async-start | bytes 8388608
  555.6 30.4 %slice-start = ((s8[8388608]{0:T(1024)(128)(4,1)}), s8[4194304]{0:T(1024)(128)(4,1)S(1)}, s32[]{:S(2)}) async-start(s8[8388608]{0:T(1024)(128)(4,1)} %bitcast.452), calls=%async_computation.4 | async-start | bytes 8388608
  601.6 187.3 %copy-start.46 = (f32[3,4,2,16,128]{4,3,2,1,0:T(8,128)}, f32[3,4,2,16,128]{4,3,2,1,0:T(8,128)S(1)}, u32[]{:S(2)}) copy-start(f32[3,4,2,16,128]{4,3,2,1,0:T(8,128)S(1)} %fusion.293) | copy-start | bytes 589828
  602.0 186.9 %copy-start.7 = (f32[128,128,8]{1,2,0:T(8,128)}, f32[128,128,8]{1,2,0:T(8,128)S(1)}, u32[]{:S(2)}) copy-start(f32[128,128,8]{1,2,0:T(8,128)S(1)} %get-tuple-element.505) | copy-start | bytes 1572868
  602.0 186.9 %copy-start.9 = (f32[128,128,8]{1,2,0:T(8,128)}, f32[128,128,8]{1,2,0:T(8,128)S(1)}, u32[]{:S(2)}) copy-start(f32[128,128,8]{1,2,0:T(8,128)S(1)} %get-tuple-element.506) | copy-start | bytes 1572868
  602.0 186.9 %copy-start.11 = (f32[128,128,8]{1,2,0:T(8,128)}, f32[128,128,8]{1,2,0:T(8,128)S(1)}, u32[]{:S(2)}) copy-start(f32[128,128,8]{1,2,0:T(8,128)S(1)} %get-tuple-element.507) | copy-start | bytes 1572868
  846.3 23.2 %all-to-all-start.1 = ((f32[4,1,49152]{2,1,0:T(1,128)}), f32[4,1,49152]{2,1,0:T(1,128)S(1)}, u32[]{:S(2)}, u32[]{:S(2)}) async-start(f32[4,1,49152]{2,1,0:T(1,128)} %reshape.1744), calls=%async_computation.1 | async-start | bytes 1572864 | tf_op jit(solution)/shard_map/all_to_all | solution.py:189
  850.4 27.9 %copy-start.101 = (f32[32]{0:T(128)}, f32[32]{0:T(128)S(1)}, u32[]{:S(2)}) copy-start(f32[32]{0:T(128)S(1)} %fusion.558) | copy-start | bytes 388
  850.4 27.9 %copy-start.103 = (f32[128]{0:T(128)}, f32[128]{0:T(128)S(1)}, u32[]{:S(2)}) copy-start(f32[128]{0:T(128)S(1)} %fusion.472) | copy-start | bytes 1540
  880.4 24.0 %copy-start.100 = (f32[32]{0:T(128)S(1)}, f32[32]{0:T(128)}, u32[]{:S(2)}) copy-start(f32[32]{0:T(128)} %fusion.470) | copy-start | bytes 388
  880.4 24.0 %copy-start.102 = (f32[32]{0:T(128)S(1)}, f32[32]{0:T(128)}, u32[]{:S(2)}) copy-start(f32[32]{0:T(128)} %copy-done.101) | copy-start | bytes 388
  880.4 24.0 %copy-start.104 = (f32[128]{0:T(128)S(1)}, f32[128]{0:T(128)}, u32[]{:S(2)}) copy-start(f32[128]{0:T(128)} %copy-done.103) | copy-start | bytes 1540
  880.4 24.0 %copy-start.105 = (f32[128]{0:T(128)S(1)}, f32[128]{0:T(128)}, u32[]{:S(2)}) copy-start(f32[128]{0:T(128)} %fusion.469) | copy-start | bytes 1540
  954.0 16.3 %all-to-all-start.3 = ((f32[8,1,24576]{2,1,0:T(1,128)}), f32[8,1,24576]{2,1,0:T(1,128)S(1)}, u32[]{:S(2)}, u32[]{:S(2)}) async-start(f32[8,1,24576]{2,1,0:T(1,128)} %reshape.1748), calls=%async_computation.3 | async-start | bytes 1572864 | tf_op jit(solution)/shard_map/all_to_all | solution.py:229
  (98 other events, 1390.6 us)
where the time goes:
time: 1030 us
  matrix products  517 us (50%)
  other arithmetic  267 us (26%)
  local copies, waits for them, and re-layouts  129 us (13%)
  blocking collectives  51.4 us (5%)
  waiting for transfers between devices  34.4 us (3%)
  starting transfers between devices  26.4 us (3%)
    dot_general x21, matrix products, pair_totals(): return jnp.einsum('nij,qnj->qni', weights, far_loads, precision=highest)  294 us
    reduce_sum x6, other arithmetic, pair_totals(): jnp.sum(separation * separation, axis=0)  209 us
    dot_general x1, matrix products, far_field(): cubes = jnp.einsum('niab,qnic->qnabc', planar, lifted, precision=highest)  174 us
    dot_general x1, matrix products, far_field(): jnp.einsum('qnabc,niab->qnic', cubes, planar, precision=highest)  21.2 us
  transfers between devices with their start and end apart: 14, of which 6 were waited for; matrix products, arithmetic and copies ran while one was open for 11% of the time, Pallas kernels for 0%

commit v1 on v0

--- a/solution.py
+++ b/solution.py
@@ -1,106 +1,197 @@
+import functools
 import math
 
 import jax
 import jax.numpy as jnp
+import numpy as np
 from jax import lax
+from jax.experimental import pallas as pl
+from jax.experimental.pallas import tpu as pltpu
 from jax.sharding import PartitionSpec as P
 
 GRID = 128
 CELL = 8
 STEPS = 3
 
-
-highest = lax.Precision.HIGHEST
 step_pace = 0.06
 drift_gain = 1.0
 couple_gain = 0.5
 bin_rate = 1.0
-face_moves = ((0, 1.0), (0, -1.0), (1, 1.0), (1, -1.0), (2, 1.0), (2, -1.0))
-
-
-def with_halo(block, sides, width):
-    for axis, dim in sides:
+RATE = 2.0 / (CELL * CELL) * math.log2(math.e)
+FACES = (None, (0, 1), (0, -1), (1, 1), (1, -1), (2, 1), (2, -1))
+VMEM_LIMIT = 56 * 1024 * 1024
+
+
+def split_three(value):
+    high = value.astype(jnp.bfloat16).astype(jnp.float32)
+    rest = value - high
+    middle = rest.astype(jnp.bfloat16).astype(jnp.float32)
+    return high, middle, rest - middle
+
+
+def split_two(value):
+    high = value.astype(jnp.bfloat16)
+    return high, (value - high.astype(jnp.float32)).astype(jnp.bfloat16)
+
+
+def near_kernel(dims, flags, place, load, place_xl, place_xh, place_yl, place_yh,
+                load_xl, load_xh, load_yl, load_yh, place_out, spin_out,
+                far_rows, load_rows, near_rows, sums):
+    nx, ny, nz, slots = dims
+    half = nz // 2
+    wide = ny + 2
+
+    def fill(places, loads, column, own):
+        base = column * nz * 8
+        xyz = [places[d] - 0.5 * CELL for d in range(3)]
+        torque = [loads[d] for d in range(3)]
+        square = -RATE * (xyz[0] * xyz[0] + xyz[1] * xyz[1] + xyz[2] * xyz[2])
+        one = jnp.ones_like(square)
+        zero = jnp.zeros_like(square)
+        moment = [torque[1] * xyz[2] - torque[2] * xyz[1],
+                  torque[2] * xyz[0] - torque[0] * xyz[2],
+                  torque[0] * xyz[1] - torque[1] * xyz[0]]
+        for row, value in enumerate(xyz + [one, square, zero, zero, zero]):
+            far_rows[pl.ds(base + row, nz, stride=8), :] = value
+        for row, value in enumerate(torque + moment + [loads[3], zero]):
+            load_rows[pl.ds(base + row, nz, stride=8), :] = value
+        if own is not None:
+            scaled = [2.0 * RATE * value for value in xyz]
+            for row, value in enumerate(scaled + [square, one, zero, zero, zero]):
+                near_rows[pl.ds(own * nz * 8 + row, nz, stride=8), :] = value
+
+    for ix in range(nx):
+        for iy in range(ny):
+            fill([place[d, ix, iy] for d in range(3)], [load[d, ix, iy] for d in range(4)],
+                 (ix + 1) * wide + iy + 1, ix * ny + iy)
+    for iy in range(ny):
+        fill([place_xl[d, 0, iy] for d in range(3)], [load_xl[d, 0, iy] for d in range(4)], iy + 1, None)
+        fill([place_xh[d, 0, iy] for d in range(3)], [load_xh[d, 0, iy] for d in range(4)],
+             (nx + 1) * wide + iy + 1, None)
+    for ix in range(nx):
+        fill([place_yl[d, ix, 0] for d in range(3)], [load_yl[d, ix, 0] for d in range(4)],
+             (ix + 1) * wide, None)
+        fill([place_yh[d, ix, 0] for d in range(3)], [load_yh[d, ix, 0] for d in range(4)],
+             (ix + 1) * wide + ny + 1, None)
+
+    row_id = lax.broadcasted_iota(jnp.int32, (8, slots), 0)
+
+    def rows_of(entries):
+        value = jnp.zeros((8, slots), jnp.float32)
+        for row, entry in entries:
+            value = jnp.where(row_id == row, jnp.float32(entry), value)
+        return value
+
+    pad = jnp.zeros((16, slots), jnp.float32)
+    blank = jnp.zeros((64, slots), jnp.bfloat16)
+
+    def near_block(start):
+        high, middle, low = split_three(near_rows[pl.ds(start, 8), :])
+        return jnp.concatenate([high, high, high, middle, middle, low, pad], 0)
+
+    def far_block(start, face):
+        value = far_rows[pl.ds(start, 8), :]
+        if face is not None:
+            axis, sign = face
+            along = far_rows[pl.ds(start + axis, 1), :]
+            value = value + rows_of([(axis, CELL * sign), (4, -RATE * CELL * CELL)])
+            value = value + rows_of([(4, -2.0 * RATE * CELL * sign)]) * along
+        high, middle, low = split_three(value)
+        return jnp.concatenate([high, middle, low, high, middle, high, pad], 0).astype(jnp.bfloat16)
+
+    def load_block(start, face, gate):
+        value = load_rows[pl.ds(start, 8), :]
+        if face is not None:
+            axis, sign = face
+            after, before = (axis + 1) % 3, (axis + 2) % 3
+            value = value + rows_of([(3 + after, CELL * sign)]) * load_rows[pl.ds(start + before, 1), :]
+            value = value - rows_of([(3 + before, CELL * sign)]) * load_rows[pl.ds(start + after, 1), :]
+            value = value * gate
+        high, low = split_two(value)
+        return jnp.concatenate([high.astype(jnp.float32), low.astype(jnp.float32)], 0).astype(jnp.bfloat16)
+
+    def pair(index, carry):
+        column = index // half
+        level = index % half
+        ix = column // ny
+        iy = column % ny
+        cells = [column * nz + level, column * nz + level + half]
+        blocks = jnp.concatenate([near_block(cell * 8) for cell in cells], 0)
+        near_side = jnp.transpose(blocks).astype(jnp.bfloat16)
+        loads = [[], []]
+        weights = [[], []]
+        for face_id, face in enumerate(FACES):
+            shift = [0, 0, 0]
+            if face is not None:
+                shift[face[0]] = face[1]
+            far_column = (ix + 1 + shift[0]) * wide + iy + 1 + shift[1]
+            starts = [(far_column * nz + (level + which * half + shift[2] + nz) % nz) * 8 for which in range(2)]
+            starts = [pl.multiple_of(start, 8) for start in starts]
+            far_side = [far_block(start, face) for start in starts]
+            right = jnp.concatenate([jnp.concatenate([far_side[0], blank], 1),
+                                     jnp.concatenate([blank, far_side[1]], 1)], 0)
+            exponent = jnp.dot(near_side, right, preferred_element_type=jnp.float32)
+            high, low = split_two(jnp.exp2(exponent))
+            for which in range(2):
+                gate = None
+                if face is not None:
+                    gate = flags[(face_id - 1) * nx * ny * nz + cells[which]].astype(jnp.float32)
+                block = load_block(starts[which], face, gate)
+                loads[which] += [block, block]
+                weights[which] += [high[:, which * slots:(which + 1) * slots],
+                                   low[:, which * slots:(which + 1) * slots]]
+        for which in range(2):
+            total = lax.dot_general(jnp.concatenate(loads[which], 1), jnp.concatenate(weights[which], 1),
+                                    (((1,), (1,)), ((), ())), preferred_element_type=jnp.float32)
+            sums[pl.ds(pl.multiple_of(cells[which] * 8, 8), 8), :] = total[:8] + total[8:]
+        return carry
+
+    lax.fori_loop(0, nx * ny * half, pair, 0)
+
+    for ix in range(nx):
+        for iy in range(ny):
+            base = (ix * ny + iy) * nz * 8
+            rows = [sums[pl.ds(base + row, nz, stride=8), :] for row in range(7)]
+            filled = load[3, ix, iy]
+            xyz = [place[d, ix, iy] - 0.5 * CELL for d in range(3)]
+            for d in range(3):
+                after, before = (d + 1) % 3, (d + 2) % 3
+                drive = rows[after] * xyz[before] - rows[before] * xyz[after] - rows[3 + d]
+                velocity = drift_gain / slots * drive * filled
+                place_out[d, ix, iy] = place[d, ix, iy] + step_pace * CELL * velocity
+                torque = load[d, ix, iy]
+                spin_out[d, ix, iy] = torque + couple_gain / slots * (filled * rows[d] - rows[6] * torque)
+
+
+def near_step(places, loads, flags, place_rim, load_rim):
+    _, nx, ny, nz, slots = places.shape
+    cells = nx * ny * nz
+    vmem = pl.BlockSpec(memory_space=pltpu.VMEM)
+    ext = (nx + 2) * (ny + 2) * nz * 8
+    return pl.pallas_call(
+        functools.partial(near_kernel, (nx, ny, nz, slots)),
+        out_shape=[jax.ShapeDtypeStruct(places.shape, jnp.float32)] * 2,
+        in_specs=[pl.BlockSpec(memory_space=pltpu.SMEM)] + [vmem] * 10,
+        out_specs=[vmem] * 2,
+        scratch_shapes=[pltpu.VMEM((ext, slots), jnp.float32), pltpu.VMEM((ext, slots), jnp.float32),
+                        pltpu.VMEM((cells * 8, slots), jnp.float32), pltpu.VMEM((cells * 8, slots), jnp.float32)],
+        compiler_params=pltpu.CompilerParams(vmem_limit_bytes=VMEM_LIMIT),
+        name="near_step",
+    )(flags, places, loads, *place_rim, *load_rim)
+
+
+def rim(block):
+    out = []
+    for axis, dim in (("row", 1), ("col", 2)):
         count = lax.axis_size(axis)
-        forward = [(i, i + 1) for i in range(count - 1)]
-        forward.append((count - 1, 0))
+        forward = [(i, (i + 1) % count) for i in range(count)]
         backward = [(target, source) for source, target in forward]
-        low = lax.ppermute(
-            lax.slice_in_dim(block, block.shape[dim] - width, None, axis=dim), axis, forward
-        )
-        high = lax.ppermute(lax.slice_in_dim(block, 0, width, axis=dim), axis, backward)
-        block = jnp.concatenate([low, block, high], axis=dim)
-    return block
-
-
-def cross_product(left_vec, right_vec):
-    return jnp.stack(
-        [
-            left_vec[1] * right_vec[2] - left_vec[2] * right_vec[1],
-            left_vec[2] * right_vec[0] - left_vec[0] * right_vec[2],
-            left_vec[0] * right_vec[1] - left_vec[1] * right_vec[0],
-        ]
-    )
-
-
-def make_loads(places, torque, filled):
-    return jnp.concatenate(
-        [torque * filled, cross_product(torque, places) * filled, filled[None]], 0
-    )
-
-
-def pair_totals(near_places, far_places, far_loads, offset_vec):
-    separation = (
-        near_places[:, :, :, None] - far_places[:, :, None, :] - offset_vec[:, None, None, None]
-    )
-    weights = jnp.exp(-jnp.sum(separation * separation, axis=0) * (2.0 / (CELL * CELL)))
-    return jnp.einsum("nij,qnj->qni", weights, far_loads, precision=highest)
-
-
-def neighbours(extended):
-    centre = extended[:, 1:-1, 1:-1]
-    return [
-        centre,
-        extended[:, 2:, 1:-1],
-        extended[:, :-2, 1:-1],
-        extended[:, 1:-1, 2:],
-        extended[:, 1:-1, :-2],
-        jnp.roll(centre, -1, axis=3),
-        jnp.roll(centre, 1, axis=3),
-    ]
-
-
-def near_field(places, torque, filled, face_flags, far_place_list, far_load_list):
-    layout = places.shape
-    cell_count = layout[1] * layout[2] * layout[3]
-
-    def flatten(values):
-        return values.reshape(values.shape[0], cell_count, layout[4])
-
-    drives = jnp.zeros(layout, jnp.float32)
-    twists = jnp.zeros(layout, jnp.float32)
-    weight_total = jnp.zeros(layout[1:], jnp.float32)
-    for face_id in range(7):
-        if face_id == 0:
-            offset_vec = jnp.zeros((3,), jnp.float32)
-            face_gate = jnp.ones(layout[1:4] + (1,), jnp.float32)
-        else:
-            axis_id, face_sign = face_moves[face_id - 1]
-            offset_vec = jnp.zeros((3,), jnp.float32).at[axis_id].set(face_sign * CELL)
-            face_gate = face_flags[face_id - 1].astype(jnp.float32)[..., None]
-        totals = pair_totals(
-            flatten(places),
-            flatten(far_place_list[face_id]),
-            flatten(far_load_list[face_id]),
-            offset_vec,
-        )
-        totals = totals.reshape((7,) + layout[1:])
-        lever = places - offset_vec[:, None, None, None, None]
-        drives = drives + face_gate * (cross_product(totals[0:3], lever) - totals[3:6])
-        twists = twists + face_gate * totals[0:3]
-        weight_total = weight_total + face_gate * totals[6]
-    velocity = drift_gain / layout[4] * drives * filled
-    spin_near = (torque + couple_gain / layout[4] * (twists - weight_total * torque)) * filled
-    return (velocity, spin_near)
+        out.append(lax.ppermute(lax.slice_in_dim(block, block.shape[dim] - 1, None, axis=dim), axis, forward))
+        out.append(lax.ppermute(lax.slice_in_dim(block, 0, 1, axis=dim), axis, backward))
+    return out
+
+
+highest = lax.Precision.HIGHEST
 
 
 def bin_weights(coordinate):
@@ -273,16 +364,12 @@
     slot_count = positions.shape[4]
     filled = (jnp.arange(slot_count, dtype=jnp.int32) < counts[..., None]).astype(jnp.float32)
     places = positions
-    spin_near = jnp.zeros(positions.shape, jnp.float32)
+    loads = jnp.concatenate([torques * filled, filled[None]], 0)
+    load_rim = rim(loads)
+    flags = neighbour_flags.reshape(-1)
+    spin_near = None
     for step_id in range(STEPS):
-        loads = make_loads(places, torques, filled)
-        state_rim = with_halo(jnp.concatenate([places, loads], 0), (("row", 1), ("col", 2)), 1)
-        place_rim = state_rim[0:3]
-        load_rim = state_rim[3:10]
-        velocity, spin_near = near_field(
-            places, torques, filled, neighbour_flags, neighbours(place_rim), neighbours(load_rim)
-        )
-        places = places + step_pace * CELL * velocity
+        places, spin_near = near_step(places, loads, flags, rim(places), load_rim)
     far_spin = far_field(places, torques, filled)
     return (places, spin_near + far_spin * filled)
 

time: 1030 us -> 588 us (0.57)
  matrix products: 517 us -> 213 us
  other arithmetic: 267 us -> 27.7 us
  Pallas kernels: 0 us -> 118 us
  local copies, waits for them, and re-layouts: 129 us -> 97.5 us
    dot_general x21 -> x0, matrix products: 294 us -> none  [pair_totals(): return jnp.einsum('nij,qnj->qni', weights, far_loads, precision=highest)]
    reduce_sum x6 -> x0, other arithmetic: 209 us -> none  [pair_totals(): jnp.sum(separation * separation, axis=0)]
    pallas_call x0 -> x3, Pallas kernels: none -> 118 us  [near_step(): pl.pallas_call(functools.partial(near_kernel, (nx, ny, nz, slots)), out_s...]
    slice x96 -> x6, local copies, waits for them, and re-layouts: 35.8 us -> 4.46 us  [rim(): lax.slice_in_dim(block, 0, 1, axis=dim)]
    ppermute x12 -> x16, starting transfers between devices: 19.2 us -> 27.8 us  [the longest x8 24.4 us: rim(): lax.ppermute(lax.slice_in_dim(block, 0, 1, axis=dim), axis, backward)]
    unnamed x272 -> x88, local copies, waits for them, and re-layouts: 18.6 us -> 22.4 us
  transfers between devices with their start and end apart: 14 -> 18, of which waited for: 6 -> 5; matrix products, arithmetic and copies ran while one was open for 11% -> 1% of each run, Pallas kernels for 0% -> 0%
where the time goes in v1:
time: 588 us; the launch traced here: 582 us
  matrix products  213 us (36%)
  Pallas kernels  118 us (20%)
  local copies, waits for them, and re-layouts  97.5 us (17%)
  blocking collectives  51.4 us (9%)
  waiting for transfers between devices  37.1 us (6%)
  starting transfers between devices  35 us (6%)
  other arithmetic  27.7 us (5%)
    dot_general x1, matrix products, far_field(): cubes = jnp.einsum('niab,qnic->qnabc', planar, lifted, precision=highest)  169 us
    pallas_call x3, Pallas kernels, near_step(): pl.pallas_call(functools.partial(near_kernel, (nx, ny, nz, slots)), out_s...  118 us
    ppermute x8, starting transfers between devices, rim(): lax.ppermute(lax.slice_in_dim(block, 0, 1, axis=dim), axis, backward)  24.4 us
    unnamed x88, local copies, waits for them, and re-layouts  22.4 us
    dot_general x1, matrix products, far_field(): jnp.einsum('qnabc,niab->qnic', cubes, planar, precision=highest)  21 us
    all_to_all x1, blocking collectives, solve_half(): lax.all_to_all(pencil, 'row', split_axis=4, concat_axis=2, tiled=True)  20 us
    all_to_all x1, waiting for transfers between devices, solve_half(): lax.all_to_all(pencil, 'row', split_axis=2, concat_axis=4, tiled=True)  17.4 us
    all_to_all x1, blocking collectives, solve_half(): lax.all_to_all(spectrum, 'col', split_axis=2, concat_axis=4, tiled=True)  16 us
  transfers between devices with their start and end apart: 18, of which 5 were waited for; matrix products, arithmetic and copies ran while one was open for 1% of the time, Pallas kernels for 0%

profile of v1, /device:TPU:0, one launch (start us, length us, event | category | flops | bytes accessed | tf_op | source)
XLA Modules:
  0.0 581.8 jit_solution(611999076906963199)
XLA Ops:
  1.5 3.1 collective-permute-start
  4.6 2.1 collective-permute-start.1
  9.4 2.6 collective-permute-start.7
  13.5 2.6 collective-permute-start.3
  16.1 3.8 collective-permute-start.5
  23.3 39.5 %near_step.3 = (f32[3,4,2,16,128]{4,3,2,1,0:T(8,128)}, f32[3,4,2,16,128]{4,3,2,1,0:T(8,128)}) custom-call(s32[768]{0:T(1024)} %reshape.912.flags, f32[3,4,2,16,128]{4,3,2,1,0:T(8,128)} %place.1, f32[4,4,2,16,128]{4,3,2,1,0:T(8,128)} %pad_maximum_fusion.4.load, f32[3,1,2,16,128]{4,3,2,1,0:T(8,128)} %copy-done.21, f32[3,1,2,16,128]{4,3,2,1,0:T(8,128)} %copy-done.22, ...), custom_call_target="tpu_custom_call" | custom-call | tf_op jit(solution)/shard_map/near_step/pallas_call | solution.py:171
  64.6 4.2 collective-permute-start.9
  68.8 2.6 collective-permute-start.11
  71.5 3.1 collective-permute-done.10.place_yl
  75.9 39.5 %near_step.4 = (f32[3,4,2,16,128]{4,3,2,1,0:T(8,128)}, f32[3,4,2,16,128]{4,3,2,1,0:T(8,128)}) custom-call(s32[768]{0:T(1024)} %reshape.912.flags, f32[3,4,2,16,128]{4,3,2,1,0:T(8,128)} %get-tuple-element.6.place, f32[4,4,2,16,128]{4,3,2,1,0:T(8,128)} %pad_maximum_fusion.4.load, f32[3,1,2,16,128]{4,3,2,1,0:T(8,128)} %copy-done.25, ...), custom_call_target="tpu_custom_call" | custom-call | tf_op jit(solution)/shard_map/near_step/pallas_call | solution.py:171
  117.2 3.8 collective-permute-start.13
  121.0 2.6 collective-permute-start.15
  123.9 2.1 collective-permute-done.14.place_yl
  127.3 39.5 %near_step.5 = (f32[3,4,2,16,128]{4,3,2,1,0:T(8,128)}, f32[3,4,2,16,128]{4,3,2,1,0:T(8,128)}) custom-call(s32[768]{0:T(1024)} %reshape.912.flags, f32[3,4,2,16,128]{4,3,2,1,0:T(8,128)} %get-tuple-element.7.place, f32[4,4,2,16,128]{4,3,2,1,0:T(8,128)} %pad_maximum_fusion.4.load, f32[3,1,2,16,128]{4,3,2,1,0:T(8,128)} %copy-done.23, ...), custom_call_target="tpu_custom_call" | custom-call | tf_op jit(solution)/shard_map/near_step/pallas_call | solution.py:171
  168.0 168.6 %fusion.2 = f32[128,3,8,8,8]{4,2,3,1,0:T(8,128)} fusion(f32[128,128,8]{1,2,0:T(8,128)S(1)} %get-tuple-element.112, f32[128,128,8]{1,2,0:T(8,128)S(1)} %get-tuple-element.113, f32[128,128,8]{1,2,0:T(8,128)S(1)} %get-tuple-element.111, f32[3,128,128]{2,0,1:T(4,128)S(1)} %copy.134), kind=kOutput, calls=%fused_computation.2 | convolution fusion | flops 303431680 | bytes 2555904 | tf_op jit(solution)/shard_map/niab,qnic->qnabc/dot_general | solution.py:345
  336.6 13.0 %copy.135 = f32[3,4,2,16,8,8,8]{6,3,5,2,4,1,0:T(8,128)} copy(f32[3,4,2,16,8,8,8]{5,6,4,0,3,2,1:T(8,128)} %bitcast.224) | data formatting | bytes 1572864 | tf_op jit(solution)/shard_map/reshape | solution.py:347
  349.7 9.1 %reshape.914 = f32[3,32,16,128]{3,2,1,0:T(8,128)S(1)} reshape(f32[3,4,8,2,8,16,8]{6,5,4,3,2,1,0:T(8,128)} %bitcast.225) | data formatting | bytes 1572864 | tf_op jit(solution)/shard_map/reshape | solution.py:349
  362.0 2.8 copy.138
  364.8 2.1 reshape.928
  367.0 16.0 %all_to_all.60 = f32[8,1,24576]{2,1,0:T(1,128)S(1)} all-to-all(f32[8,1,24576]{2,1,0:T(1,128)} %reshape.928), channel_id=1, replica_groups=mesh['row'=4,'col'=8] {'col'}, dimensions={0} | all-to-all | bytes 1572864 | tf_op jit(solution)/shard_map/all_to_all | solution.py:274
  383.5 3.7 reduce.1
  387.2 2.2 reshape.929
  390.3 2.7 fusion.72
  393.1 2.7 fusion.74
  395.8 2.7 fusion.21
  398.5 2.7 fusion.22
  402.5 2.1 copy.146
  404.7 2.5 reshape.930
  407.1 3.5 all-to-all-start.1
  412.9 17.4 %all-to-all-done.1 = f32[4,1,49152]{2,1,0:T(1,128)S(1)} async-done(((f32[4,1,49152]{2,1,0:T(1,128)}), f32[4,1,49152]{2,1,0:T(1,128)S(1)}, u32[]{:S(2)}, u32[]{:S(2)}) %all-to-all-start.1) | async-done | bytes 786464 | tf_op jit(solution)/shard_map/all_to_all | solution.py:280
  430.4 3.8 reduce.2
  434.2 2.2 reshape.931
  436.4 2.0 copy.220
  443.5 15.3 %all-gather = f32[2,3,128,1,128]{4,2,1,3,0:T(8,128)S(1)} all-gather(f32[2,3,32,1,128]{4,2,1,3,0:T(8,128)S(1)} %pad_maximum_fusion.5), channel_id=2, replica_groups=mesh['row'=4,'col'=8] {'row'}, dimensions={2}, use_global_device_ids=true | all-gather | bytes 491520 | tf_op jit(solution)/shard_map/all_gather | solution.py:296
  465.8 2.2 copy.161
  468.0 2.5 reshape.932
  470.5 20.0 %all_to_all.61 = f32[4,1,49152]{2,1,0:T(1,128)S(1)} all-to-all(f32[4,1,49152]{2,1,0:T(1,128)} %reshape.932), channel_id=1, replica_groups=mesh['row'=4,'col'=8] {'row'}, dimensions={0} | all-to-all | bytes 1572864 | tf_op jit(solution)/shard_map/all_to_all | solution.py:315
  490.5 3.8 reduce.3
  494.3 2.2 reshape.933
  504.0 2.1 copy.163
  506.1 2.1 reshape.934
  508.3 3.8 all-to-all-start.3
  512.0 12.5 %all-to-all-done.3 = f32[8,1,24576]{2,1,0:T(1,128)S(1)} async-done(((f32[8,1,24576]{2,1,0:T(1,128)}), f32[8,1,24576]{2,1,0:T(1,128)S(1)}, u32[]{:S(2)}, u32[]{:S(2)}) %all-to-all-start.3) | async-done | bytes 786464 | tf_op jit(solution)/shard_map/all_to_all | solution.py:320
  524.5 3.7 reduce.4
  528.2 2.2 reshape.935
  536.8 8.6 %reshape.915 = f32[3,4,8,2,8,16,8]{6,5,4,3,2,1,0:T(8,128)} reshape(f32[3,32,16,128]{3,2,1,0:T(8,128)S(1)} %fusion.16) | data formatting | bytes 1572864 | tf_op jit(solution)/shard_map/reshape | solution.py:353
  545.4 14.2 %copy.189 = f32[3,4,2,16,8,8,8]{5,6,4,0,3,2,1:T(8,128)} copy(f32[3,4,2,16,8,8,8]{6,3,5,2,4,1,0:T(8,128)} %bitcast.226) | data formatting | bytes 1572864 | tf_op jit(solution)/shard_map/reshape | solution.py:355
  559.6 21.0 %fusion.11 = f32[128,128,3]{1,2,0:T(4,128)S(1)} fusion(f32[3,128,8,8,8]{3,4,2,0,1:T(8,128)} %bitcast.223, f32[128,128,8]{1,2,0:T(8,128)S(1)} %copy-done.3, f32[128,128,8]{1,2,0:T(8,128)S(1)} %copy-done.5, f32[128,128,8]{1,2,0:T(8,128)S(1)} %copy-done.1), kind=kOutput, calls=%fused_computation.15 | convolution fusion | flops 303775744 | bytes 2555904 | tf_op jit(solution)/shard_map/qnabc,niab->qnic/dot_general | solution.py:357
  (195 shorter events, 50.7 us)
Async XLA Ops:
  0.6 11.4 %copy-start.7 = (f32[3,4,2,16,128]{4,3,2,1,0:T(8,128)S(1)}, f32[3,4,2,16,128]{4,3,2,1,0:T(8,128)}, u32[]{:S(2)}) copy-start(f32[3,4,2,16,128]{4,3,2,1,0:T(8,128)} %place.1) | copy-start | bytes 589828
  0.6 12.2 %copy-start.27 = (s32[6,4,2,16]{3,2,1,0:T(2,128)S(1)}, s32[6,4,2,16]{3,2,1,0:T(2,128)}, u32[]{:S(2)}) copy-start(s32[6,4,2,16]{3,2,1,0:T(2,128)} %param.7) | copy-start | bytes 9220
  1.5 12.0 %collective-permute-start = (f32[3,1,2,16,128]{4,3,2,1,0:T(8,128)S(1)}, f32[3,1,2,16,128]{4,3,2,1,0:T(8,128)S(1)}, u32[]{:S(2)}, u32[]{:S(2)}) collective-permute-start(f32[3,1,2,16,128]{4,3,2,1,0:T(8,128)S(1)} %get-tuple-element.61), channel_id=1, source_target_pairs={{0,8},{8,16},{16,24},{24,0},{1,9},{9,17},{17,25},{25,1},{2,10},{10... | collective-permute-start | bytes 147464 | tf_op jit(solution)/shard_map/ppermute | solution.py:189
  4.6 8.9 %collective-permute-start.1 = (f32[3,1,2,16,128]{4,3,2,1,0:T(8,128)S(1)}, f32[3,1,2,16,128]{4,3,2,1,0:T(8,128)S(1)}, u32[]{:S(2)}, u32[]{:S(2)}) collective-permute-start(f32[3,1,2,16,128]{4,3,2,1,0:T(8,128)S(1)} %get-tuple-element.60), channel_id=1, source_target_pairs={{8,0},{16,8},{24,16},{0,24},{9,1},{17,9},{25,17},{1,25},{10,2},{18... | collective-permute-start | bytes 147464 | tf_op jit(solution)/shard_map/ppermute | solution.py:190
  8.2 3.8 copy-start.12
  9.2 6.9 %collective-permute-start.4 = (f32[4,1,2,16,128]{4,3,2,1,0:T(8,128)S(1)}, f32[4,1,2,16,128]{4,3,2,1,0:T(8,128)S(1)}, u32[]{:S(2)}, u32[]{:S(2)}) collective-permute-start(f32[4,1,2,16,128]{4,3,2,1,0:T(8,128)S(1)} %get-tuple-element.46), channel_id=1, source_target_pairs={{0,8},{8,16},{16,24},{24,0},{1,9},{9,17},{17,25},{25,1},{2,10},{10... | collective-permute-start | bytes 196616 | tf_op jit(solution)/shard_map/ppermute | solution.py:189
  9.3 12.5 %collective-permute-start.6 = (f32[4,4,1,16,128]{4,3,2,1,0:T(8,128)S(1)}, f32[4,4,1,16,128]{4,3,2,1,0:T(8,128)S(1)}, u32[]{:S(2)}, u32[]{:S(2)}) collective-permute-start(f32[4,4,1,16,128]{4,3,2,1,0:T(8,128)S(1)} %get-tuple-element.44), channel_id=1, source_target_pairs={{0,1},{1,2},{2,3},{3,4},{4,5},{5,6},{6,7},{7,0},{8,9},{9,10},{10,1... | collective-permute-start | bytes 393224 | tf_op jit(solution)/shard_map/ppermute | solution.py:189
  9.4 12.5 %collective-permute-start.7 = (f32[4,4,1,16,128]{4,3,2,1,0:T(8,128)S(1)}, f32[4,4,1,16,128]{4,3,2,1,0:T(8,128)S(1)}, u32[]{:S(2)}, u32[]{:S(2)}) collective-permute-start(f32[4,4,1,16,128]{4,3,2,1,0:T(8,128)S(1)} %get-tuple-element.43), channel_id=1, source_target_pairs={{1,0},{2,1},{3,2},{4,3},{5,4},{6,5},{7,6},{0,7},{9,8},{10,9},{11,1... | collective-permute-start | bytes 393224 | tf_op jit(solution)/shard_map/ppermute | solution.py:190
  13.5 8.4 %copy-start.21 = (f32[3,1,2,16,128]{4,3,2,1,0:T(8,128)}, f32[3,1,2,16,128]{4,3,2,1,0:T(8,128)S(1)}, u32[]{:S(2)}) copy-start(f32[3,1,2,16,128]{4,3,2,1,0:T(8,128)S(1)} %collective-permute-done.place_xl) | copy-start | bytes 147460
  13.5 8.4 %collective-permute-start.2 = (f32[3,4,1,16,128]{4,3,2,1,0:T(8,128)S(1)}, f32[3,4,1,16,128]{4,3,2,1,0:T(8,128)S(1)}, u32[]{:S(2)}, u32[]{:S(2)}) collective-permute-start(f32[3,4,1,16,128]{4,3,2,1,0:T(8,128)S(1)} %get-tuple-element.59), channel_id=1, source_target_pairs={{0,1},{1,2},{2,3},{3,4},{4,5},{5,6},{6,7},{7,0},{8,9},{9,10},{10,1... | collective-permute-start | bytes 294920 | tf_op jit(solution)/shard_map/ppermute | solution.py:189
  13.5 8.4 %copy-start.22 = (f32[3,1,2,16,128]{4,3,2,1,0:T(8,128)}, f32[3,1,2,16,128]{4,3,2,1,0:T(8,128)S(1)}, u32[]{:S(2)}) copy-start(f32[3,1,2,16,128]{4,3,2,1,0:T(8,128)S(1)} %collective-permute-done.1.place_xh) | copy-start | bytes 147460
  13.5 8.4 %collective-permute-start.3 = (f32[3,4,1,16,128]{4,3,2,1,0:T(8,128)S(1)}, f32[3,4,1,16,128]{4,3,2,1,0:T(8,128)S(1)}, u32[]{:S(2)}, u32[]{:S(2)}) collective-permute-start(f32[3,4,1,16,128]{4,3,2,1,0:T(8,128)S(1)} %get-tuple-element.58), channel_id=1, source_target_pairs={{1,0},{2,1},{3,2},{4,3},{5,4},{6,5},{7,6},{0,7},{9,8},{10,9},{11,1... | collective-permute-start | bytes 294920 | tf_op jit(solution)/shard_map/ppermute | solution.py:190
  16.1 5.8 copy-start.10
  16.1 5.7 collective-permute-start.5
  21.9 0.7 copy-start.8
  64.5 6.9 %collective-permute-start.8 = (f32[3,1,2,16,128]{4,3,2,1,0:T(8,128)S(1)}, f32[3,1,2,16,128]{4,3,2,1,0:T(8,128)S(1)}, u32[]{:S(2)}, u32[]{:S(2)}) collective-permute-start(f32[3,1,2,16,128]{4,3,2,1,0:T(8,128)S(1)} %get-tuple-element.57), channel_id=1, source_target_pairs={{0,8},{8,16},{16,24},{24,0},{1,9},{9,17},{17,25},{25,1},{2,10},{10... | collective-permute-start | bytes 147464 | tf_op jit(solution)/shard_map/ppermute | solution.py:189
  64.6 6.8 %collective-permute-start.9 = (f32[3,1,2,16,128]{4,3,2,1,0:T(8,128)S(1)}, f32[3,1,2,16,128]{4,3,2,1,0:T(8,128)S(1)}, u32[]{:S(2)}, u32[]{:S(2)}) collective-permute-start(f32[3,1,2,16,128]{4,3,2,1,0:T(8,128)S(1)} %get-tuple-element.56), channel_id=1, source_target_pairs={{8,0},{16,8},{24,16},{0,24},{9,1},{17,9},{25,17},{1,25},{10,2},{18... | collective-permute-start | bytes 147464 | tf_op jit(solution)/shard_map/ppermute | solution.py:190
  68.8 5.8 collective-permute-start.10
  68.8 5.8 collective-permute-start.11
  71.5 288.2 %copy-start.34 = (f32[128]{0:T(128)}, f32[128]{0:T(128)S(1)}, u32[]{:S(2)}) copy-start(f32[128]{0:T(128)S(1)} %fusion.197) | copy-start | bytes 1540
  71.5 3.1 copy-start.25
  71.5 3.1 copy-start.26
  117.2 6.7 %collective-permute-start.12 = (f32[3,1,2,16,128]{4,3,2,1,0:T(8,128)S(1)}, f32[3,1,2,16,128]{4,3,2,1,0:T(8,128)S(1)}, u32[]{:S(2)}, u32[]{:S(2)}) collective-permute-start(f32[3,1,2,16,128]{4,3,2,1,0:T(8,128)S(1)} %get-tuple-element.53), channel_id=1, source_target_pairs={{0,8},{8,16},{16,24},{24,0},{1,9},{9,17},{17,25},{25,1},{2,10},{10... | collective-permute-start | bytes 147464 | tf_op jit(solution)/shard_map/ppermute | solution.py:189
  117.2 6.6 %collective-permute-start.13 = (f32[3,1,2,16,128]{4,3,2,1,0:T(8,128)S(1)}, f32[3,1,2,16,128]{4,3,2,1,0:T(8,128)S(1)}, u32[]{:S(2)}, u32[]{:S(2)}) collective-permute-start(f32[3,1,2,16,128]{4,3,2,1,0:T(8,128)S(1)} %get-tuple-element.52), channel_id=1, source_target_pairs={{8,0},{16,8},{24,16},{0,24},{9,1},{17,9},{25,17},{1,25},{10,2},{18... | collective-permute-start | bytes 147464 | tf_op jit(solution)/shard_map/ppermute | solution.py:190
  121.0 4.9 collective-permute-start.14
  121.0 4.9 collective-permute-start.15
  123.7 236.0 %copy-start.36 = (pred[64]{0:T(512)(128)(4,1)}, pred[64]{0:T(512)(128)(4,1)S(1)}, u32[]{:S(2)}) copy-start(pred[64]{0:T(512)(128)(4,1)S(1)} %iota_compare_fusion.3) | copy-start | bytes 196
  123.8 2.1 copy-start.23
  123.9 2.1 copy-start.24
  168.0 168.6 %copy-start = (f32[128,128,8]{1,2,0:T(8,128)}, f32[128,128,8]{1,2,0:T(8,128)S(1)}, u32[]{:S(2)}) copy-start(f32[128,128,8]{1,2,0:T(8,128)S(1)} %get-tuple-element.111) | copy-start | bytes 1572868
  168.0 168.6 %copy-start.2 = (f32[128,128,8]{1,2,0:T(8,128)}, f32[128,128,8]{1,2,0:T(8,128)S(1)}, u32[]{:S(2)}) copy-start(f32[128,128,8]{1,2,0:T(8,128)S(1)} %get-tuple-element.112) | copy-start | bytes 1572868
  168.0 168.6 %copy-start.4 = (f32[128,128,8]{1,2,0:T(8,128)}, f32[128,128,8]{1,2,0:T(8,128)S(1)}, u32[]{:S(2)}) copy-start(f32[128,128,8]{1,2,0:T(8,128)S(1)} %get-tuple-element.113) | copy-start | bytes 1572868
  407.1 23.2 %all-to-all-start.1 = ((f32[4,1,49152]{2,1,0:T(1,128)}), f32[4,1,49152]{2,1,0:T(1,128)S(1)}, u32[]{:S(2)}, u32[]{:S(2)}) async-start(f32[4,1,49152]{2,1,0:T(1,128)} %reshape.930), calls=%async_computation.1 | async-start | bytes 1572864 | tf_op jit(solution)/shard_map/all_to_all | solution.py:280
  411.2 19.1 %copy-start.29 = (f32[32]{0:T(128)}, f32[32]{0:T(128)S(1)}, u32[]{:S(2)}) copy-start(f32[32]{0:T(128)S(1)} %fusion.263) | copy-start | bytes 388
  411.2 19.1 %copy-start.31 = (f32[128]{0:T(128)}, f32[128]{0:T(128)S(1)}, u32[]{:S(2)}) copy-start(f32[128]{0:T(128)S(1)} %fusion.201) | copy-start | bytes 1540
  443.4 15.5 %copy-start.28 = (f32[32]{0:T(128)S(1)}, f32[32]{0:T(128)}, u32[]{:S(2)}) copy-start(f32[32]{0:T(128)} %fusion.199) | copy-start | bytes 388
  443.4 15.5 %copy-start.33 = (f32[128]{0:T(128)S(1)}, f32[128]{0:T(128)}, u32[]{:S(2)}) copy-start(f32[128]{0:T(128)} %fusion.198) | copy-start | bytes 1540
  443.4 15.5 %copy-start.38 = (f32[8]{0:T(128)S(1)}, f32[8]{0:T(128)}, u32[]{:S(2)}) copy-start(f32[8]{0:T(128)} %fusion.262) | copy-start | bytes 100
  443.4 15.5 %copy-start.39 = (f32[8]{0:T(128)S(1)}, f32[8]{0:T(128)}, u32[]{:S(2)}) copy-start(f32[8]{0:T(128)} %fusion.200) | copy-start | bytes 100
  508.3 16.3 %all-to-all-start.3 = ((f32[8,1,24576]{2,1,0:T(1,128)}), f32[8,1,24576]{2,1,0:T(1,128)S(1)}, u32[]{:S(2)}, u32[]{:S(2)}) async-start(f32[8,1,24576]{2,1,0:T(1,128)} %reshape.934), calls=%async_computation.3 | async-start | bytes 1572864 | tf_op jit(solution)/shard_map/all_to_all | solution.py:320
  533.8 1.1 copy-start.6
  533.8 2.0 copy-start.35
  533.8 2.0 copy-start.37
  545.4 14.2 %copy-start.1 = (f32[128,128,8]{1,2,0:T(8,128)S(1)}, f32[128,128,8]{1,2,0:T(8,128)}, u32[]{:S(2)}) copy-start(f32[128,128,8]{1,2,0:T(8,128)} %copy-done) | copy-start | bytes 1572868
  545.4 14.2 %copy-start.3 = (f32[128,128,8]{1,2,0:T(8,128)S(1)}, f32[128,128,8]{1,2,0:T(8,128)}, u32[]{:S(2)}) copy-start(f32[128,128,8]{1,2,0:T(8,128)} %copy-done.2) | copy-start | bytes 1572868
  545.4 14.2 %copy-start.5 = (f32[128,128,8]{1,2,0:T(8,128)S(1)}, f32[128,128,8]{1,2,0:T(8,128)}, u32[]{:S(2)}) copy-start(f32[128,128,8]{1,2,0:T(8,128)} %copy-done.4) | copy-start | bytes 1572868
  559.6 21.1 %copy-start.13 = (f32[4,2,16,128]{3,2,1,0:T(8,128)S(1)}, f32[4,2,16,128]{3,2,1,0:T(8,128)}, u32[]{:S(2)}) copy-start(f32[4,2,16,128]{3,2,1,0:T(8,128)} %copy-done.12) | copy-start | bytes 196612
  559.6 21.1 %copy-start.14 = (f32[3,4,2,16,128]{4,3,2,1,0:T(8,128)S(1)}, f32[3,4,2,16,128]{4,3,2,1,0:T(8,128)}, u32[]{:S(2)}) copy-start(f32[3,4,2,16,128]{4,3,2,1,0:T(8,128)} %get-tuple-element.9) | copy-start | bytes 589828
  (10 other events, 6.5 us)

commit v2 on v1

--- a/solution.py
+++ b/solution.py
@@ -9,7 +9,6 @@
 from jax.experimental.pallas import tpu as pltpu
 from jax.sharding import PartitionSpec as P
 
-GRID = 128
 CELL = 8
 STEPS = 3
 
@@ -191,173 +190,318 @@
     return out
 
 
-highest = lax.Precision.HIGHEST
-
-
-def bin_weights(coordinate):
-    centres = jnp.arange(CELL, dtype=jnp.float32) + 0.5
-    separation = coordinate[..., None] - centres
+def lane_field(rows, lanes, stride, count):
+    return lax.broadcasted_iota(jnp.int32, (rows, lanes), 1) // stride % count
+
+
+def trade(parts, stride):
+    parts = list(parts)
+    rows, lanes = parts[0].shape
+    bit = 1
+    while bit < len(parts):
+        step = bit * stride
+        upper = lane_field(rows, lanes, step, 2) == 1
+        for low in range(len(parts)):
+            if low & bit == 0:
+                first, second = parts[low], parts[low | bit]
+                parts[low] = jnp.where(upper, pltpu.roll(second, step, 1), first)
+                parts[low | bit] = jnp.where(upper, second, pltpu.roll(first, lanes - step, 1))
+        bit *= 2
+    return parts
+
+
+def swap_halves(value, width):
+    lanes = value.shape[1]
+    if 2 * width == lanes:
+        return pltpu.roll(value, width, 1)
+    upper = lane_field(value.shape[0], lanes, width, 2) == 1
+    return jnp.where(upper, pltpu.roll(value, width, 1), pltpu.roll(value, lanes - width, 1))
+
+
+def apply_table(table, value):
+    high, low = split_two(value)
+    dot = functools.partial(jnp.dot, preferred_element_type=jnp.float32)
+    return dot(table[0], high) + (dot(table[1], high) + dot(table[0], low))
+
+
+def wave_tables(length, order):
+    half = length // 2
+    point = np.arange(length)
+    wave = np.arange(half)
+    angle = (wave[:, None] * point[None, :] % length) * (2.0 * np.pi / length)
+    sine = np.sin(angle)
+    sine[0] = 1.0 - 2.0 * (point % 2)
+    forward = np.concatenate([np.cos(angle), sine])
+    fold = np.where(np.arange(length) % half == 0, 1.0, 2.0) / length
+    inverse = (forward * fold[:, None]).T
+
+    def parts(table):
+        high = table.astype(np.float32).astype(jnp.bfloat16)
+        low = (table - high.astype(np.float64)).astype(np.float32).astype(jnp.bfloat16)
+        return jnp.asarray(np.stack([high, low]))
+
+    return parts(forward[order]), parts(inverse[:, order])
+
+
+def third_order(grid, rows, cols):
+    local = grid // cols
+    low_count = local // rows
+    order = []
+    for slot in range(local):
+        parity, wave = slot_of(slot // low_count, slot % low_count, rows, low_count)
+        for owner in range(cols):
+            order.append(parity * (grid // 2) + owner * (local // 2) + wave)
+    return np.array(order)
+
+
+def slot_of(high, low, high_count, low_count):
+    if low_count > 1:
+        half = low_count // 2
+        return low // half, high * half + low % half
+    half = high_count // 2
+    return high // half, high % half
+
+
+def bins(coordinate):
+    rows = lax.broadcasted_iota(jnp.int32, (CELL, coordinate.shape[1]), 0).astype(jnp.float32)
+    separation = coordinate - (rows + 0.5)
     return jnp.exp(-separation * separation * bin_rate)
 
 
-def signed_wave(values):
-    return jnp.where(values < GRID // 2, values, values - GRID).astype(jnp.float32)
-
-
-def stokes(spectrum, wave_x, wave_y, wave_z):
-    wave_square = wave_x * wave_x + wave_y * wave_y + wave_z * wave_z
-    damping = 0.25 * jnp.exp(-wave_square * (math.pi / GRID) ** 2)
-    along = (wave_x * spectrum[0] + wave_y * spectrum[1] + wave_z * spectrum[2]) / jnp.maximum(
-        wave_square, 1.0
-    )
-    return jnp.stack(
-        [
-            damping * (spectrum[0] - wave_x * along),
-            damping * (spectrum[1] - wave_y * along),
-            damping * (spectrum[2] - wave_z * along),
-        ]
-    )
-
-
-def dft_tables(length):
-    counter = jnp.arange(length, dtype=jnp.int32)
-    phase = counter[:, None] * counter[None, :] % length
-    angle = phase.astype(jnp.float32) * (2.0 * math.pi / length)
-    return (jnp.cos(angle), jnp.sin(angle))
-
-
-def half_tables(length):
-    counter = jnp.arange(length, dtype=jnp.int32)
-    half_index = jnp.arange(length // 2, dtype=jnp.int32)
-    phase = counter[:, None] * half_index[None, :] % length
-    angle = phase.astype(jnp.float32) * (2.0 * math.pi / length)
-    alternate = 1.0 - 2.0 * (counter % 2).astype(jnp.float32)
-    cos_half = jnp.cos(angle)
-    sin_half = jnp.where(half_index[None, :] == 0, -alternate[:, None], jnp.sin(angle))
-    folding = jnp.where(half_index == 0, 1.0, 2.0).astype(jnp.float32)[:, None]
-    return (cos_half, sin_half, folding * cos_half.T, folding * sin_half.T)
-
-
-def spectral_forward(pieces, form, cosine, sine_tab):
-    real_out = jnp.einsum(form, pieces[0], cosine, precision=highest) + jnp.einsum(
-        form, pieces[1], sine_tab, precision=highest
-    )
-    imag_out = jnp.einsum(form, pieces[1], cosine, precision=highest) - jnp.einsum(
-        form, pieces[0], sine_tab, precision=highest
-    )
-    return jnp.stack([real_out, imag_out])
-
-
-def spectral_inverse(pieces, form, cosine, sine_tab):
-    real_out = jnp.einsum(form, pieces[0], cosine, precision=highest) - jnp.einsum(
-        form, pieces[1], sine_tab, precision=highest
-    )
-    imag_out = jnp.einsum(form, pieces[1], cosine, precision=highest) + jnp.einsum(
-        form, pieces[0], sine_tab, precision=highest
-    )
-    return jnp.stack([real_out, imag_out])
-
-
-def apply_stokes(spectrum, wave_x, wave_y, wave_z):
-    return jnp.stack(
-        [stokes(spectrum[0], wave_x, wave_y, wave_z), stokes(spectrum[1], wave_x, wave_y, wave_z)]
-    )
-
-
-def solve_half(grid_field):
-    cosine, sine_tab = dft_tables(GRID)
-    cos_half, sin_half, cos_back, sin_back = half_tables(GRID)
-    real_part = jnp.einsum("cxyz,zk->ckxy", grid_field, cos_half, precision=highest)
-    imag_part = -jnp.einsum("cxyz,zk->ckxy", grid_field, sin_half, precision=highest)
-    spectrum = jnp.stack([real_part, imag_part])
-    pencil = spectral_forward(
-        lax.all_to_all(spectrum, "col", split_axis=2, concat_axis=4, tiled=True),
-        "ckxy,yl->clkx",
-        cosine,
-        sine_tab,
-    )
-    pencil = spectral_forward(
-        lax.all_to_all(pencil, "row", split_axis=2, concat_axis=4, tiled=True),
-        "clkx,xm->clkm",
-        cosine,
-        sine_tab,
-    )
-    ky_count = pencil.shape[2]
-    kz_count = pencil.shape[3]
+def planar_pair(place, ix, iy, cz):
+    highs, lows, thirds = [], [], []
+    blank = None
+    for which in range(2):
+        rows = [place[d, ix + which, iy, pl.ds(cz, 1), :] for d in range(3)]
+        first, second = bins(rows[0]), bins(rows[1])
+        planar = jnp.concatenate([first[a:a + 1] * second for a in range(CELL)], 0)
+        high, low = split_two(planar)
+        blank = jnp.zeros_like(high)
+        pick = [high, low]
+        for store, value in zip((highs, lows), pick):
+            store.append(jnp.concatenate([value, blank] if which == 0 else [blank, value], 1))
+        thirds.append(bins(rows[2]))
+    return jnp.concatenate(highs, 0), jnp.concatenate(lows, 0), thirds
+
+
+def paired(value):
+    high = value.astype(jnp.bfloat16).astype(jnp.float32)
+    low = value - high
+    return jnp.concatenate([jnp.concatenate([high, high], 1),
+                            jnp.concatenate([low, jnp.zeros_like(low)], 1)], 0).astype(jnp.bfloat16)
+
+
+def spread_kernel(dims, cols, place, load, table, out, cubes):
+    nx, ny, nz, slots = dims
+    for xp in range(nx // 2):
+        for iy in range(ny):
+            def cell(cz, carry, xp=xp, iy=iy):
+                high, low, thirds = planar_pair(place, 2 * xp, iy, cz)
+                lifted = jnp.concatenate(
+                    [jnp.concatenate([load[q, 2 * xp + which, iy, pl.ds(cz, 1), :] * thirds[which]
+                                      for q in range(3)], 0) for which in range(2)], 1)
+                total = lax.dot_general(paired(lifted), jnp.concatenate([high, low], 1), (((1,), (1,)), ((), ())),
+                                        preferred_element_type=jnp.float32)
+                total = total[:3 * CELL] + total[3 * CELL:]
+                for q in range(3):
+                    cubes[q, xp, iy, pl.ds(pl.multiple_of(cz * CELL, CELL), CELL), :] = total[q * CELL:(q + 1) * CELL]
+                return carry
+
+            lax.fori_loop(0, nz, cell, 0, unroll=4)
+    per = 2 * CELL // cols
+    for q in range(3):
+        for xp in range(nx // 2):
+            for iy in range(ny):
+                lines = jnp.transpose(apply_table(table, cubes[q, xp, iy]))
+                for part in range(per):
+                    rows = [lines[(part * cols + j) * CELL:(part * cols + j + 1) * CELL] for j in range(cols)]
+                    for owner, value in enumerate(trade(rows, 1)):
+                        out[owner, q, xp * per + part, iy * CELL:(iy + 1) * CELL, :] = value
+
+
+def gather_kernel(dims, cols, place, load, near, table, lines_in, out, cubes):
+    nx, ny, nz, slots = dims
+    per = 2 * CELL // cols
+    for q in range(3):
+        for xp in range(nx // 2):
+            for iy in range(ny):
+                rows = []
+                for part in range(per):
+                    rows += trade([lines_in[owner, q, xp * per + part, iy * CELL:(iy + 1) * CELL, :]
+                                   for owner in range(cols)], 1)
+                cubes[q, xp, iy] = apply_table(table, jnp.transpose(jnp.concatenate(rows, 0)))
+    for xp in range(nx // 2):
+        for iy in range(ny):
+            def cell(cz, carry, xp=xp, iy=iy):
+                high, low, thirds = planar_pair(place, 2 * xp, iy, cz)
+                cube = jnp.concatenate([cubes[q, xp, iy, pl.ds(pl.multiple_of(cz * CELL, CELL), CELL), :]
+                                        for q in range(3)], 0)
+                total = jnp.dot(paired(cube), jnp.concatenate([high, low], 0), preferred_element_type=jnp.float32)
+                total = total[:3 * CELL] + total[3 * CELL:]
+                for which in range(2):
+                    at = (2 * xp + which, iy, pl.ds(cz, 1))
+                    filled = load[3, *at, :]
+                    for q in range(3):
+                        part = total[q * CELL:(q + 1) * CELL, which * slots:(which + 1) * slots] * thirds[which]
+                        out[q, *at, :] = near[q, *at, :] + filled * jnp.sum(part, axis=0, keepdims=True)
+                return carry
+
+            lax.fori_loop(0, nz, cell, 0, unroll=4)
+
+
+def second_kernel(rows, cols, table, lines_in, out):
+    parts = lines_in.shape[2]
+    grid = lines_in.shape[4]
+    wave = grid // 2 // rows
+    block = grid // rows
+    for q in range(3):
+        lines = jnp.concatenate(
+            [jnp.concatenate([lines_in[owner, q, part] for owner in range(cols)], 0) for part in range(parts)], 1)
+        lines = apply_table(table, lines)
+        for part in range(parts):
+            turned = jnp.transpose(lines[:, part * grid:(part + 1) * grid])
+            pieces = [turned[j * block:(j + 1) * block] for j in range(rows)]
+            for owner, value in enumerate(trade(pieces, wave)):
+                out[owner, q, part] = value
+
+
+def second_back_kernel(rows, cols, table, lines_in, out):
+    parts = lines_in.shape[2]
+    grid = lines_in.shape[4]
+    wave = grid // 2 // rows
+    share = grid // cols
+    for q in range(3):
+        lines = []
+        for part in range(parts):
+            pieces = trade([lines_in[owner, q, part] for owner in range(rows)], wave)
+            lines.append(jnp.transpose(jnp.concatenate(pieces, 0)))
+        lines = apply_table(table, jnp.concatenate(lines, 1))
+        for part in range(parts):
+            for owner in range(cols):
+                out[owner, q, part] = lines[owner * share:(owner + 1) * share, part * grid:(part + 1) * grid]
+
+
+def first_kernel(rows, cols, table, back, lines_in, out):
+    parts = lines_in.shape[2]
+    grid = lines_in.shape[4]
+    half = grid // 2
+    wave_count = half // rows
+    local = grid // cols
+    low_count = local // rows
     row_place = lax.axis_index("row")
     col_place = lax.axis_index("col")
-    wave_ky = signed_wave(row_place * ky_count + jnp.arange(ky_count, dtype=jnp.int32))
-    wave_kz = signed_wave(col_place * kz_count + jnp.arange(kz_count, dtype=jnp.int32))
-    wave_kx = signed_wave(jnp.arange(GRID, dtype=jnp.int32))
-    regular = apply_stokes(
-        pencil, wave_kx[None, None, :], wave_ky[:, None, None], wave_kz[None, :, None]
-    )
-    edge_plane = pencil[:, :, :, 0, :]
-    whole_plane = lax.all_gather(edge_plane, "row", axis=2, tiled=True)
-    mirrored = jnp.roll(jnp.flip(whole_plane, (2, 3)), 1, (2, 3))
-    partner = lax.dynamic_slice_in_dim(mirrored, row_place * ky_count, ky_count, 2)
-    even_part = jnp.stack([(edge_plane[0] + partner[0]) * 0.5, (edge_plane[1] - partner[1]) * 0.5])
-    odd_part = jnp.stack([(edge_plane[1] + partner[1]) * 0.5, (partner[0] - edge_plane[0]) * 0.5])
-    plane_x = wave_kx[None, :]
-    plane_y = wave_ky[:, None]
-    zero_wave = jnp.zeros((1, 1), wave_kx.dtype)
-    nyquist_wave = zero_wave + GRID // 2
-    even_out = apply_stokes(even_part, plane_x, plane_y, zero_wave)
-    odd_out = 0.5 * (
-        apply_stokes(odd_part, plane_x, plane_y, nyquist_wave)
-        + apply_stokes(odd_part, plane_x, plane_y, -nyquist_wave)
-    )
-    packed = jnp.stack([even_out[0] - odd_out[1], even_out[1] + odd_out[0]])
-    first_slot = jnp.where(col_place == 0, packed, regular[:, :, :, 0, :])
-    pencil = jnp.concatenate([first_slot[:, :, :, None], regular[:, :, :, 1:]], 3)
-    pencil = spectral_inverse(pencil, "clkm,mx->clkx", cosine, sine_tab)
-    pencil = spectral_inverse(
-        lax.all_to_all(pencil, "row", split_axis=4, concat_axis=2, tiled=True),
-        "clkx,ly->ckxy",
-        cosine,
-        sine_tab,
-    )
-    pieces = lax.all_to_all(pencil, "col", split_axis=4, concat_axis=2, tiled=True)
-    summed = jnp.einsum("ckxy,kz->cxyz", pieces[0], cos_back, precision=highest) - jnp.einsum(
-        "ckxy,kz->cxyz", pieces[1], sin_back, precision=highest
-    )
-    return summed * (1.0 / GRID) ** 3
-
-
-def solve_far(grid_field):
-    return solve_half(grid_field)
-
-
-def far_field(places, torque, filled):
-    cells_x, cells_y, cells_z, slot_count = (
-        places.shape[1],
-        places.shape[2],
-        places.shape[3],
-        places.shape[4],
-    )
-    cell_count = cells_x * cells_y * cells_z
-    flat_places = places.reshape(3, cell_count, slot_count)
-    weight_x = bin_weights(flat_places[0])
-    weight_y = bin_weights(flat_places[1])
-    weight_z = bin_weights(flat_places[2])
-    planar = weight_x[:, :, :, None] * weight_y[:, :, None, :]
-    lifted = (torque * filled).reshape(3, cell_count, slot_count)[:, :, :, None] * weight_z[None]
-    cubes = jnp.einsum("niab,qnic->qnabc", planar, lifted, precision=highest)
-    grid_field = (
-        cubes.reshape(3, cells_x, cells_y, cells_z, CELL, CELL, CELL)
-        .transpose(0, 1, 4, 2, 5, 3, 6)
-        .reshape(3, cells_x * CELL, cells_y * CELL, cells_z * CELL)
-    )
-    far_grid = solve_far(grid_field)
-    cubes = (
-        far_grid.reshape(3, cells_x, CELL, cells_y, CELL, cells_z, CELL)
-        .transpose(0, 1, 3, 5, 2, 4, 6)
-        .reshape(3, cell_count, CELL, CELL, CELL)
-    )
-    partial_sum = jnp.einsum("qnabc,niab->qnic", cubes, planar, precision=highest)
-    return jnp.sum(partial_sum * weight_z[None], axis=3).reshape(
-        3, cells_x, cells_y, cells_z, slot_count
-    )
+    shape = (grid, grid)
+    row_id = lax.broadcasted_iota(jnp.int32, shape, 0)
+    lane_id = lax.broadcasted_iota(jnp.int32, shape, 1)
+
+    def signed(wave, parity):
+        value = wave.astype(jnp.float32)
+        slope = jnp.where(parity == 0, value, -value)
+        edge = jnp.where((wave == 0) & (parity == 1), jnp.float32(half), jnp.float32(0.0))
+        return slope, edge, value * value + edge * edge
+
+    slope_x, edge_x, square_x = signed(row_id % half, row_id // half)
+    slope_y, edge_y, square_y = signed(row_place * wave_count + lane_id % wave_count, lane_id // half)
+    high_id = lane_id // wave_count % rows
+
+    def third(low):
+        if low_count > 1:
+            middle = low_count // 2
+            parity = jnp.full(shape, low // middle, jnp.int32)
+            wave = high_id * middle + low % middle
+        else:
+            parity = high_id // (rows // 2)
+            wave = high_id % (rows // 2)
+        return signed(col_place * (local // 2) + wave, parity)
+
+    def along_x(value):
+        return slope_x * jnp.concatenate([value[half:], value[:half]], 0)
+
+    def along_y(value):
+        return slope_y * swap_halves(value, half)
+
+    def along_z(values, slopes):
+        if low_count > 1:
+            turned = [values[1], values[0]]
+        else:
+            turned = [swap_halves(values[0], wave_count * rows // 2)]
+        return [slope * value for slope, value in zip(slopes, turned)]
+
+    middle = max(low_count // 2, 1)
+    for low in range(middle):
+        lows = [low, low + middle] if low_count > 1 else [low]
+        lines = []
+        for q in range(3):
+            for at in lows:
+                lines.append(jnp.concatenate(
+                    [lines_in[owner, q, part, at * cols:(at + 1) * cols, :] for owner in range(rows)
+                     for part in range(parts)], 0))
+        lines = apply_table(table, jnp.concatenate(lines, 1))
+        count = len(lows)
+        spectrum = [[lines[:, (q * count + n) * grid:(q * count + n + 1) * grid] for n in range(count)]
+                    for q in range(3)]
+        thirds = [third(at) for at in lows]
+        slopes = [entry[0] for entry in thirds]
+        turned_z = along_z(spectrum[2], slopes)
+        flow, edge, inverse, damping = [], [], [], []
+        for n in range(count):
+            _, edge_z, square_z = thirds[n]
+            wave_square = square_x + square_y + square_z
+            flow.append(along_x(spectrum[0][n]) + along_y(spectrum[1][n]) + turned_z[n])
+            edge.append(edge_x * spectrum[0][n] + edge_y * spectrum[1][n] + edge_z * spectrum[2][n])
+            inverse.append(1.0 / jnp.maximum(wave_square, 1.0))
+            damping.append(0.25 * jnp.exp(-wave_square * (math.pi / grid) ** 2))
+        flow_z = along_z(flow, slopes)
+        results = [[], [], []]
+        for n in range(count):
+            edges = (edge_x, edge_y, thirds[n][1])
+            turns = (along_x(flow[n]), along_y(flow[n]), flow_z[n])
+            for q in range(3):
+                results[q].append(damping[n] * (spectrum[q][n] + (turns[q] - edges[q] * edge[n]) * inverse[n]))
+        lines = apply_table(back, jnp.concatenate([value for entry in results for value in entry], 1))
+        share = grid // rows
+        for q in range(3):
+            for n, at in enumerate(lows):
+                piece = lines[:, (q * count + n) * grid:(q * count + n + 1) * grid]
+                for owner in range(rows):
+                    for part in range(parts):
+                        start = owner * share + part * cols
+                        out[owner, q, part, at * cols:(at + 1) * cols, :] = piece[start:start + cols]
+
+
+def local_call(kernel, name, shape, args, scratch=()):
+    vmem = pl.BlockSpec(memory_space=pltpu.VMEM)
+    return pl.pallas_call(
+        kernel, out_shape=jax.ShapeDtypeStruct(shape, jnp.float32), in_specs=[vmem] * len(args), out_specs=vmem,
+        scratch_shapes=list(scratch), compiler_params=pltpu.CompilerParams(vmem_limit_bytes=VMEM_LIMIT), name=name,
+    )(*args)
+
+
+def far_field(places, loads, spin_near):
+    _, nx, ny, nz, slots = places.shape
+    rows, cols = lax.axis_size("row"), lax.axis_size("col")
+    grid = nz * CELL
+    dims = (nx, ny, nz, slots)
+    natural = np.arange(grid)
+    table, back = wave_tables(grid, natural)
+    third_table, third_back = wave_tables(grid, third_order(grid, rows, cols))
+    parts = nx * CELL // cols
+    col_shape = (cols, 3, parts, ny * CELL, grid)
+    row_shape = (rows, 3, parts, grid // rows, grid)
+    cubes = [pltpu.VMEM((3, nx // 2, ny, grid, 2 * CELL * CELL), jnp.float32)]
+
+    def turn(lines, axis):
+        return lax.all_to_all(lines, axis, split_axis=0, concat_axis=0, tiled=True)
+
+    lines = local_call(functools.partial(spread_kernel, dims, cols), "spread_third", col_shape,
+                       (places, loads, third_table), cubes)
+    lines = local_call(functools.partial(second_kernel, rows, cols), "second", row_shape, (table, turn(lines, "col")))
+    lines = local_call(functools.partial(first_kernel, rows, cols), "first_stokes", row_shape,
+                       (table, back, turn(lines, "row")))
+    lines = local_call(functools.partial(second_back_kernel, rows, cols), "second_back", col_shape,
+                       (back, turn(lines, "row")))
+    return local_call(functools.partial(gather_kernel, dims, cols), "third_gather", places.shape,
+                      (places, loads, spin_near, third_back, turn(lines, "col")), cubes)
 
 
 def shards(positions, torques, counts, neighbour_flags):
@@ -370,8 +514,7 @@
     spin_near = None
     for step_id in range(STEPS):
         places, spin_near = near_step(places, loads, flags, rim(places), load_rim)
-    far_spin = far_field(places, torques, filled)
-    return (places, spin_near + far_spin * filled)
+    return (places, far_field(places, loads, spin_near))
 
 
 def solution(mesh):

time: 588 us -> 273 us (0.46)
  matrix products: 213 us -> 0 us
  local copies, waits for them, and re-layouts: 97.5 us -> 8.2 us
  blocking collectives: 51.4 us -> 80.9 us
  Pallas kernels: 118 us -> 147 us
  other arithmetic: 27.7 us -> 1.7 us
  waiting for transfers between devices: 37.1 us -> 14.3 us
  starting transfers between devices: 35 us -> 19.1 us
    dot_general x22 -> x0, matrix products: 213 us -> none  [the longest x1 169 us: far_field(): cubes = jnp.einsum('niab,qnic->qnabc', planar, lifted, precision=highest)]
    all_to_all x2 -> x4, blocking collectives: 36 us -> 80.9 us  [turn(): return lax.all_to_all(lines, axis, split_axis=0, concat_axis=0, tiled=True)]
    reshape x4 -> x0, local copies, waits for them, and re-layouts: 44.9 us -> none  [the longest x1 14.2 us: far_field(): cubes = far_grid.reshape(3, cells_x, CELL, cells_y, CELL, cells_z, CELL)....]
    all_to_all x2 -> x0, waiting for transfers between devices: 29.9 us -> none  [the longest x1 17.4 us: solve_half(): lax.all_to_all(pencil, 'row', split_axis=2, concat_axis=4, tiled=True)]
    pallas_call x0 -> x5, Pallas kernels: none -> 28.4 us  [local_call(): pl.pallas_call(kernel, out_shape=jax.ShapeDtypeStruct(shape, jnp.float32)...]
    unnamed x88 -> x44, local copies, waits for them, and re-layouts: 22.4 us -> 4.62 us
    all_gather x1 -> x0, blocking collectives: 15.3 us -> none  [solve_half(): whole_plane = lax.all_gather(edge_plane, 'row', axis=2, tiled=True)]
    all_to_all x4 -> x0, other arithmetic: 15 us -> none  [the longest x1 3.81 us: solve_half(): lax.all_to_all(pencil, 'row', split_axis=2, concat_axis=4, tiled=True)]
  transfers between devices with their start and end apart: 18 -> 16, of which waited for: 5 -> 6; matrix products, arithmetic and copies ran while one was open for 1% -> 1% of each run, Pallas kernels for 0% -> 0%
where the time goes in v2:
time: 273 us; the launch traced here: 272 us
  Pallas kernels  147 us (54%)
  blocking collectives  80.9 us (30%)
  starting transfers between devices  19.1 us (7%)
  waiting for transfers between devices  14.3 us (5%)
  local copies, waits for them, and re-layouts  8.2 us (3%)
    pallas_call x3, Pallas kernels, near_step(): pl.pallas_call(functools.partial(near_kernel, (nx, ny, nz, slots)), out_s...  118 us
    all_to_all x4, blocking collectives, turn(): return lax.all_to_all(lines, axis, split_axis=0, concat_axis=0, tiled=True)  80.9 us
    pallas_call x5, Pallas kernels, local_call(): pl.pallas_call(kernel, out_shape=jax.ShapeDtypeStruct(shape, jnp.float32)...  28.4 us
    ppermute x8, starting transfers between devices, rim(): lax.ppermute(lax.slice_in_dim(block, 0, 1, axis=dim), axis, backward)  17.4 us
    ppermute x8, waiting for transfers between devices, rim(): lax.ppermute(lax.slice_in_dim(block, block.shape[dim] - 1, None, axis=dim...  10.4 us
  transfers between devices with their start and end apart: 16, of which 6 were waited for; matrix products, arithmetic and copies ran while one was open for 1% of the time, Pallas kernels for 0%

profile of v2, /device:TPU:0, one launch (start us, length us, event | category | flops | bytes accessed | tf_op | source)
XLA Modules:
  0.0 271.8 jit_solution(1739175990608117896)
XLA Ops:
  0.6 0.9 fusion.11
  1.5 5.1 %collective-permute-start.1 = (f32[3,1,2,16,128]{4,3,2,1,0:T(8,128)S(1)}, f32[3,1,2,16,128]{4,3,2,1,0:T(8,128)S(1)}, u32[]{:S(2)}, u32[]{:S(2)}) collective-permute-start(f32[3,1,2,16,128]{4,3,2,1,0:T(8,128)S(1)} %get-tuple-element.24), channel_id=1, source_target_pairs={{8,0},{16,8},{24,16},{0,24},{9,1},{17,9},{25,17},{1,25},{10,2},{18... | collective-permute-start | bytes 147464 | tf_op jit(solution)/shard_map/ppermute | solution.py:189
  6.6 0.8 fusion.5
  7.5 0.1 fusion.4
  7.6 0.0 copy-start
  7.6 3.8 %collective-permute-start.5 = (f32[4,1,2,16,128]{4,3,2,1,0:T(8,128)S(1)}, f32[4,1,2,16,128]{4,3,2,1,0:T(8,128)S(1)}, u32[]{:S(2)}, u32[]{:S(2)}) collective-permute-start(f32[4,1,2,16,128]{4,3,2,1,0:T(8,128)S(1)} %get-tuple-element.12), channel_id=1, source_target_pairs={{8,0},{16,8},{24,16},{0,24},{9,1},{17,9},{25,17},{1,25},{10,2},{18... | collective-permute-start | bytes 196616 | tf_op jit(solution)/shard_map/ppermute | solution.py:189
  11.4 1.1 collective-permute-start.7
  12.5 0.0 collective-permute-start.6
  12.6 0.7 copy-done.20
  13.3 0.7 reshape.18.flags
  14.0 0.0 collective-permute-done.1.place_xh
  14.0 0.0 collective-permute-start.4
  14.0 2.0 collective-permute-start.3
  16.0 0.7 pad_maximum_fusion.load
  16.7 3.3 %collective-permute-done.4.load_xl = f32[4,1,2,16,128]{4,3,2,1,0:T(8,128)S(1)} collective-permute-done((f32[4,1,2,16,128]{4,3,2,1,0:T(8,128)S(1)}, f32[4,1,2,16,128]{4,3,2,1,0:T(8,128)S(1)}, u32[]{:S(2)}, u32[]{:S(2)}) %collective-permute-start.4) | collective-permute-done | bytes 65568 | tf_op jit(solution)/shard_map/ppermute | solution.py:188
  20.0 0.9 collective-permute-done.2.place_yl
  21.0 0.6 copy-done.13
  21.6 0.1 copy-done.3
  21.6 0.7 copy-done.4
  22.3 39.5 %near_step.3 = (f32[3,4,2,16,128]{4,3,2,1,0:T(8,128)}, f32[3,4,2,16,128]{4,3,2,1,0:T(8,128)}) custom-call(s32[768]{0:T(1024)} %reshape.18.flags, f32[3,4,2,16,128]{4,3,2,1,0:T(8,128)} %place.1, f32[4,4,2,16,128]{4,3,2,1,0:T(8,128)} %pad_maximum_fusion.load, f32[3,1,2,16,128]{4,3,2,1,0:T(8,128)} %copy-done.15, f32[3,1,2,16,128]{4,3,2,1,0:T(8,128)} %copy-done.14, ...), custom_call_target="tpu_custom_call" | custom-call | tf_op jit(solution)/shard_map/near_step/pallas_call | solution.py:170
  61.8 1.0 fusion.8
  62.8 0.9 collective-permute-start.11
  63.7 3.1 %collective-permute-start.9 = (f32[3,1,2,16,128]{4,3,2,1,0:T(8,128)S(1)}, f32[3,1,2,16,128]{4,3,2,1,0:T(8,128)S(1)}, u32[]{:S(2)}, u32[]{:S(2)}) collective-permute-start(f32[3,1,2,16,128]{4,3,2,1,0:T(8,128)S(1)} %get-tuple-element.20), channel_id=1, source_target_pairs={{8,0},{16,8},{24,16},{0,24},{9,1},{17,9},{25,17},{1,25},{10,2},{18... | collective-permute-start | bytes 147464 | tf_op jit(solution)/shard_map/ppermute | solution.py:189
  66.9 1.7 collective-permute-done.9.place_xh
  68.6 4.1 %collective-permute-done.8.place_xl = f32[3,1,2,16,128]{4,3,2,1,0:T(8,128)S(1)} collective-permute-done((f32[3,1,2,16,128]{4,3,2,1,0:T(8,128)S(1)}, f32[3,1,2,16,128]{4,3,2,1,0:T(8,128)S(1)}, u32[]{:S(2)}, u32[]{:S(2)}) %collective-permute-start.8) | collective-permute-done | bytes 49184 | tf_op jit(solution)/shard_map/ppermute | solution.py:188
  72.8 0.6 copy-done.19
  73.4 0.0 copy-done.11
  73.4 0.6 copy-done.12
  74.1 39.5 %near_step.4 = (f32[3,4,2,16,128]{4,3,2,1,0:T(8,128)}, f32[3,4,2,16,128]{4,3,2,1,0:T(8,128)}) custom-call(s32[768]{0:T(1024)} %reshape.18.flags, f32[3,4,2,16,128]{4,3,2,1,0:T(8,128)} %get-tuple-element.6.place, f32[4,4,2,16,128]{4,3,2,1,0:T(8,128)} %pad_maximum_fusion.load, f32[3,1,2,16,128]{4,3,2,1,0:T(8,128)} %copy-done.19, ...), custom_call_target="tpu_custom_call" | custom-call | tf_op jit(solution)/shard_map/near_step/pallas_call | solution.py:170
  113.5 1.0 fusion.6
  114.5 0.9 collective-permute-start.15
  115.5 0.4 collective-permute-start.13
  115.9 1.7 collective-permute-start.12
  117.6 2.1 collective-permute-done.13.place_xh
  119.6 2.1 collective-permute-done.12.place_xl
  121.8 0.6 copy-done.17
  122.4 0.0 copy-done.8
  122.4 0.6 copy-done.9
  123.0 39.5 %near_step.5 = (f32[3,4,2,16,128]{4,3,2,1,0:T(8,128)}, f32[3,4,2,16,128]{4,3,2,1,0:T(8,128)}) custom-call(s32[768]{0:T(1024)} %reshape.18.flags, f32[3,4,2,16,128]{4,3,2,1,0:T(8,128)} %get-tuple-element.7.place, f32[4,4,2,16,128]{4,3,2,1,0:T(8,128)} %pad_maximum_fusion.load, f32[3,1,2,16,128]{4,3,2,1,0:T(8,128)} %copy-done.17, ...), custom_call_target="tpu_custom_call" | custom-call | tf_op jit(solution)/shard_map/near_step/pallas_call | solution.py:170
  162.5 9.4 %spread_third.1 = f32[8,3,4,16,128]{4,3,2,1,0:T(8,128)} custom-call(f32[3,4,2,16,128]{4,3,2,1,0:T(8,128)} %get-tuple-element.4.place, f32[4,4,2,16,128]{4,3,2,1,0:T(8,128)} %pad_maximum_fusion.load, bf16[2,128,128]{2,1,0:T(8,128)(2,1)} %constant.10.clone.table), custom_call_target="tpu_custom_call" | custom-call | tf_op jit(solution)/shard_map/spread_third/pallas_call | solution.py:474
  171.9 16.8 %all_to_all.20.lines_in = f32[8,3,4,16,128]{4,3,2,1,0:T(8,128)} all-to-all(f32[8,3,4,16,128]{4,3,2,1,0:T(8,128)} %spread_third.1), channel_id=1, replica_groups=mesh['row'=4,'col'=8] {'col'}, dimensions={0} | all-to-all | bytes 1572864 | tf_op jit(solution)/shard_map/all_to_all | solution.py:494
  188.6 3.4 %second.1 = f32[4,3,4,32,128]{4,3,2,1,0:T(8,128)} custom-call(bf16[2,128,128]{2,1,0:T(8,128)(2,1)} %constant.8.clone.table, f32[8,3,4,16,128]{4,3,2,1,0:T(8,128)} %all_to_all.20.lines_in), custom_call_target="tpu_custom_call" | custom-call | tf_op jit(solution)/shard_map/second/pallas_call | solution.py:474
  192.1 24.0 %all_to_all.21.lines_in = f32[4,3,4,32,128]{4,3,2,1,0:T(8,128)} all-to-all(f32[4,3,4,32,128]{4,3,2,1,0:T(8,128)} %second.1), channel_id=1, replica_groups=mesh['row'=4,'col'=8] {'row'}, dimensions={0} | all-to-all | bytes 1572864 | tf_op jit(solution)/shard_map/all_to_all | solution.py:494
  216.1 3.4 %first_stokes.1 = f32[4,3,4,32,128]{4,3,2,1,0:T(8,128)} custom-call(bf16[2,128,128]{2,1,0:T(8,128)(2,1)} %constant.8.clone.table, bf16[2,128,128]{2,1,0:T(8,128)(2,1)} %constant.9.clone.back.table, f32[4,3,4,32,128]{4,3,2,1,0:T(8,128)} %all_to_all.21.lines_in), custom_call_target="tpu_custom_call" | custom-call | tf_op jit(solution)/shard_map/first_stokes/pallas_call | solution.py:474
  219.5 23.4 %all_to_all.22.lines_in = f32[4,3,4,32,128]{4,3,2,1,0:T(8,128)} all-to-all(f32[4,3,4,32,128]{4,3,2,1,0:T(8,128)} %first_stokes.1), channel_id=1, replica_groups=mesh['row'=4,'col'=8] {'row'}, dimensions={0} | all-to-all | bytes 1572864 | tf_op jit(solution)/shard_map/all_to_all | solution.py:494
  242.9 3.4 %second_back.1 = f32[8,3,4,16,128]{4,3,2,1,0:T(8,128)} custom-call(bf16[2,128,128]{2,1,0:T(8,128)(2,1)} %constant.9.clone.back.table, f32[4,3,4,32,128]{4,3,2,1,0:T(8,128)} %all_to_all.22.lines_in), custom_call_target="tpu_custom_call" | custom-call | tf_op jit(solution)/shard_map/second_back/pallas_call | solution.py:474
  246.4 16.8 %all_to_all.23.lines_in = f32[8,3,4,16,128]{4,3,2,1,0:T(8,128)} all-to-all(f32[8,3,4,16,128]{4,3,2,1,0:T(8,128)} %second_back.1), channel_id=1, replica_groups=mesh['row'=4,'col'=8] {'col'}, dimensions={0} | all-to-all | bytes 1572864 | tf_op jit(solution)/shard_map/all_to_all | solution.py:494
  263.1 8.7 %third_gather.1 = f32[3,4,2,16,128]{4,3,2,1,0:T(8,128)} custom-call(f32[3,4,2,16,128]{4,3,2,1,0:T(8,128)} %get-tuple-element.4.place, f32[4,4,2,16,128]{4,3,2,1,0:T(8,128)} %pad_maximum_fusion.load, f32[3,4,2,16,128]{4,3,2,1,0:T(8,128)} %get-tuple-element.9.near, bf16[2,128,128]{2,1,0:T(8,128)(2,1)} %constant.11.clone.table, ...), custom_call_target="tpu_custom_call" | custom-call | tf_op jit(solution)/shard_map/third_gather/pallas_call | solution.py:474
  (53 shorter events, 0.2 us)
Async XLA Ops:
  0.6 6.9 %copy-start.7 = (f32[3,4,2,16,128]{4,3,2,1,0:T(8,128)S(1)}, f32[3,4,2,16,128]{4,3,2,1,0:T(8,128)}, u32[]{:S(2)}) copy-start(f32[3,4,2,16,128]{4,3,2,1,0:T(8,128)} %param.9) | copy-start | bytes 589828
  1.5 12.5 %collective-permute-start.1 = (f32[3,1,2,16,128]{4,3,2,1,0:T(8,128)S(1)}, f32[3,1,2,16,128]{4,3,2,1,0:T(8,128)S(1)}, u32[]{:S(2)}, u32[]{:S(2)}) collective-permute-start(f32[3,1,2,16,128]{4,3,2,1,0:T(8,128)S(1)} %get-tuple-element.24), channel_id=1, source_target_pairs={{8,0},{16,8},{24,16},{0,24},{9,1},{17,9},{25,17},{1,25},{10,2},{18... | collective-permute-start | bytes 147464 | tf_op jit(solution)/shard_map/ppermute | solution.py:189
  6.6 0.8 copy-start.21
  6.6 7.4 %collective-permute-start = (f32[3,1,2,16,128]{4,3,2,1,0:T(8,128)S(1)}, f32[3,1,2,16,128]{4,3,2,1,0:T(8,128)S(1)}, u32[]{:S(2)}, u32[]{:S(2)}) collective-permute-start(f32[3,1,2,16,128]{4,3,2,1,0:T(8,128)S(1)} %get-tuple-element.25), channel_id=1, source_target_pairs={{0,8},{8,16},{16,24},{24,0},{1,9},{9,17},{17,25},{25,1},{2,10},{10... | collective-permute-start | bytes 147464 | tf_op jit(solution)/shard_map/ppermute | solution.py:188
  7.6 4.9 %copy-start = (f32[3,4,2,16,128]{4,3,2,1,0:T(8,128)S(1)}, f32[3,4,2,16,128]{4,3,2,1,0:T(8,128)}, u32[]{:S(2)}) copy-start(f32[3,4,2,16,128]{4,3,2,1,0:T(8,128)} %place.1) | copy-start | bytes 589828
  7.6 8.4 %collective-permute-start.5 = (f32[4,1,2,16,128]{4,3,2,1,0:T(8,128)S(1)}, f32[4,1,2,16,128]{4,3,2,1,0:T(8,128)S(1)}, u32[]{:S(2)}, u32[]{:S(2)}) collective-permute-start(f32[4,1,2,16,128]{4,3,2,1,0:T(8,128)S(1)} %get-tuple-element.12), channel_id=1, source_target_pairs={{8,0},{16,8},{24,16},{0,24},{9,1},{17,9},{25,17},{1,25},{10,2},{18... | collective-permute-start | bytes 196616 | tf_op jit(solution)/shard_map/ppermute | solution.py:189
  11.4 9.5 %collective-permute-start.7 = (f32[4,4,1,16,128]{4,3,2,1,0:T(8,128)S(1)}, f32[4,4,1,16,128]{4,3,2,1,0:T(8,128)S(1)}, u32[]{:S(2)}, u32[]{:S(2)}) collective-permute-start(f32[4,4,1,16,128]{4,3,2,1,0:T(8,128)S(1)} %get-tuple-element.10), channel_id=1, source_target_pairs={{1,0},{2,1},{3,2},{4,3},{5,4},{6,5},{7,6},{0,7},{9,8},{10,9},{11,1... | collective-permute-start | bytes 393224 | tf_op jit(solution)/shard_map/ppermute | solution.py:189
  12.5 0.7 copy-start.20
  12.5 8.4 %collective-permute-start.6 = (f32[4,4,1,16,128]{4,3,2,1,0:T(8,128)S(1)}, f32[4,4,1,16,128]{4,3,2,1,0:T(8,128)S(1)}, u32[]{:S(2)}, u32[]{:S(2)}) collective-permute-start(f32[4,4,1,16,128]{4,3,2,1,0:T(8,128)S(1)} %get-tuple-element.11), channel_id=1, source_target_pairs={{0,1},{1,2},{2,3},{3,4},{4,5},{5,6},{6,7},{7,0},{8,9},{9,10},{10,1... | collective-permute-start | bytes 393224 | tf_op jit(solution)/shard_map/ppermute | solution.py:188
  14.0 2.8 %copy-start.14 = (f32[3,1,2,16,128]{4,3,2,1,0:T(8,128)}, f32[3,1,2,16,128]{4,3,2,1,0:T(8,128)S(1)}, u32[]{:S(2)}) copy-start(f32[3,1,2,16,128]{4,3,2,1,0:T(8,128)S(1)} %collective-permute-done.1.place_xh) | copy-start | bytes 147460
  14.0 6.1 %collective-permute-start.4 = (f32[4,1,2,16,128]{4,3,2,1,0:T(8,128)S(1)}, f32[4,1,2,16,128]{4,3,2,1,0:T(8,128)S(1)}, u32[]{:S(2)}, u32[]{:S(2)}) collective-permute-start(f32[4,1,2,16,128]{4,3,2,1,0:T(8,128)S(1)} %get-tuple-element.13), channel_id=1, source_target_pairs={{0,8},{8,16},{16,24},{24,0},{1,9},{9,17},{17,25},{25,1},{2,10},{10... | collective-permute-start | bytes 196616 | tf_op jit(solution)/shard_map/ppermute | solution.py:188
  14.0 2.8 %copy-start.15 = (f32[3,1,2,16,128]{4,3,2,1,0:T(8,128)}, f32[3,1,2,16,128]{4,3,2,1,0:T(8,128)S(1)}, u32[]{:S(2)}) copy-start(f32[3,1,2,16,128]{4,3,2,1,0:T(8,128)S(1)} %collective-permute-done.place_xl) | copy-start | bytes 147460
  14.0 6.0 %collective-permute-start.3 = (f32[3,4,1,16,128]{4,3,2,1,0:T(8,128)S(1)}, f32[3,4,1,16,128]{4,3,2,1,0:T(8,128)S(1)}, u32[]{:S(2)}, u32[]{:S(2)}) collective-permute-start(f32[3,4,1,16,128]{4,3,2,1,0:T(8,128)S(1)} %get-tuple-element.22), channel_id=1, source_target_pairs={{1,0},{2,1},{3,2},{4,3},{5,4},{6,5},{7,6},{0,7},{9,8},{10,9},{11,1... | collective-permute-start | bytes 294920 | tf_op jit(solution)/shard_map/ppermute | solution.py:189
  16.0 0.8 copy-start.5
  16.0 4.9 %collective-permute-start.2 = (f32[3,4,1,16,128]{4,3,2,1,0:T(8,128)S(1)}, f32[3,4,1,16,128]{4,3,2,1,0:T(8,128)S(1)}, u32[]{:S(2)}, u32[]{:S(2)}) collective-permute-start(f32[3,4,1,16,128]{4,3,2,1,0:T(8,128)S(1)} %get-tuple-element.23), channel_id=1, source_target_pairs={{0,1},{1,2},{2,3},{3,4},{4,5},{5,6},{6,7},{7,0},{8,9},{9,10},{10,1... | collective-permute-start | bytes 294920 | tf_op jit(solution)/shard_map/ppermute | solution.py:188
  20.0 0.9 copy-start.6
  20.0 0.9 copy-start.10
  20.9 0.6 copy-start.13
  20.9 0.7 copy-start.3
  21.6 0.7 copy-start.4
  61.8 1.9 copy-start.2
  62.8 10.0 %collective-permute-start.11 = (f32[3,4,1,16,128]{4,3,2,1,0:T(8,128)S(1)}, f32[3,4,1,16,128]{4,3,2,1,0:T(8,128)S(1)}, u32[]{:S(2)}, u32[]{:S(2)}) collective-permute-start(f32[3,4,1,16,128]{4,3,2,1,0:T(8,128)S(1)} %get-tuple-element.18), channel_id=1, source_target_pairs={{1,0},{2,1},{3,2},{4,3},{5,4},{6,5},{7,6},{0,7},{9,8},{10,9},{11,1... | collective-permute-start | bytes 294920 | tf_op jit(solution)/shard_map/ppermute | solution.py:189
  63.7 9.1 %collective-permute-start.10 = (f32[3,4,1,16,128]{4,3,2,1,0:T(8,128)S(1)}, f32[3,4,1,16,128]{4,3,2,1,0:T(8,128)S(1)}, u32[]{:S(2)}, u32[]{:S(2)}) collective-permute-start(f32[3,4,1,16,128]{4,3,2,1,0:T(8,128)S(1)} %get-tuple-element.19), channel_id=1, source_target_pairs={{0,1},{1,2},{2,3},{3,4},{4,5},{5,6},{6,7},{7,0},{8,9},{9,10},{10,1... | collective-permute-start | bytes 294920 | tf_op jit(solution)/shard_map/ppermute | solution.py:188
  63.7 4.9 %collective-permute-start.9 = (f32[3,1,2,16,128]{4,3,2,1,0:T(8,128)S(1)}, f32[3,1,2,16,128]{4,3,2,1,0:T(8,128)S(1)}, u32[]{:S(2)}, u32[]{:S(2)}) collective-permute-start(f32[3,1,2,16,128]{4,3,2,1,0:T(8,128)S(1)} %get-tuple-element.20), channel_id=1, source_target_pairs={{8,0},{16,8},{24,16},{0,24},{9,1},{17,9},{25,17},{1,25},{10,2},{18... | collective-permute-start | bytes 147464 | tf_op jit(solution)/shard_map/ppermute | solution.py:189
  66.9 5.9 %collective-permute-start.8 = (f32[3,1,2,16,128]{4,3,2,1,0:T(8,128)S(1)}, f32[3,1,2,16,128]{4,3,2,1,0:T(8,128)S(1)}, u32[]{:S(2)}, u32[]{:S(2)}) collective-permute-start(f32[3,1,2,16,128]{4,3,2,1,0:T(8,128)S(1)} %get-tuple-element.21), channel_id=1, source_target_pairs={{0,8},{8,16},{16,24},{24,0},{1,9},{9,17},{17,25},{25,1},{2,10},{10... | collective-permute-start | bytes 147464 | tf_op jit(solution)/shard_map/ppermute | solution.py:188
  68.6 4.2 %copy-start.18 = (f32[3,1,2,16,128]{4,3,2,1,0:T(8,128)}, f32[3,1,2,16,128]{4,3,2,1,0:T(8,128)S(1)}, u32[]{:S(2)}) copy-start(f32[3,1,2,16,128]{4,3,2,1,0:T(8,128)S(1)} %collective-permute-done.9.place_xh) | copy-start | bytes 147460
  72.8 0.6 copy-start.19
  72.8 0.7 copy-start.11
  73.4 0.6 copy-start.12
  113.5 1.9 copy-start.1
  114.5 7.2 %collective-permute-start.15 = (f32[3,4,1,16,128]{4,3,2,1,0:T(8,128)S(1)}, f32[3,4,1,16,128]{4,3,2,1,0:T(8,128)S(1)}, u32[]{:S(2)}, u32[]{:S(2)}) collective-permute-start(f32[3,4,1,16,128]{4,3,2,1,0:T(8,128)S(1)} %get-tuple-element.14), channel_id=1, source_target_pairs={{1,0},{2,1},{3,2},{4,3},{5,4},{6,5},{7,6},{0,7},{9,8},{10,9},{11,1... | collective-permute-start | bytes 294920 | tf_op jit(solution)/shard_map/ppermute | solution.py:189
  115.5 6.3 %collective-permute-start.14 = (f32[3,4,1,16,128]{4,3,2,1,0:T(8,128)S(1)}, f32[3,4,1,16,128]{4,3,2,1,0:T(8,128)S(1)}, u32[]{:S(2)}, u32[]{:S(2)}) collective-permute-start(f32[3,4,1,16,128]{4,3,2,1,0:T(8,128)S(1)} %get-tuple-element.15), channel_id=1, source_target_pairs={{0,1},{1,2},{2,3},{3,4},{4,5},{5,6},{6,7},{7,0},{8,9},{9,10},{10,1... | collective-permute-start | bytes 294920 | tf_op jit(solution)/shard_map/ppermute | solution.py:188
  115.5 4.2 %collective-permute-start.13 = (f32[3,1,2,16,128]{4,3,2,1,0:T(8,128)S(1)}, f32[3,1,2,16,128]{4,3,2,1,0:T(8,128)S(1)}, u32[]{:S(2)}, u32[]{:S(2)}) collective-permute-start(f32[3,1,2,16,128]{4,3,2,1,0:T(8,128)S(1)} %get-tuple-element.16), channel_id=1, source_target_pairs={{8,0},{16,8},{24,16},{0,24},{9,1},{17,9},{25,17},{1,25},{10,2},{18... | collective-permute-start | bytes 147464 | tf_op jit(solution)/shard_map/ppermute | solution.py:189
  115.9 5.9 %collective-permute-start.12 = (f32[3,1,2,16,128]{4,3,2,1,0:T(8,128)S(1)}, f32[3,1,2,16,128]{4,3,2,1,0:T(8,128)S(1)}, u32[]{:S(2)}, u32[]{:S(2)}) collective-permute-start(f32[3,1,2,16,128]{4,3,2,1,0:T(8,128)S(1)} %get-tuple-element.17), channel_id=1, source_target_pairs={{0,8},{8,16},{16,24},{24,0},{1,9},{9,17},{17,25},{25,1},{2,10},{10... | collective-permute-start | bytes 147464 | tf_op jit(solution)/shard_map/ppermute | solution.py:188
  119.6 2.1 copy-start.16
  121.7 0.6 copy-start.17
  121.8 0.6 copy-start.8
  122.4 0.6 copy-start.9

commit v3 on v2

--- a/solution.py
+++ b/solution.py
@@ -33,119 +33,192 @@
     return high, (value - high.astype(jnp.float32)).astype(jnp.bfloat16)
 
 
-def near_kernel(dims, flags, place, load, place_xl, place_xh, place_yl, place_yh,
-                load_xl, load_xh, load_yl, load_yh, place_out, spin_out,
-                far_rows, load_rows, near_rows, sums):
+def fill_source(places, loads, base, count, source_rows, load_rows):
+    xyz = [place - 0.5 * CELL for place in places]
+    torque = loads[:3]
+    square = -RATE * (xyz[0] * xyz[0] + xyz[1] * xyz[1] + xyz[2] * xyz[2])
+    zero = jnp.zeros_like(square)
+    moment = [torque[1] * xyz[2] - torque[2] * xyz[1],
+              torque[2] * xyz[0] - torque[0] * xyz[2],
+              torque[0] * xyz[1] - torque[1] * xyz[0]]
+    for row, value in enumerate(xyz + [jnp.ones_like(square), square, zero, zero, zero]):
+        source_rows[pl.ds(base + row, count, stride=8), :] = value
+    for row, value in enumerate(torque + moment + [loads[3], zero]):
+        load_rows[pl.ds(base + row, count, stride=8), :] = value
+
+
+def fill_target(places, base, count, target_rows):
+    xyz = [place - 0.5 * CELL for place in places]
+    square = -RATE * (xyz[0] * xyz[0] + xyz[1] * xyz[1] + xyz[2] * xyz[2])
+    zero = jnp.zeros_like(square)
+    for row, value in enumerate([2.0 * RATE * d for d in xyz] + [square, jnp.ones_like(square), zero, zero, zero]):
+        target_rows[pl.ds(base + row, count, stride=8), :] = value
+
+
+def rows_of(entries, slots):
+    row_id = lax.broadcasted_iota(jnp.int32, (8, slots), 0)
+    value = jnp.zeros((8, slots), jnp.float32)
+    for row, entry in entries:
+        value = jnp.where(row_id == row, jnp.float32(entry), value)
+    return value
+
+
+def source_side(source_rows, starts):
+    blocks = []
+    for start in starts:
+        high, middle, low = split_three(source_rows[pl.ds(start, 8), :])
+        blocks += [high, middle, low, high, middle, high, jnp.zeros((16, high.shape[1]), jnp.float32)]
+    return jnp.transpose(jnp.concatenate(blocks, 0)).astype(jnp.bfloat16)
+
+
+def target_block(target_rows, start, face):
+    value = target_rows[pl.ds(start, 8), :]
+    slots = value.shape[1]
+    if face is not None:
+        axis, sign = face
+        along = target_rows[pl.ds(start + axis, 1), :]
+        value = value + rows_of([(axis, -2.0 * RATE * CELL * sign), (3, -RATE * CELL * CELL)], slots)
+        value = value + rows_of([(3, CELL * sign)], slots) * along
+    high, middle, low = split_three(value)
+    pad = jnp.zeros((16, slots), jnp.float32)
+    return jnp.concatenate([high, high, high, middle, middle, low, pad], 0).astype(jnp.bfloat16)
+
+
+def load_block(load_rows, start, face, gate):
+    value = load_rows[pl.ds(start, 8), :]
+    slots = value.shape[1]
+    if face is not None:
+        axis, sign = face
+        after, before = (axis + 1) % 3, (axis + 2) % 3
+        value = value + rows_of([(3 + after, CELL * sign)], slots) * load_rows[pl.ds(start + before, 1), :]
+        value = value - rows_of([(3 + before, CELL * sign)], slots) * load_rows[pl.ds(start + after, 1), :]
+        value = value * gate
+    high = value.astype(jnp.bfloat16).astype(jnp.float32)
+    block = jnp.concatenate([high, value - high], 0)
+    return jnp.concatenate([block, block], 1).astype(jnp.bfloat16)
+
+
+def act(side, source_starts, target_starts, face_id, flags, cells, target_rows, load_rows, sums):
+    face = FACES[face_id]
+    blocks = [target_block(target_rows, start, face) for start in target_starts]
+    blank = jnp.zeros_like(blocks[0])
+    right = jnp.concatenate([jnp.concatenate([blocks[0], blank], 1), jnp.concatenate([blank, blocks[1]], 1)], 0)
+    high, low = split_two(jnp.exp2(jnp.dot(side, right, preferred_element_type=jnp.float32)))
+    slots = high.shape[0]
+    totals = []
+    for which in range(2):
+        gate = None
+        if face is not None:
+            gate = flags[(face_id - 1) * cells + target_starts[which] // 8].astype(jnp.float32)
+        block = load_block(load_rows, source_starts[which], face, gate)
+        lanes = slice(which * slots, (which + 1) * slots)
+        total = jnp.dot(block, jnp.concatenate([high[:, lanes], low[:, lanes]], 0), preferred_element_type=jnp.float32)
+        totals.append(total[:8] + total[8:])
+    return totals
+
+
+def aligned(start):
+    return start if isinstance(start, int) else pl.multiple_of(start, 8)
+
+
+def local_kernel(dims, flags, place, load, sums, source_rows, load_rows, target_rows, sides):
     nx, ny, nz, slots = dims
     half = nz // 2
-    wide = ny + 2
-
-    def fill(places, loads, column, own):
-        base = column * nz * 8
-        xyz = [places[d] - 0.5 * CELL for d in range(3)]
-        torque = [loads[d] for d in range(3)]
-        square = -RATE * (xyz[0] * xyz[0] + xyz[1] * xyz[1] + xyz[2] * xyz[2])
-        one = jnp.ones_like(square)
-        zero = jnp.zeros_like(square)
-        moment = [torque[1] * xyz[2] - torque[2] * xyz[1],
-                  torque[2] * xyz[0] - torque[0] * xyz[2],
-                  torque[0] * xyz[1] - torque[1] * xyz[0]]
-        for row, value in enumerate(xyz + [one, square, zero, zero, zero]):
-            far_rows[pl.ds(base + row, nz, stride=8), :] = value
-        for row, value in enumerate(torque + moment + [loads[3], zero]):
-            load_rows[pl.ds(base + row, nz, stride=8), :] = value
-        if own is not None:
-            scaled = [2.0 * RATE * value for value in xyz]
-            for row, value in enumerate(scaled + [square, one, zero, zero, zero]):
-                near_rows[pl.ds(own * nz * 8 + row, nz, stride=8), :] = value
-
+    cells = nx * ny * nz
     for ix in range(nx):
         for iy in range(ny):
-            fill([place[d, ix, iy] for d in range(3)], [load[d, ix, iy] for d in range(4)],
-                 (ix + 1) * wide + iy + 1, ix * ny + iy)
+            base = (ix * ny + iy) * nz * 8
+            places = [place[d, ix, iy] for d in range(3)]
+            fill_source(places, [load[d, ix, iy] for d in range(4)], base, nz, source_rows, load_rows)
+            fill_target(places, base, nz, target_rows)
+
+    def starts_of(ix, iy, level):
+        base = (ix * ny + iy) * nz
+        return [aligned((base + (level + which * half + nz) % nz) * 8) for which in range(2)]
+
+    def column(index, carry):
+        iy = index // half
+        level = index % half
+        lines = [starts_of(ix, iy, level) for ix in range(nx)]
+        turned = [source_side(source_rows, starts) for starts in lines]
+        for ix in range(nx):
+            sides[(ix * ny + iy) * half + level] = turned[ix]
+        args = (flags, cells, target_rows, load_rows, sums)
+        for ix in range(nx):
+            total = act(turned[ix], lines[ix], lines[ix], 0, *args)
+            for near, step in ((1, 1), (2, -1)):
+                other = ix + step
+                if 0 <= other < nx:
+                    more = act(turned[other], lines[other], lines[ix], near, *args)
+                    total = [a + b for a, b in zip(total, more)]
+            for near, step in ((5, 1), (6, -1)):
+                shifted = starts_of(ix, iy, level + step)
+                side = source_side(source_rows, shifted)
+                more = act(side, shifted, lines[ix], near, *args)
+                total = [a + b for a, b in zip(total, more)]
+            for which in range(2):
+                sums[pl.ds(lines[ix][which], 8), :] = total[which]
+        return carry
+
+    lax.fori_loop(0, ny * half, column, 0)
+
+    def across(level, carry):
+        args = (flags, cells, target_rows, load_rows, sums)
+        for ix in range(nx):
+            for iy in range(ny):
+                target = starts_of(ix, iy, level)
+                total = None
+                for near, step in ((3, 1), (4, -1)):
+                    other = iy + step
+                    if 0 <= other < ny:
+                        source = starts_of(ix, other, level)
+                        more = act(sides[(ix * ny + other) * half + level], source, target, near, *args)
+                        total = more if total is None else [a + b for a, b in zip(total, more)]
+                for which in range(2):
+                    sums[pl.ds(target[which], 8), :] = sums[pl.ds(target[which], 8), :] + total[which]
+        return carry
+
+    if ny > 1:
+        lax.fori_loop(0, half, across, 0)
+
+
+def rim_kernel(dims, flags, place, load, part, place_xl, place_xh, place_yl, place_yh,
+               load_xl, load_xh, load_yl, load_yh, place_out, spin_out,
+               source_rows, load_rows, target_rows, sums):
+    nx, ny, nz, slots = dims
+    half = nz // 2
+    cells = nx * ny * nz
+    for ix in range(nx):
+        for iy in range(ny):
+            fill_target([place[d, ix, iy] for d in range(3)], (ix * ny + iy) * nz * 8, nz, target_rows)
+    sums[...] = part[...]
+    links = []
     for iy in range(ny):
-        fill([place_xl[d, 0, iy] for d in range(3)], [load_xl[d, 0, iy] for d in range(4)], iy + 1, None)
-        fill([place_xh[d, 0, iy] for d in range(3)], [load_xh[d, 0, iy] for d in range(4)],
-             (nx + 1) * wide + iy + 1, None)
+        links.append((0, iy, 2, place_xl, load_xl, (0, iy)))
+        links.append((nx - 1, iy, 1, place_xh, load_xh, (0, iy)))
     for ix in range(nx):
-        fill([place_yl[d, ix, 0] for d in range(3)], [load_yl[d, ix, 0] for d in range(4)],
-             (ix + 1) * wide, None)
-        fill([place_yh[d, ix, 0] for d in range(3)], [load_yh[d, ix, 0] for d in range(4)],
-             (ix + 1) * wide + ny + 1, None)
-
-    row_id = lax.broadcasted_iota(jnp.int32, (8, slots), 0)
-
-    def rows_of(entries):
-        value = jnp.zeros((8, slots), jnp.float32)
-        for row, entry in entries:
-            value = jnp.where(row_id == row, jnp.float32(entry), value)
-        return value
-
-    pad = jnp.zeros((16, slots), jnp.float32)
-    blank = jnp.zeros((64, slots), jnp.bfloat16)
-
-    def near_block(start):
-        high, middle, low = split_three(near_rows[pl.ds(start, 8), :])
-        return jnp.concatenate([high, high, high, middle, middle, low, pad], 0)
-
-    def far_block(start, face):
-        value = far_rows[pl.ds(start, 8), :]
-        if face is not None:
-            axis, sign = face
-            along = far_rows[pl.ds(start + axis, 1), :]
-            value = value + rows_of([(axis, CELL * sign), (4, -RATE * CELL * CELL)])
-            value = value + rows_of([(4, -2.0 * RATE * CELL * sign)]) * along
-        high, middle, low = split_three(value)
-        return jnp.concatenate([high, middle, low, high, middle, high, pad], 0).astype(jnp.bfloat16)
-
-    def load_block(start, face, gate):
-        value = load_rows[pl.ds(start, 8), :]
-        if face is not None:
-            axis, sign = face
-            after, before = (axis + 1) % 3, (axis + 2) % 3
-            value = value + rows_of([(3 + after, CELL * sign)]) * load_rows[pl.ds(start + before, 1), :]
-            value = value - rows_of([(3 + before, CELL * sign)]) * load_rows[pl.ds(start + after, 1), :]
-            value = value * gate
-        high, low = split_two(value)
-        return jnp.concatenate([high.astype(jnp.float32), low.astype(jnp.float32)], 0).astype(jnp.bfloat16)
-
-    def pair(index, carry):
-        column = index // half
-        level = index % half
-        ix = column // ny
-        iy = column % ny
-        cells = [column * nz + level, column * nz + level + half]
-        blocks = jnp.concatenate([near_block(cell * 8) for cell in cells], 0)
-        near_side = jnp.transpose(blocks).astype(jnp.bfloat16)
-        loads = [[], []]
-        weights = [[], []]
-        for face_id, face in enumerate(FACES):
-            shift = [0, 0, 0]
-            if face is not None:
-                shift[face[0]] = face[1]
-            far_column = (ix + 1 + shift[0]) * wide + iy + 1 + shift[1]
-            starts = [(far_column * nz + (level + which * half + shift[2] + nz) % nz) * 8 for which in range(2)]
-            starts = [pl.multiple_of(start, 8) for start in starts]
-            far_side = [far_block(start, face) for start in starts]
-            right = jnp.concatenate([jnp.concatenate([far_side[0], blank], 1),
-                                     jnp.concatenate([blank, far_side[1]], 1)], 0)
-            exponent = jnp.dot(near_side, right, preferred_element_type=jnp.float32)
-            high, low = split_two(jnp.exp2(exponent))
+        links.append((ix, 0, 4, place_yl, load_yl, (ix, 0)))
+        links.append((ix, ny - 1, 3, place_yh, load_yh, (ix, 0)))
+    for slot, (_, _, _, places, loads, at) in enumerate(links):
+        fill_source([places[d, *at] for d in range(3)], [loads[d, *at] for d in range(4)],
+                    slot * nz * 8, nz, source_rows, load_rows)
+
+    def level_of(level, carry):
+        gained = {}
+        for slot, (ix, iy, face_id, _, _, _) in enumerate(links):
+            source = [aligned((slot * nz + level + which * half) * 8) for which in range(2)]
+            target = [aligned(((ix * ny + iy) * nz + level + which * half) * 8) for which in range(2)]
+            side = source_side(source_rows, source)
+            more = act(side, source, target, face_id, flags, cells, target_rows, load_rows, sums)
+            if (ix, iy) in gained:
+                more = [a + b for a, b in zip(gained[ix, iy][1], more)]
+            gained[ix, iy] = (target, more)
+        for target, more in gained.values():
             for which in range(2):
-                gate = None
-                if face is not None:
-                    gate = flags[(face_id - 1) * nx * ny * nz + cells[which]].astype(jnp.float32)
-                block = load_block(starts[which], face, gate)
-                loads[which] += [block, block]
-                weights[which] += [high[:, which * slots:(which + 1) * slots],
-                                   low[:, which * slots:(which + 1) * slots]]
-        for which in range(2):
-            total = lax.dot_general(jnp.concatenate(loads[which], 1), jnp.concatenate(weights[which], 1),
-                                    (((1,), (1,)), ((), ())), preferred_element_type=jnp.float32)
-            sums[pl.ds(pl.multiple_of(cells[which] * 8, 8), 8), :] = total[:8] + total[8:]
+                sums[pl.ds(target[which], 8), :] = sums[pl.ds(target[which], 8), :] + more[which]
         return carry
 
-    lax.fori_loop(0, nx * ny * half, pair, 0)
+    lax.fori_loop(0, half, level_of, 0)
 
     for ix in range(nx):
         for iy in range(ny):
@@ -162,21 +235,33 @@
                 spin_out[d, ix, iy] = torque + couple_gain / slots * (filled * rows[d] - rows[6] * torque)
 
 
-def near_step(places, loads, flags, place_rim, load_rim):
+def pair_cost(tiles, slots):
+    return pl.CostEstimate(flops=tiles * slots * slots * 256, bytes_accessed=4 * 1024 * 1024,
+                           transcendentals=tiles * slots * slots)
+
+
+def near_step(places, loads, flags, load_rim):
     _, nx, ny, nz, slots = places.shape
     cells = nx * ny * nz
     vmem = pl.BlockSpec(memory_space=pltpu.VMEM)
-    ext = (nx + 2) * (ny + 2) * nz * 8
+    smem = pl.BlockSpec(memory_space=pltpu.SMEM)
+    dims = (nx, ny, nz, slots)
+    faces = nx * ny * 7 - 2 * (nx + ny)
+    rows = pltpu.VMEM((cells * 8, slots), jnp.float32)
+    params = pltpu.CompilerParams(vmem_limit_bytes=VMEM_LIMIT)
+    place_rim = rim(places)
+    part = pl.pallas_call(
+        functools.partial(local_kernel, dims), out_shape=jax.ShapeDtypeStruct((cells * 8, slots), jnp.float32),
+        in_specs=[smem, vmem, vmem], out_specs=vmem,
+        scratch_shapes=[rows, rows, rows, pltpu.VMEM((cells // 2, slots, 128), jnp.bfloat16)],
+        compiler_params=params, cost_estimate=pair_cost(faces * nz, slots), name="near_local",
+    )(flags, places, loads)
+    rim_rows = pltpu.VMEM((2 * (nx + ny) * nz * 8, slots), jnp.float32)
     return pl.pallas_call(
-        functools.partial(near_kernel, (nx, ny, nz, slots)),
-        out_shape=[jax.ShapeDtypeStruct(places.shape, jnp.float32)] * 2,
-        in_specs=[pl.BlockSpec(memory_space=pltpu.SMEM)] + [vmem] * 10,
-        out_specs=[vmem] * 2,
-        scratch_shapes=[pltpu.VMEM((ext, slots), jnp.float32), pltpu.VMEM((ext, slots), jnp.float32),
-                        pltpu.VMEM((cells * 8, slots), jnp.float32), pltpu.VMEM((cells * 8, slots), jnp.float32)],
-        compiler_params=pltpu.CompilerParams(vmem_limit_bytes=VMEM_LIMIT),
-        name="near_step",
-    )(flags, places, loads, *place_rim, *load_rim)
+        functools.partial(rim_kernel, dims), out_shape=[jax.ShapeDtypeStruct(places.shape, jnp.float32)] * 2,
+        in_specs=[smem] + [vmem] * 11, out_specs=[vmem] * 2, scratch_shapes=[rim_rows, rim_rows, rows, rows],
+        compiler_params=params, cost_estimate=pair_cost(2 * (nx + ny) * nz, slots), name="near_rim",
+    )(flags, places, loads, part, *place_rim, *load_rim)
 
 
 def rim(block):
@@ -513,7 +598,7 @@
     flags = neighbour_flags.reshape(-1)
     spin_near = None
     for step_id in range(STEPS):
-        places, spin_near = near_step(places, loads, flags, rim(places), load_rim)
+        places, spin_near = near_step(places, loads, flags, load_rim)
     return (places, far_field(places, loads, spin_near))
 
 

time: 273 us -> 237 us (0.87)
  Pallas kernels: 147 us -> 120 us
  waiting for transfers between devices: 14.3 us -> 0.04 us
  starting transfers between devices: 19.1 us -> 24.5 us
    pallas_call x3 -> x6, Pallas kernels: 118 us -> 91.5 us  [the longest x3 65.4 us: near_step(): pl.pallas_call(functools.partial(local_kernel, dims), out_shape=jax.Shape...]
    ppermute x8, waiting for transfers between devices: 10.4 us -> 0.02 us  [rim(): lax.ppermute(lax.slice_in_dim(block, block.shape[dim] - 1, None, axis=dim...]
    ppermute x8, starting transfers between devices: 17.4 us -> 24.5 us  [rim(): lax.ppermute(lax.slice_in_dim(block, 0, 1, axis=dim), axis, backward)]
    ppermute x8, waiting for transfers between devices: 3.84 us -> 0.02 us  [rim(): lax.ppermute(lax.slice_in_dim(block, 0, 1, axis=dim), axis, backward)]
  transfers between devices with their start and end apart: 16 -> 16, of which waited for: 6 -> 0; matrix products, arithmetic and copies ran while one was open for 1% -> 1% of each run, Pallas kernels for 0% -> 28%
where the time goes in v3:
time: 237 us
  Pallas kernels  120 us (51%)
  blocking collectives  81.3 us (34%)
  starting transfers between devices  24.5 us (10%)
  local copies, waits for them, and re-layouts  8.16 us (3%)
    all_to_all x4, blocking collectives, turn(): return lax.all_to_all(lines, axis, split_axis=0, concat_axis=0, tiled=True)  81.3 us
    pallas_call x3, Pallas kernels, near_step(): pl.pallas_call(functools.partial(local_kernel, dims), out_shape=jax.Shape...  65.4 us
    pallas_call x5, Pallas kernels, local_call(): pl.pallas_call(kernel, out_shape=jax.ShapeDtypeStruct(shape, jnp.float32)...  28.4 us
    pallas_call x3, Pallas kernels, near_step(): pl.pallas_call(functools.partial(rim_kernel, dims), out_shape=[jax.ShapeD...  26.1 us
    ppermute x8, starting transfers between devices, rim(): lax.ppermute(lax.slice_in_dim(block, 0, 1, axis=dim), axis, backward)  24.5 us
    unnamed x44, local copies, waits for them, and re-layouts  4.82 us
  transfers between devices with their start and end apart: 16, of which 0 were waited for; matrix products, arithmetic and copies ran while one was open for 1% of the time, Pallas kernels for 28%

profile of v3, /device:TPU:0, one launch (start us, length us, event | category | flops | bytes accessed | tf_op | source)
XLA Modules:
  0.0 236.6 jit_solution(9161836839403337047)
XLA Ops:
  0.6 0.9 fusion.11
  1.5 5.1 %collective-permute-start.1 = (f32[3,1,2,16,128]{4,3,2,1,0:T(8,128)S(1)}, f32[3,1,2,16,128]{4,3,2,1,0:T(8,128)S(1)}, u32[]{:S(2)}, u32[]{:S(2)}) collective-permute-start(f32[3,1,2,16,128]{4,3,2,1,0:T(8,128)S(1)} %get-tuple-element.24), channel_id=1, source_target_pairs={{8,0},{16,8},{24,16},{0,24},{9,1},{17,9},{25,17},{1,25},{10,2},{18... | collective-permute-start | bytes 147464 | tf_op jit(solution)/shard_map/ppermute | solution.py:274
  6.6 0.8 fusion.5
  7.5 0.1 fusion.4
  7.6 0.0 copy-start
  7.6 3.8 %collective-permute-start.5 = (f32[4,1,2,16,128]{4,3,2,1,0:T(8,128)S(1)}, f32[4,1,2,16,128]{4,3,2,1,0:T(8,128)S(1)}, u32[]{:S(2)}, u32[]{:S(2)}) collective-permute-start(f32[4,1,2,16,128]{4,3,2,1,0:T(8,128)S(1)} %get-tuple-element.12), channel_id=1, source_target_pairs={{8,0},{16,8},{24,16},{0,24},{9,1},{17,9},{25,17},{1,25},{10,2},{18... | collective-permute-start | bytes 196616 | tf_op jit(solution)/shard_map/ppermute | solution.py:274
  11.4 1.1 collective-permute-start.3
  12.5 0.7 pad_maximum_fusion.load
  13.3 0.7 copy-done.4
  14.0 0.7 reshape.18.flags
  14.7 2.6 %collective-permute-start.7 = (f32[4,4,1,16,128]{4,3,2,1,0:T(8,128)S(1)}, f32[4,4,1,16,128]{4,3,2,1,0:T(8,128)S(1)}, u32[]{:S(2)}, u32[]{:S(2)}) collective-permute-start(f32[4,4,1,16,128]{4,3,2,1,0:T(8,128)S(1)} %get-tuple-element.10), channel_id=1, source_target_pairs={{1,0},{2,1},{3,2},{4,3},{5,4},{6,5},{7,6},{0,7},{9,8},{10,9},{11,1... | collective-permute-start | bytes 393224 | tf_op jit(solution)/shard_map/ppermute | solution.py:274
  17.4 21.8 %near_local.3.part = f32[1024,128]{1,0:T(8,128)} custom-call(s32[768]{0:T(1024)} %reshape.18.flags, f32[3,4,2,16,128]{4,3,2,1,0:T(8,128)} %place.3, f32[4,4,2,16,128]{4,3,2,1,0:T(8,128)} %pad_maximum_fusion.load), custom_call_target="tpu_custom_call" | custom-call | flops 2952790016 | bytes 4194304 | tf_op jit(solution)/shard_map/near_local/pallas_call | solution.py:253
  39.3 0.5 copy-done.15
  39.8 0.1 copy-done.8
  39.9 0.1 copy-done.9
  39.9 0.0 copy-done.6
  40.0 0.6 copy-done.7
  40.6 8.7 %near_rim.3 = (f32[3,4,2,16,128]{4,3,2,1,0:T(8,128)}, f32[3,4,2,16,128]{4,3,2,1,0:T(8,128)}) custom-call(s32[768]{0:T(1024)} %reshape.18.flags, f32[3,4,2,16,128]{4,3,2,1,0:T(8,128)} %place.3, f32[4,4,2,16,128]{4,3,2,1,0:T(8,128)} %pad_maximum_fusion.load, f32[1024,128]{1,0:T(8,128)} %near_local.3.part, f32[3,1,2,16,128]{4,3,2,1,0:T(8,128)} %copy-done.17, ...), custom_call_target="tpu_custom_call" | custom-call | flops 805306368 | bytes 4194304 | tf_op jit(solution)/shard_map/near_rim/pallas_call | solution.py:260
  49.3 0.9 fusion.9
  50.2 0.1 copy-done.2
  50.3 3.6 %collective-permute-start.9 = (f32[3,1,2,16,128]{4,3,2,1,0:T(8,128)S(1)}, f32[3,1,2,16,128]{4,3,2,1,0:T(8,128)S(1)}, u32[]{:S(2)}, u32[]{:S(2)}) collective-permute-start(f32[3,1,2,16,128]{4,3,2,1,0:T(8,128)S(1)} %get-tuple-element.20), channel_id=1, source_target_pairs={{8,0},{16,8},{24,16},{0,24},{9,1},{17,9},{25,17},{1,25},{10,2},{18... | collective-permute-start | bytes 147464 | tf_op jit(solution)/shard_map/ppermute | solution.py:274
  53.9 2.3 collective-permute-start.11
  56.2 21.8 %near_local.4.part = f32[1024,128]{1,0:T(8,128)} custom-call(s32[768]{0:T(1024)} %reshape.18.flags, f32[3,4,2,16,128]{4,3,2,1,0:T(8,128)} %get-tuple-element.6.place, f32[4,4,2,16,128]{4,3,2,1,0:T(8,128)} %pad_maximum_fusion.load), custom_call_target="tpu_custom_call" | custom-call | flops 2952790016 | bytes 4194304 | tf_op jit(solution)/shard_map/near_local/pallas_call | solution.py:253
  78.1 0.6 copy-done.20
  78.7 0.0 copy-done.21
  78.7 0.1 copy-done.12
  78.7 0.6 copy-done.13
  79.4 8.7 %near_rim.4 = (f32[3,4,2,16,128]{4,3,2,1,0:T(8,128)}, f32[3,4,2,16,128]{4,3,2,1,0:T(8,128)}) custom-call(s32[768]{0:T(1024)} %reshape.18.flags, f32[3,4,2,16,128]{4,3,2,1,0:T(8,128)} %get-tuple-element.6.place, f32[4,4,2,16,128]{4,3,2,1,0:T(8,128)} %pad_maximum_fusion.load, f32[1024,128]{1,0:T(8,128)} %near_local.4.part, f32[3,1,2,16,128]{4,3,2,1,0:T(8,128)} %copy-done.21, ...), custom_call_target="tpu_custom_call" | custom-call | flops 805306368 | bytes 4194304 | tf_op jit(solution)/shard_map/near_rim/pallas_call | solution.py:260
  88.1 0.9 fusion.7
  89.0 0.1 copy-done.1
  89.1 3.6 %collective-permute-start.13 = (f32[3,1,2,16,128]{4,3,2,1,0:T(8,128)S(1)}, f32[3,1,2,16,128]{4,3,2,1,0:T(8,128)S(1)}, u32[]{:S(2)}, u32[]{:S(2)}) collective-permute-start(f32[3,1,2,16,128]{4,3,2,1,0:T(8,128)S(1)} %get-tuple-element.16), channel_id=1, source_target_pairs={{8,0},{16,8},{24,16},{0,24},{9,1},{17,9},{25,17},{1,25},{10,2},{18... | collective-permute-start | bytes 147464 | tf_op jit(solution)/shard_map/ppermute | solution.py:274
  92.7 2.4 collective-permute-start.15
  95.0 0.0 collective-permute-start.14
  95.0 21.8 %near_local.5.part = f32[1024,128]{1,0:T(8,128)} custom-call(s32[768]{0:T(1024)} %reshape.18.flags, f32[3,4,2,16,128]{4,3,2,1,0:T(8,128)} %get-tuple-element.7.place, f32[4,4,2,16,128]{4,3,2,1,0:T(8,128)} %pad_maximum_fusion.load), custom_call_target="tpu_custom_call" | custom-call | flops 2952790016 | bytes 4194304 | tf_op jit(solution)/shard_map/near_local/pallas_call | solution.py:253
  116.9 0.6 copy-done.18
  117.5 0.0 copy-done.19
  117.5 0.0 copy-done.10
  117.5 0.6 copy-done.11
  118.2 8.7 %near_rim.5 = (f32[3,4,2,16,128]{4,3,2,1,0:T(8,128)}, f32[3,4,2,16,128]{4,3,2,1,0:T(8,128)}) custom-call(s32[768]{0:T(1024)} %reshape.18.flags, f32[3,4,2,16,128]{4,3,2,1,0:T(8,128)} %get-tuple-element.7.place, f32[4,4,2,16,128]{4,3,2,1,0:T(8,128)} %pad_maximum_fusion.load, f32[1024,128]{1,0:T(8,128)} %near_local.5.part, f32[3,1,2,16,128]{4,3,2,1,0:T(8,128)} %copy-done.19, ...), custom_call_target="tpu_custom_call" | custom-call | flops 805306368 | bytes 4194304 | tf_op jit(solution)/shard_map/near_rim/pallas_call | solution.py:260
  126.9 9.4 %spread_third.1 = f32[8,3,4,16,128]{4,3,2,1,0:T(8,128)} custom-call(f32[3,4,2,16,128]{4,3,2,1,0:T(8,128)} %get-tuple-element.4.place, f32[4,4,2,16,128]{4,3,2,1,0:T(8,128)} %pad_maximum_fusion.load, bf16[2,128,128]{2,1,0:T(8,128)(2,1)} %constant.10.clone.table), custom_call_target="tpu_custom_call" | custom-call | tf_op jit(solution)/shard_map/spread_third/pallas_call | solution.py:559
  136.2 16.8 %all_to_all.20.lines_in = f32[8,3,4,16,128]{4,3,2,1,0:T(8,128)} all-to-all(f32[8,3,4,16,128]{4,3,2,1,0:T(8,128)} %spread_third.1), channel_id=1, replica_groups=mesh['row'=4,'col'=8] {'col'}, dimensions={0} | all-to-all | bytes 1572864 | tf_op jit(solution)/shard_map/all_to_all | solution.py:579
  153.0 3.4 %second.1 = f32[4,3,4,32,128]{4,3,2,1,0:T(8,128)} custom-call(bf16[2,128,128]{2,1,0:T(8,128)(2,1)} %constant.8.clone.table, f32[8,3,4,16,128]{4,3,2,1,0:T(8,128)} %all_to_all.20.lines_in), custom_call_target="tpu_custom_call" | custom-call | tf_op jit(solution)/shard_map/second/pallas_call | solution.py:559
  156.4 24.4 %all_to_all.21.lines_in = f32[4,3,4,32,128]{4,3,2,1,0:T(8,128)} all-to-all(f32[4,3,4,32,128]{4,3,2,1,0:T(8,128)} %second.1), channel_id=1, replica_groups=mesh['row'=4,'col'=8] {'row'}, dimensions={0} | all-to-all | bytes 1572864 | tf_op jit(solution)/shard_map/all_to_all | solution.py:579
  180.8 3.4 %first_stokes.1 = f32[4,3,4,32,128]{4,3,2,1,0:T(8,128)} custom-call(bf16[2,128,128]{2,1,0:T(8,128)(2,1)} %constant.8.clone.table, bf16[2,128,128]{2,1,0:T(8,128)(2,1)} %constant.9.clone.back.table, f32[4,3,4,32,128]{4,3,2,1,0:T(8,128)} %all_to_all.21.lines_in), custom_call_target="tpu_custom_call" | custom-call | tf_op jit(solution)/shard_map/first_stokes/pallas_call | solution.py:559
  184.3 23.4 %all_to_all.22.lines_in = f32[4,3,4,32,128]{4,3,2,1,0:T(8,128)} all-to-all(f32[4,3,4,32,128]{4,3,2,1,0:T(8,128)} %first_stokes.1), channel_id=1, replica_groups=mesh['row'=4,'col'=8] {'row'}, dimensions={0} | all-to-all | bytes 1572864 | tf_op jit(solution)/shard_map/all_to_all | solution.py:579
  207.7 3.4 %second_back.1 = f32[8,3,4,16,128]{4,3,2,1,0:T(8,128)} custom-call(bf16[2,128,128]{2,1,0:T(8,128)(2,1)} %constant.9.clone.back.table, f32[4,3,4,32,128]{4,3,2,1,0:T(8,128)} %all_to_all.22.lines_in), custom_call_target="tpu_custom_call" | custom-call | tf_op jit(solution)/shard_map/second_back/pallas_call | solution.py:559
  211.1 16.8 %all_to_all.23.lines_in = f32[8,3,4,16,128]{4,3,2,1,0:T(8,128)} all-to-all(f32[8,3,4,16,128]{4,3,2,1,0:T(8,128)} %second_back.1), channel_id=1, replica_groups=mesh['row'=4,'col'=8] {'col'}, dimensions={0} | all-to-all | bytes 1572864 | tf_op jit(solution)/shard_map/all_to_all | solution.py:579
  227.9 8.7 %third_gather.1 = f32[3,4,2,16,128]{4,3,2,1,0:T(8,128)} custom-call(f32[3,4,2,16,128]{4,3,2,1,0:T(8,128)} %get-tuple-element.4.place, f32[4,4,2,16,128]{4,3,2,1,0:T(8,128)} %pad_maximum_fusion.load, f32[3,4,2,16,128]{4,3,2,1,0:T(8,128)} %get-tuple-element.9.near, bf16[2,128,128]{2,1,0:T(8,128)(2,1)} %constant.11.clone.table, ...), custom_call_target="tpu_custom_call" | custom-call | tf_op jit(solution)/shard_map/third_gather/pallas_call | solution.py:559
  (56 shorter events, 0.2 us)
Async XLA Ops:
  0.6 6.9 %copy-start.3 = (f32[3,4,2,16,128]{4,3,2,1,0:T(8,128)S(1)}, f32[3,4,2,16,128]{4,3,2,1,0:T(8,128)}, u32[]{:S(2)}) copy-start(f32[3,4,2,16,128]{4,3,2,1,0:T(8,128)} %param.9) | copy-start | bytes 589828
  1.5 13.2 %collective-permute-start.1 = (f32[3,1,2,16,128]{4,3,2,1,0:T(8,128)S(1)}, f32[3,1,2,16,128]{4,3,2,1,0:T(8,128)S(1)}, u32[]{:S(2)}, u32[]{:S(2)}) collective-permute-start(f32[3,1,2,16,128]{4,3,2,1,0:T(8,128)S(1)} %get-tuple-element.24), channel_id=1, source_target_pairs={{8,0},{16,8},{24,16},{0,24},{9,1},{17,9},{25,17},{1,25},{10,2},{18... | collective-permute-start | bytes 147464 | tf_op jit(solution)/shard_map/ppermute | solution.py:274
  6.6 0.8 copy-start.5
  6.6 8.1 %collective-permute-start = (f32[3,1,2,16,128]{4,3,2,1,0:T(8,128)S(1)}, f32[3,1,2,16,128]{4,3,2,1,0:T(8,128)S(1)}, u32[]{:S(2)}, u32[]{:S(2)}) collective-permute-start(f32[3,1,2,16,128]{4,3,2,1,0:T(8,128)S(1)} %get-tuple-element.25), channel_id=1, source_target_pairs={{0,8},{8,16},{16,24},{24,0},{1,9},{9,17},{17,25},{25,1},{2,10},{10... | collective-permute-start | bytes 147464 | tf_op jit(solution)/shard_map/ppermute | solution.py:273
  7.6 3.8 %copy-start = (f32[3,4,2,16,128]{4,3,2,1,0:T(8,128)S(1)}, f32[3,4,2,16,128]{4,3,2,1,0:T(8,128)}, u32[]{:S(2)}) copy-start(f32[3,4,2,16,128]{4,3,2,1,0:T(8,128)} %place.3) | copy-start | bytes 589828
  7.6 9.7 %collective-permute-start.5 = (f32[4,1,2,16,128]{4,3,2,1,0:T(8,128)S(1)}, f32[4,1,2,16,128]{4,3,2,1,0:T(8,128)S(1)}, u32[]{:S(2)}, u32[]{:S(2)}) collective-permute-start(f32[4,1,2,16,128]{4,3,2,1,0:T(8,128)S(1)} %get-tuple-element.12), channel_id=1, source_target_pairs={{8,0},{16,8},{24,16},{0,24},{9,1},{17,9},{25,17},{1,25},{10,2},{18... | collective-permute-start | bytes 196616 | tf_op jit(solution)/shard_map/ppermute | solution.py:274
  11.4 27.8 %collective-permute-start.4 = (f32[4,1,2,16,128]{4,3,2,1,0:T(8,128)S(1)}, f32[4,1,2,16,128]{4,3,2,1,0:T(8,128)S(1)}, u32[]{:S(2)}, u32[]{:S(2)}) collective-permute-start(f32[4,1,2,16,128]{4,3,2,1,0:T(8,128)S(1)} %get-tuple-element.13), channel_id=1, source_target_pairs={{0,8},{8,16},{16,24},{24,0},{1,9},{9,17},{17,25},{25,1},{2,10},{10... | collective-permute-start | bytes 196616 | tf_op jit(solution)/shard_map/ppermute | solution.py:273
  11.4 27.8 %collective-permute-start.3 = (f32[3,4,1,16,128]{4,3,2,1,0:T(8,128)S(1)}, f32[3,4,1,16,128]{4,3,2,1,0:T(8,128)S(1)}, u32[]{:S(2)}, u32[]{:S(2)}) collective-permute-start(f32[3,4,1,16,128]{4,3,2,1,0:T(8,128)S(1)} %get-tuple-element.22), channel_id=1, source_target_pairs={{1,0},{2,1},{3,2},{4,3},{5,4},{6,5},{7,6},{0,7},{9,8},{10,9},{11,1... | collective-permute-start | bytes 294920 | tf_op jit(solution)/shard_map/ppermute | solution.py:274
  13.3 0.7 copy-start.4
  14.7 24.5 %copy-start.16 = (f32[3,1,2,16,128]{4,3,2,1,0:T(8,128)}, f32[3,1,2,16,128]{4,3,2,1,0:T(8,128)S(1)}, u32[]{:S(2)}) copy-start(f32[3,1,2,16,128]{4,3,2,1,0:T(8,128)S(1)} %collective-permute-done.1.place_xh) | copy-start | bytes 147460
  14.7 24.5 %collective-permute-start.2 = (f32[3,4,1,16,128]{4,3,2,1,0:T(8,128)S(1)}, f32[3,4,1,16,128]{4,3,2,1,0:T(8,128)S(1)}, u32[]{:S(2)}, u32[]{:S(2)}) collective-permute-start(f32[3,4,1,16,128]{4,3,2,1,0:T(8,128)S(1)} %get-tuple-element.23), channel_id=1, source_target_pairs={{0,1},{1,2},{2,3},{3,4},{4,5},{5,6},{6,7},{7,0},{8,9},{9,10},{10,1... | collective-permute-start | bytes 294920 | tf_op jit(solution)/shard_map/ppermute | solution.py:273
  14.7 24.5 %copy-start.17 = (f32[3,1,2,16,128]{4,3,2,1,0:T(8,128)}, f32[3,1,2,16,128]{4,3,2,1,0:T(8,128)S(1)}, u32[]{:S(2)}) copy-start(f32[3,1,2,16,128]{4,3,2,1,0:T(8,128)S(1)} %collective-permute-done.place_xl) | copy-start | bytes 147460
  14.7 24.5 %collective-permute-start.7 = (f32[4,4,1,16,128]{4,3,2,1,0:T(8,128)S(1)}, f32[4,4,1,16,128]{4,3,2,1,0:T(8,128)S(1)}, u32[]{:S(2)}, u32[]{:S(2)}) collective-permute-start(f32[4,4,1,16,128]{4,3,2,1,0:T(8,128)S(1)} %get-tuple-element.10), channel_id=1, source_target_pairs={{1,0},{2,1},{3,2},{4,3},{5,4},{6,5},{7,6},{0,7},{9,8},{10,9},{11,1... | collective-permute-start | bytes 393224 | tf_op jit(solution)/shard_map/ppermute | solution.py:274
  17.3 21.8 %copy-start.14 = (f32[4,1,2,16,128]{4,3,2,1,0:T(8,128)}, f32[4,1,2,16,128]{4,3,2,1,0:T(8,128)S(1)}, u32[]{:S(2)}) copy-start(f32[4,1,2,16,128]{4,3,2,1,0:T(8,128)S(1)} %collective-permute-done.5.load_xh) | copy-start | bytes 196612
  17.3 21.9 %collective-permute-start.6 = (f32[4,4,1,16,128]{4,3,2,1,0:T(8,128)S(1)}, f32[4,4,1,16,128]{4,3,2,1,0:T(8,128)S(1)}, u32[]{:S(2)}, u32[]{:S(2)}) collective-permute-start(f32[4,4,1,16,128]{4,3,2,1,0:T(8,128)S(1)} %get-tuple-element.11), channel_id=1, source_target_pairs={{0,1},{1,2},{2,3},{3,4},{4,5},{5,6},{6,7},{7,0},{8,9},{9,10},{10,1... | collective-permute-start | bytes 393224 | tf_op jit(solution)/shard_map/ppermute | solution.py:273
  39.2 0.6 copy-start.15
  39.2 0.7 copy-start.8
  39.2 0.7 copy-start.9
  39.3 0.7 copy-start.6
  40.0 0.6 copy-start.7
  49.3 1.0 copy-start.2
  50.3 27.7 %collective-permute-start.9 = (f32[3,1,2,16,128]{4,3,2,1,0:T(8,128)S(1)}, f32[3,1,2,16,128]{4,3,2,1,0:T(8,128)S(1)}, u32[]{:S(2)}, u32[]{:S(2)}) collective-permute-start(f32[3,1,2,16,128]{4,3,2,1,0:T(8,128)S(1)} %get-tuple-element.20), channel_id=1, source_target_pairs={{8,0},{16,8},{24,16},{0,24},{9,1},{17,9},{25,17},{1,25},{10,2},{18... | collective-permute-start | bytes 147464 | tf_op jit(solution)/shard_map/ppermute | solution.py:274
  53.9 24.2 %collective-permute-start.8 = (f32[3,1,2,16,128]{4,3,2,1,0:T(8,128)S(1)}, f32[3,1,2,16,128]{4,3,2,1,0:T(8,128)S(1)}, u32[]{:S(2)}, u32[]{:S(2)}) collective-permute-start(f32[3,1,2,16,128]{4,3,2,1,0:T(8,128)S(1)} %get-tuple-element.21), channel_id=1, source_target_pairs={{0,8},{8,16},{16,24},{24,0},{1,9},{9,17},{17,25},{25,1},{2,10},{10... | collective-permute-start | bytes 147464 | tf_op jit(solution)/shard_map/ppermute | solution.py:273
  53.9 24.2 %collective-permute-start.11 = (f32[3,4,1,16,128]{4,3,2,1,0:T(8,128)S(1)}, f32[3,4,1,16,128]{4,3,2,1,0:T(8,128)S(1)}, u32[]{:S(2)}, u32[]{:S(2)}) collective-permute-start(f32[3,4,1,16,128]{4,3,2,1,0:T(8,128)S(1)} %get-tuple-element.18), channel_id=1, source_target_pairs={{1,0},{2,1},{3,2},{4,3},{5,4},{6,5},{7,6},{0,7},{9,8},{10,9},{11,1... | collective-permute-start | bytes 294920 | tf_op jit(solution)/shard_map/ppermute | solution.py:274
  56.2 21.8 %collective-permute-start.10 = (f32[3,4,1,16,128]{4,3,2,1,0:T(8,128)S(1)}, f32[3,4,1,16,128]{4,3,2,1,0:T(8,128)S(1)}, u32[]{:S(2)}, u32[]{:S(2)}) collective-permute-start(f32[3,4,1,16,128]{4,3,2,1,0:T(8,128)S(1)} %get-tuple-element.19), channel_id=1, source_target_pairs={{0,1},{1,2},{2,3},{3,4},{4,5},{5,6},{6,7},{7,0},{8,9},{9,10},{10,1... | collective-permute-start | bytes 294920 | tf_op jit(solution)/shard_map/ppermute | solution.py:273
  78.0 0.6 copy-start.20
  78.1 0.6 copy-start.21
  78.1 0.7 copy-start.12
  78.7 0.6 copy-start.13
  88.1 1.0 copy-start.1
  89.1 27.8 %collective-permute-start.13 = (f32[3,1,2,16,128]{4,3,2,1,0:T(8,128)S(1)}, f32[3,1,2,16,128]{4,3,2,1,0:T(8,128)S(1)}, u32[]{:S(2)}, u32[]{:S(2)}) collective-permute-start(f32[3,1,2,16,128]{4,3,2,1,0:T(8,128)S(1)} %get-tuple-element.16), channel_id=1, source_target_pairs={{8,0},{16,8},{24,16},{0,24},{9,1},{17,9},{25,17},{1,25},{10,2},{18... | collective-permute-start | bytes 147464 | tf_op jit(solution)/shard_map/ppermute | solution.py:274
  92.7 24.2 %collective-permute-start.12 = (f32[3,1,2,16,128]{4,3,2,1,0:T(8,128)S(1)}, f32[3,1,2,16,128]{4,3,2,1,0:T(8,128)S(1)}, u32[]{:S(2)}, u32[]{:S(2)}) collective-permute-start(f32[3,1,2,16,128]{4,3,2,1,0:T(8,128)S(1)} %get-tuple-element.17), channel_id=1, source_target_pairs={{0,8},{8,16},{16,24},{24,0},{1,9},{9,17},{17,25},{25,1},{2,10},{10... | collective-permute-start | bytes 147464 | tf_op jit(solution)/shard_map/ppermute | solution.py:273
  92.7 24.2 %collective-permute-start.15 = (f32[3,4,1,16,128]{4,3,2,1,0:T(8,128)S(1)}, f32[3,4,1,16,128]{4,3,2,1,0:T(8,128)S(1)}, u32[]{:S(2)}, u32[]{:S(2)}) collective-permute-start(f32[3,4,1,16,128]{4,3,2,1,0:T(8,128)S(1)} %get-tuple-element.14), channel_id=1, source_target_pairs={{1,0},{2,1},{3,2},{4,3},{5,4},{6,5},{7,6},{0,7},{9,8},{10,9},{11,1... | collective-permute-start | bytes 294920 | tf_op jit(solution)/shard_map/ppermute | solution.py:274
  95.0 21.9 %collective-permute-start.14 = (f32[3,4,1,16,128]{4,3,2,1,0:T(8,128)S(1)}, f32[3,4,1,16,128]{4,3,2,1,0:T(8,128)S(1)}, u32[]{:S(2)}, u32[]{:S(2)}) collective-permute-start(f32[3,4,1,16,128]{4,3,2,1,0:T(8,128)S(1)} %get-tuple-element.15), channel_id=1, source_target_pairs={{0,1},{1,2},{2,3},{3,4},{4,5},{5,6},{6,7},{7,0},{8,9},{9,10},{10,1... | collective-permute-start | bytes 294920 | tf_op jit(solution)/shard_map/ppermute | solution.py:273
  116.8 0.6 copy-start.18
  116.9 0.6 copy-start.19
  116.9 0.6 copy-start.10
  117.5 0.6 copy-start.11

commit v4 on v3

--- a/solution.py
+++ b/solution.py
@@ -309,6 +309,12 @@
     return dot(table[0], high) + (dot(table[1], high) + dot(table[0], low))
 
 
+def apply_right(table, value):
+    high, low = split_two(value)
+    dot = functools.partial(jnp.dot, preferred_element_type=jnp.float32)
+    return dot(high, table[0]) + (dot(high, table[1]) + dot(low, table[0]))
+
+
 def wave_tables(length, order):
     half = length // 2
     point = np.arange(length)
@@ -325,7 +331,8 @@
         low = (table - high.astype(np.float64)).astype(np.float32).astype(jnp.bfloat16)
         return jnp.asarray(np.stack([high, low]))
 
-    return parts(forward[order]), parts(inverse[:, order])
+    forward, inverse = forward[order], inverse[:, order]
+    return parts(forward), parts(inverse), parts(forward.T), parts(inverse.T)
 
 
 def third_order(grid, rows, cols):
@@ -337,6 +344,12 @@
         for owner in range(cols):
             order.append(parity * (grid // 2) + owner * (local // 2) + wave)
     return np.array(order)
+
+
+def slab_order(grid, count):
+    waves = grid // 2 // count
+    return np.array([parity * (grid // 2) + owner * waves + wave
+                     for parity in range(2) for wave in range(waves) for owner in range(count)])
 
 
 def slot_of(high, low, high_count, low_count):
@@ -393,28 +406,33 @@
                 return carry
 
             lax.fori_loop(0, nz, cell, 0, unroll=4)
-    per = 2 * CELL // cols
+    span = max(cols // (2 * CELL), 1)
     for q in range(3):
-        for xp in range(nx // 2):
-            for iy in range(ny):
-                lines = jnp.transpose(apply_table(table, cubes[q, xp, iy]))
-                for part in range(per):
+        for iy in range(ny):
+            for first in range(0, nx // 2, span):
+                lines = jnp.concatenate([jnp.transpose(apply_table(table, cubes[q, first + n, iy]))
+                                         for n in range(span)], 0)
+                for part in range(2 * CELL * span // cols):
                     rows = [lines[(part * cols + j) * CELL:(part * cols + j + 1) * CELL] for j in range(cols)]
                     for owner, value in enumerate(trade(rows, 1)):
-                        out[owner, q, xp * per + part, iy * CELL:(iy + 1) * CELL, :] = value
+                        at = first * 2 * CELL // cols + part
+                        out[owner, q, at, iy * CELL:(iy + 1) * CELL, :] = value
 
 
 def gather_kernel(dims, cols, place, load, near, table, lines_in, out, cubes):
     nx, ny, nz, slots = dims
-    per = 2 * CELL // cols
+    span = max(cols // (2 * CELL), 1)
     for q in range(3):
-        for xp in range(nx // 2):
-            for iy in range(ny):
+        for iy in range(ny):
+            for first in range(0, nx // 2, span):
                 rows = []
-                for part in range(per):
-                    rows += trade([lines_in[owner, q, xp * per + part, iy * CELL:(iy + 1) * CELL, :]
-                                   for owner in range(cols)], 1)
-                cubes[q, xp, iy] = apply_table(table, jnp.transpose(jnp.concatenate(rows, 0)))
+                for part in range(2 * CELL * span // cols):
+                    at = first * 2 * CELL // cols + part
+                    rows += trade([lines_in[owner, q, at, iy * CELL:(iy + 1) * CELL, :] for owner in range(cols)], 1)
+                lines = jnp.concatenate(rows, 0)
+                for n in range(span):
+                    block = lines[n * 2 * CELL * CELL:(n + 1) * 2 * CELL * CELL]
+                    cubes[q, first + n, iy] = apply_table(table, jnp.transpose(block))
     for xp in range(nx // 2):
         for iy in range(ny):
             def cell(cz, carry, xp=xp, iy=iy):
@@ -554,6 +572,75 @@
                         out[owner, q, part, at * cols:(at + 1) * cols, :] = piece[start:start + cols]
 
 
+def plane_kernel(rows, cols, table, table_turned, back, back_turned, lines_in, out):
+    count = rows * cols
+    share = lines_in.shape[2]
+    grid = lines_in.shape[3]
+    half = grid // 2
+    waves = half // count
+    slots = 2 * waves
+    width = grid // rows
+    place = lax.axis_index("row") * cols + lax.axis_index("col")
+    shape = (grid, grid)
+    row_id = lax.broadcasted_iota(jnp.int32, shape, 0)
+    lane_id = lax.broadcasted_iota(jnp.int32, shape, 1)
+
+    def signed(wave, parity):
+        value = wave.astype(jnp.float32)
+        slope = jnp.where(parity == 0, value, -value)
+        edge = jnp.where((wave == 0) & (parity == 1), jnp.float32(half), jnp.float32(0.0))
+        return slope, edge, value * value + edge * edge
+
+    slope_x, edge_x, square_x = signed(lane_id % half, lane_id // half)
+    slope_y, edge_y, square_y = signed(row_id % half, row_id // half)
+    zero_id = jnp.zeros(shape, jnp.int32)
+    thirds = [signed(zero_id + (place * waves + slot % waves), zero_id + slot // waves) for slot in range(slots)]
+
+    spectrum = []
+    for q in range(3):
+        planes = [[] for _ in range(slots)]
+        for c in range(cols):
+            pieces = trade([lines_in[r * cols + c, q] for r in range(rows)], width)
+            for slot in range(slots):
+                planes[slot].append(pieces[slot])
+        lines = apply_table(table, jnp.concatenate([jnp.concatenate(plane, 0) for plane in planes], 1))
+        lines = jnp.concatenate([lines[:, slot * grid:(slot + 1) * grid] for slot in range(slots)], 0)
+        lines = apply_right(table_turned, lines)
+        spectrum.append([lines[slot * grid:(slot + 1) * grid] for slot in range(slots)])
+
+    def along_x(value):
+        return slope_x * swap_halves(value, half)
+
+    def along_y(value):
+        return slope_y * jnp.concatenate([value[half:], value[:half]], 0)
+
+    def partner(slot):
+        return (slot + waves) % slots
+
+    flow, edge, inverse, damping = [], [], [], []
+    for slot in range(slots):
+        slope_z, edge_z, square_z = thirds[slot]
+        wave_square = square_x + square_y + square_z
+        flow.append(along_x(spectrum[0][slot]) + along_y(spectrum[1][slot]) + slope_z * spectrum[2][partner(slot)])
+        edge.append(edge_x * spectrum[0][slot] + edge_y * spectrum[1][slot] + edge_z * spectrum[2][slot])
+        inverse.append(1.0 / jnp.maximum(wave_square, 1.0))
+        damping.append(0.25 * jnp.exp(-wave_square * (math.pi / grid) ** 2))
+    for q in range(3):
+        results = []
+        for slot in range(slots):
+            edges = (edge_x, edge_y, thirds[slot][1])[q]
+            turned = (along_x(flow[slot]) if q == 0 else along_y(flow[slot]) if q == 1
+                      else thirds[slot][0] * flow[partner(slot)])
+            results.append(damping[slot] * (spectrum[q][slot] + (turned - edges * edge[slot]) * inverse[slot]))
+        lines = apply_right(back_turned, jnp.concatenate(results, 0))
+        lines = jnp.concatenate([lines[slot * grid:(slot + 1) * grid] for slot in range(slots)], 1)
+        lines = apply_table(back, lines)
+        for c in range(cols):
+            pieces = [lines[c * share:(c + 1) * share, slot * grid:(slot + 1) * grid] for slot in range(slots)]
+            for r, value in enumerate(trade(pieces, width)):
+                out[r * cols + c, q] = value
+
+
 def local_call(kernel, name, shape, args, scratch=()):
     vmem = pl.BlockSpec(memory_space=pltpu.VMEM)
     return pl.pallas_call(
@@ -568,8 +655,11 @@
     grid = nz * CELL
     dims = (nx, ny, nz, slots)
     natural = np.arange(grid)
-    table, back = wave_tables(grid, natural)
-    third_table, third_back = wave_tables(grid, third_order(grid, rows, cols))
+    table, back, table_turned, back_turned = wave_tables(grid, natural)
+    count = rows * cols
+    slab = grid // 2 % count == 0 and nx * CELL == count and 2 * (grid // 2 // count) == rows
+    order = slab_order(grid, count) if slab else third_order(grid, rows, cols)
+    third_table, third_back = wave_tables(grid, order)[:2]
     parts = nx * CELL // cols
     col_shape = (cols, 3, parts, ny * CELL, grid)
     row_shape = (rows, 3, parts, grid // rows, grid)
@@ -578,6 +668,16 @@
     def turn(lines, axis):
         return lax.all_to_all(lines, axis, split_axis=0, concat_axis=0, tiled=True)
 
+    if slab:
+        both = ("row", "col")
+        shape = (count, 3, 1, ny * CELL, grid)
+        plane = (count, 3, ny * CELL, grid)
+        lines = local_call(functools.partial(spread_kernel, dims, count), "spread_third", shape,
+                           (places, loads, third_table), cubes)
+        lines = local_call(functools.partial(plane_kernel, rows, cols), "planes_stokes", plane,
+                           (table, table_turned, back, back_turned, turn(lines.reshape(plane), both)))
+        return local_call(functools.partial(gather_kernel, dims, count), "third_gather", places.shape,
+                          (places, loads, spin_near, third_back, turn(lines, both).reshape(shape)), cubes)
     lines = local_call(functools.partial(spread_kernel, dims, cols), "spread_third", col_shape,
                        (places, loads, third_table), cubes)
     lines = local_call(functools.partial(second_kernel, rows, cols), "second", row_shape, (table, turn(lines, "col")))

time: 237 us -> 201 us (0.85)
  blocking collectives: 81.3 us -> 51.1 us
  Pallas kernels: 120 us -> 114 us
    all_to_all x4 -> x2, blocking collectives: 81.3 us -> 51.1 us  [turn(): return lax.all_to_all(lines, axis, split_axis=0, concat_axis=0, tiled=True)]
    pallas_call x5 -> x3, Pallas kernels: 28.4 us -> 22.2 us  [local_call(): pl.pallas_call(kernel, out_shape=jax.ShapeDtypeStruct(shape, jnp.float32)...]
  transfers between devices with their start and end apart: 16 -> 16, of which waited for: 0 -> 0; matrix products, arithmetic and copies ran while one was open for 1% -> 1% of each run, Pallas kernels for 28% -> 33%
where the time goes in v4:
time: 201 us; the launch traced here: 200 us
  Pallas kernels  114 us (57%)
  blocking collectives  51.1 us (25%)
  starting transfers between devices  24.5 us (12%)
  local copies, waits for them, and re-layouts  8.16 us (4%)
    pallas_call x3, Pallas kernels, near_step(): pl.pallas_call(functools.partial(local_kernel, dims), out_shape=jax.Shape...  65.4 us
    all_to_all x2, blocking collectives, turn(): return lax.all_to_all(lines, axis, split_axis=0, concat_axis=0, tiled=True)  51.1 us
    pallas_call x3, Pallas kernels, near_step(): pl.pallas_call(functools.partial(rim_kernel, dims), out_shape=[jax.ShapeD...  26.1 us
    ppermute x8, starting transfers between devices, rim(): lax.ppermute(lax.slice_in_dim(block, 0, 1, axis=dim), axis, backward)  24.5 us
    pallas_call x3, Pallas kernels, local_call(): pl.pallas_call(kernel, out_shape=jax.ShapeDtypeStruct(shape, jnp.float32)...  22.2 us
    unnamed x44, local copies, waits for them, and re-layouts  4.82 us
  transfers between devices with their start and end apart: 16, of which 0 were waited for; matrix products, arithmetic and copies ran while one was open for 1% of the time, Pallas kernels for 33%

profile of v4, /device:TPU:0, one launch (start us, length us, event | category | flops | bytes accessed | tf_op | source)
XLA Modules:
  0.0 200.1 jit_solution(15530105528450561883)
XLA Ops:
  0.6 0.9 fusion.11
  1.5 5.1 %collective-permute-start.1 = (f32[3,1,2,16,128]{4,3,2,1,0:T(8,128)S(1)}, f32[3,1,2,16,128]{4,3,2,1,0:T(8,128)S(1)}, u32[]{:S(2)}, u32[]{:S(2)}) collective-permute-start(f32[3,1,2,16,128]{4,3,2,1,0:T(8,128)S(1)} %get-tuple-element.24), channel_id=1, source_target_pairs={{8,0},{16,8},{24,16},{0,24},{9,1},{17,9},{25,17},{1,25},{10,2},{18... | collective-permute-start | bytes 147464 | tf_op jit(solution)/shard_map/ppermute | solution.py:274
  6.6 0.0 collective-permute-start
  6.6 0.8 fusion.5
  7.5 0.1 fusion.4
  7.6 0.0 copy-start
  7.6 3.8 %collective-permute-start.5 = (f32[4,1,2,16,128]{4,3,2,1,0:T(8,128)S(1)}, f32[4,1,2,16,128]{4,3,2,1,0:T(8,128)S(1)}, u32[]{:S(2)}, u32[]{:S(2)}) collective-permute-start(f32[4,1,2,16,128]{4,3,2,1,0:T(8,128)S(1)} %get-tuple-element.12), channel_id=1, source_target_pairs={{8,0},{16,8},{24,16},{0,24},{9,1},{17,9},{25,17},{1,25},{10,2},{18... | collective-permute-start | bytes 196616 | tf_op jit(solution)/shard_map/ppermute | solution.py:274
  11.4 0.0 collective-permute-start.4
  11.4 1.1 collective-permute-start.3
  12.5 0.7 pad_maximum_fusion.load
  13.3 0.7 copy-done.4
  14.0 0.7 reshape.24.flags
  14.7 0.0 collective-permute-start.2
  14.7 0.0 collective-permute-done.place_xl
  14.7 2.6 %collective-permute-start.7 = (f32[4,4,1,16,128]{4,3,2,1,0:T(8,128)S(1)}, f32[4,4,1,16,128]{4,3,2,1,0:T(8,128)S(1)}, u32[]{:S(2)}, u32[]{:S(2)}) collective-permute-start(f32[4,4,1,16,128]{4,3,2,1,0:T(8,128)S(1)} %get-tuple-element.10), channel_id=1, source_target_pairs={{1,0},{2,1},{3,2},{4,3},{5,4},{6,5},{7,6},{0,7},{9,8},{10,9},{11,1... | collective-permute-start | bytes 393224 | tf_op jit(solution)/shard_map/ppermute | solution.py:274
  17.4 21.8 %near_local.3.part = f32[1024,128]{1,0:T(8,128)} custom-call(s32[768]{0:T(1024)} %reshape.24.flags, f32[3,4,2,16,128]{4,3,2,1,0:T(8,128)} %place.3, f32[4,4,2,16,128]{4,3,2,1,0:T(8,128)} %pad_maximum_fusion.load), custom_call_target="tpu_custom_call" | custom-call | flops 2952790016 | bytes 4194304 | tf_op jit(solution)/shard_map/near_local/pallas_call | solution.py:253
  39.3 0.5 copy-done.15
  39.8 0.1 copy-done.8
  39.9 0.1 copy-done.9
  39.9 0.0 copy-done.6
  40.0 0.6 copy-done.7
  40.6 8.7 %near_rim.3 = (f32[3,4,2,16,128]{4,3,2,1,0:T(8,128)}, f32[3,4,2,16,128]{4,3,2,1,0:T(8,128)}) custom-call(s32[768]{0:T(1024)} %reshape.24.flags, f32[3,4,2,16,128]{4,3,2,1,0:T(8,128)} %place.3, f32[4,4,2,16,128]{4,3,2,1,0:T(8,128)} %pad_maximum_fusion.load, f32[1024,128]{1,0:T(8,128)} %near_local.3.part, f32[3,1,2,16,128]{4,3,2,1,0:T(8,128)} %copy-done.17, ...), custom_call_target="tpu_custom_call" | custom-call | flops 805306368 | bytes 4194304 | tf_op jit(solution)/shard_map/near_rim/pallas_call | solution.py:260
  49.3 0.9 fusion.9
  50.2 0.1 copy-done.2
  50.3 3.6 %collective-permute-start.9 = (f32[3,1,2,16,128]{4,3,2,1,0:T(8,128)S(1)}, f32[3,1,2,16,128]{4,3,2,1,0:T(8,128)S(1)}, u32[]{:S(2)}, u32[]{:S(2)}) collective-permute-start(f32[3,1,2,16,128]{4,3,2,1,0:T(8,128)S(1)} %get-tuple-element.20), channel_id=1, source_target_pairs={{8,0},{16,8},{24,16},{0,24},{9,1},{17,9},{25,17},{1,25},{10,2},{18... | collective-permute-start | bytes 147464 | tf_op jit(solution)/shard_map/ppermute | solution.py:274
  53.9 2.3 %collective-permute-start.11 = (f32[3,4,1,16,128]{4,3,2,1,0:T(8,128)S(1)}, f32[3,4,1,16,128]{4,3,2,1,0:T(8,128)S(1)}, u32[]{:S(2)}, u32[]{:S(2)}) collective-permute-start(f32[3,4,1,16,128]{4,3,2,1,0:T(8,128)S(1)} %get-tuple-element.18), channel_id=1, source_target_pairs={{1,0},{2,1},{3,2},{4,3},{5,4},{6,5},{7,6},{0,7},{9,8},{10,9},{11,1... | collective-permute-start | bytes 294920 | tf_op jit(solution)/shard_map/ppermute | solution.py:274
  56.2 21.8 %near_local.4.part = f32[1024,128]{1,0:T(8,128)} custom-call(s32[768]{0:T(1024)} %reshape.24.flags, f32[3,4,2,16,128]{4,3,2,1,0:T(8,128)} %get-tuple-element.6.place, f32[4,4,2,16,128]{4,3,2,1,0:T(8,128)} %pad_maximum_fusion.load), custom_call_target="tpu_custom_call" | custom-call | flops 2952790016 | bytes 4194304 | tf_op jit(solution)/shard_map/near_local/pallas_call | solution.py:253
  78.1 0.6 copy-done.20
  78.7 0.0 copy-done.21
  78.7 0.1 copy-done.12
  78.7 0.6 copy-done.13
  79.4 8.7 %near_rim.4 = (f32[3,4,2,16,128]{4,3,2,1,0:T(8,128)}, f32[3,4,2,16,128]{4,3,2,1,0:T(8,128)}) custom-call(s32[768]{0:T(1024)} %reshape.24.flags, f32[3,4,2,16,128]{4,3,2,1,0:T(8,128)} %get-tuple-element.6.place, f32[4,4,2,16,128]{4,3,2,1,0:T(8,128)} %pad_maximum_fusion.load, f32[1024,128]{1,0:T(8,128)} %near_local.4.part, f32[3,1,2,16,128]{4,3,2,1,0:T(8,128)} %copy-done.21, ...), custom_call_target="tpu_custom_call" | custom-call | flops 805306368 | bytes 4194304 | tf_op jit(solution)/shard_map/near_rim/pallas_call | solution.py:260
  88.1 0.9 fusion.7
  89.0 0.1 copy-done.1
  89.1 3.6 %collective-permute-start.13 = (f32[3,1,2,16,128]{4,3,2,1,0:T(8,128)S(1)}, f32[3,1,2,16,128]{4,3,2,1,0:T(8,128)S(1)}, u32[]{:S(2)}, u32[]{:S(2)}) collective-permute-start(f32[3,1,2,16,128]{4,3,2,1,0:T(8,128)S(1)} %get-tuple-element.16), channel_id=1, source_target_pairs={{8,0},{16,8},{24,16},{0,24},{9,1},{17,9},{25,17},{1,25},{10,2},{18... | collective-permute-start | bytes 147464 | tf_op jit(solution)/shard_map/ppermute | solution.py:274
  92.7 2.4 %collective-permute-start.15 = (f32[3,4,1,16,128]{4,3,2,1,0:T(8,128)S(1)}, f32[3,4,1,16,128]{4,3,2,1,0:T(8,128)S(1)}, u32[]{:S(2)}, u32[]{:S(2)}) collective-permute-start(f32[3,4,1,16,128]{4,3,2,1,0:T(8,128)S(1)} %get-tuple-element.14), channel_id=1, source_target_pairs={{1,0},{2,1},{3,2},{4,3},{5,4},{6,5},{7,6},{0,7},{9,8},{10,9},{11,1... | collective-permute-start | bytes 294920 | tf_op jit(solution)/shard_map/ppermute | solution.py:274
  95.0 0.0 collective-permute-start.14
  95.0 21.8 %near_local.5.part = f32[1024,128]{1,0:T(8,128)} custom-call(s32[768]{0:T(1024)} %reshape.24.flags, f32[3,4,2,16,128]{4,3,2,1,0:T(8,128)} %get-tuple-element.7.place, f32[4,4,2,16,128]{4,3,2,1,0:T(8,128)} %pad_maximum_fusion.load), custom_call_target="tpu_custom_call" | custom-call | flops 2952790016 | bytes 4194304 | tf_op jit(solution)/shard_map/near_local/pallas_call | solution.py:253
  116.9 0.6 copy-done.18
  117.5 0.0 copy-done.19
  117.5 0.0 copy-done.10
  117.5 0.6 copy-done.11
  118.2 8.7 %near_rim.5 = (f32[3,4,2,16,128]{4,3,2,1,0:T(8,128)}, f32[3,4,2,16,128]{4,3,2,1,0:T(8,128)}) custom-call(s32[768]{0:T(1024)} %reshape.24.flags, f32[3,4,2,16,128]{4,3,2,1,0:T(8,128)} %get-tuple-element.7.place, f32[4,4,2,16,128]{4,3,2,1,0:T(8,128)} %pad_maximum_fusion.load, f32[1024,128]{1,0:T(8,128)} %near_local.5.part, f32[3,1,2,16,128]{4,3,2,1,0:T(8,128)} %copy-done.19, ...), custom_call_target="tpu_custom_call" | custom-call | flops 805306368 | bytes 4194304 | tf_op jit(solution)/shard_map/near_rim/pallas_call | solution.py:260
  126.9 9.2 %spread_third.1 = f32[32,3,1,16,128]{4,3,2,1,0:T(8,128)} custom-call(f32[3,4,2,16,128]{4,3,2,1,0:T(8,128)} %get-tuple-element.4.place, f32[4,4,2,16,128]{4,3,2,1,0:T(8,128)} %pad_maximum_fusion.load, bf16[2,128,128]{2,1,0:T(8,128)(2,1)} %constant.16.clone.table), custom_call_target="tpu_custom_call" | custom-call | tf_op jit(solution)/shard_map/spread_third/pallas_call | solution.py:646
  136.0 26.7 %all_to_all.10.lines_in = f32[32,3,16,128]{3,2,1,0:T(8,128)} all-to-all(f32[32,3,16,128]{3,2,1,0:T(8,128)} %bitcast.2), channel_id=1, replica_groups=mesh['row'=4,'col'=8] {'row','col'}, dimensions={0} | all-to-all | bytes 1572864 | tf_op jit(solution)/shard_map/all_to_all | solution.py:669
  162.8 5.0 %planes_stokes.1 = f32[32,3,16,128]{3,2,1,0:T(8,128)} custom-call(bf16[2,128,128]{2,1,0:T(8,128)(2,1)} %constant.12.clone.table, bf16[2,128,128]{2,1,0:T(8,128)(2,1)} %constant.14.clone.table_turned, bf16[2,128,128]{2,1,0:T(8,128)(2,1)} %constant.13.clone.back, bf16[2,128,128]{2,1,0:T(8,128)(2,1)} %constant.15.clone.back_turned, ...), custom_call_target="tpu_custom_call" | custom-call | tf_op jit(solution)/shard_map/planes_stokes/pallas_call | solution.py:646
  167.8 24.4 %all_to_all.11 = f32[32,3,16,128]{3,2,1,0:T(8,128)} all-to-all(f32[32,3,16,128]{3,2,1,0:T(8,128)} %planes_stokes.1), channel_id=1, replica_groups=mesh['row'=4,'col'=8] {'row','col'}, dimensions={0} | all-to-all | bytes 1572864 | tf_op jit(solution)/shard_map/all_to_all | solution.py:669
  192.1 8.0 %third_gather.1 = f32[3,4,2,16,128]{4,3,2,1,0:T(8,128)} custom-call(f32[3,4,2,16,128]{4,3,2,1,0:T(8,128)} %get-tuple-element.4.place, f32[4,4,2,16,128]{4,3,2,1,0:T(8,128)} %pad_maximum_fusion.load, f32[3,4,2,16,128]{4,3,2,1,0:T(8,128)} %get-tuple-element.9.near, bf16[2,128,128]{2,1,0:T(8,128)(2,1)} %constant.17.clone.table, f32[32,3,1,16,128]{4,3,2,1,0:T(8,128)} %bitcast.3), custom_call_target="tpu_custom_call" | custom-call | tf_op jit(solution)/shard_map/third_gather/pallas_call | solution.py:646
  (52 shorter events, 0.2 us)
Async XLA Ops:
  0.6 6.9 %copy-start.3 = (f32[3,4,2,16,128]{4,3,2,1,0:T(8,128)S(1)}, f32[3,4,2,16,128]{4,3,2,1,0:T(8,128)}, u32[]{:S(2)}) copy-start(f32[3,4,2,16,128]{4,3,2,1,0:T(8,128)} %param.11) | copy-start | bytes 589828
  1.5 13.2 %collective-permute-start.1 = (f32[3,1,2,16,128]{4,3,2,1,0:T(8,128)S(1)}, f32[3,1,2,16,128]{4,3,2,1,0:T(8,128)S(1)}, u32[]{:S(2)}, u32[]{:S(2)}) collective-permute-start(f32[3,1,2,16,128]{4,3,2,1,0:T(8,128)S(1)} %get-tuple-element.24), channel_id=1, source_target_pairs={{8,0},{16,8},{24,16},{0,24},{9,1},{17,9},{25,17},{1,25},{10,2},{18... | collective-permute-start | bytes 147464 | tf_op jit(solution)/shard_map/ppermute | solution.py:274
  6.6 0.8 copy-start.5
  6.6 8.1 %collective-permute-start = (f32[3,1,2,16,128]{4,3,2,1,0:T(8,128)S(1)}, f32[3,1,2,16,128]{4,3,2,1,0:T(8,128)S(1)}, u32[]{:S(2)}, u32[]{:S(2)}) collective-permute-start(f32[3,1,2,16,128]{4,3,2,1,0:T(8,128)S(1)} %get-tuple-element.25), channel_id=1, source_target_pairs={{0,8},{8,16},{16,24},{24,0},{1,9},{9,17},{17,25},{25,1},{2,10},{10... | collective-permute-start | bytes 147464 | tf_op jit(solution)/shard_map/ppermute | solution.py:273
  7.6 3.8 %copy-start = (f32[3,4,2,16,128]{4,3,2,1,0:T(8,128)S(1)}, f32[3,4,2,16,128]{4,3,2,1,0:T(8,128)}, u32[]{:S(2)}) copy-start(f32[3,4,2,16,128]{4,3,2,1,0:T(8,128)} %place.3) | copy-start | bytes 589828
  7.6 9.7 %collective-permute-start.5 = (f32[4,1,2,16,128]{4,3,2,1,0:T(8,128)S(1)}, f32[4,1,2,16,128]{4,3,2,1,0:T(8,128)S(1)}, u32[]{:S(2)}, u32[]{:S(2)}) collective-permute-start(f32[4,1,2,16,128]{4,3,2,1,0:T(8,128)S(1)} %get-tuple-element.12), channel_id=1, source_target_pairs={{8,0},{16,8},{24,16},{0,24},{9,1},{17,9},{25,17},{1,25},{10,2},{18... | collective-permute-start | bytes 196616 | tf_op jit(solution)/shard_map/ppermute | solution.py:274
  11.4 27.8 %collective-permute-start.4 = (f32[4,1,2,16,128]{4,3,2,1,0:T(8,128)S(1)}, f32[4,1,2,16,128]{4,3,2,1,0:T(8,128)S(1)}, u32[]{:S(2)}, u32[]{:S(2)}) collective-permute-start(f32[4,1,2,16,128]{4,3,2,1,0:T(8,128)S(1)} %get-tuple-element.13), channel_id=1, source_target_pairs={{0,8},{8,16},{16,24},{24,0},{1,9},{9,17},{17,25},{25,1},{2,10},{10... | collective-permute-start | bytes 196616 | tf_op jit(solution)/shard_map/ppermute | solution.py:273
  11.4 27.8 %collective-permute-start.3 = (f32[3,4,1,16,128]{4,3,2,1,0:T(8,128)S(1)}, f32[3,4,1,16,128]{4,3,2,1,0:T(8,128)S(1)}, u32[]{:S(2)}, u32[]{:S(2)}) collective-permute-start(f32[3,4,1,16,128]{4,3,2,1,0:T(8,128)S(1)} %get-tuple-element.22), channel_id=1, source_target_pairs={{1,0},{2,1},{3,2},{4,3},{5,4},{6,5},{7,6},{0,7},{9,8},{10,9},{11,1... | collective-permute-start | bytes 294920 | tf_op jit(solution)/shard_map/ppermute | solution.py:274
  13.3 0.7 copy-start.4
  14.7 24.5 %copy-start.16 = (f32[3,1,2,16,128]{4,3,2,1,0:T(8,128)}, f32[3,1,2,16,128]{4,3,2,1,0:T(8,128)S(1)}, u32[]{:S(2)}) copy-start(f32[3,1,2,16,128]{4,3,2,1,0:T(8,128)S(1)} %collective-permute-done.1.place_xh) | copy-start | bytes 147460
  14.7 24.5 %collective-permute-start.2 = (f32[3,4,1,16,128]{4,3,2,1,0:T(8,128)S(1)}, f32[3,4,1,16,128]{4,3,2,1,0:T(8,128)S(1)}, u32[]{:S(2)}, u32[]{:S(2)}) collective-permute-start(f32[3,4,1,16,128]{4,3,2,1,0:T(8,128)S(1)} %get-tuple-element.23), channel_id=1, source_target_pairs={{0,1},{1,2},{2,3},{3,4},{4,5},{5,6},{6,7},{7,0},{8,9},{9,10},{10,1... | collective-permute-start | bytes 294920 | tf_op jit(solution)/shard_map/ppermute | solution.py:273
  14.7 24.5 %copy-start.17 = (f32[3,1,2,16,128]{4,3,2,1,0:T(8,128)}, f32[3,1,2,16,128]{4,3,2,1,0:T(8,128)S(1)}, u32[]{:S(2)}) copy-start(f32[3,1,2,16,128]{4,3,2,1,0:T(8,128)S(1)} %collective-permute-done.place_xl) | copy-start | bytes 147460
  14.7 24.5 %collective-permute-start.7 = (f32[4,4,1,16,128]{4,3,2,1,0:T(8,128)S(1)}, f32[4,4,1,16,128]{4,3,2,1,0:T(8,128)S(1)}, u32[]{:S(2)}, u32[]{:S(2)}) collective-permute-start(f32[4,4,1,16,128]{4,3,2,1,0:T(8,128)S(1)} %get-tuple-element.10), channel_id=1, source_target_pairs={{1,0},{2,1},{3,2},{4,3},{5,4},{6,5},{7,6},{0,7},{9,8},{10,9},{11,1... | collective-permute-start | bytes 393224 | tf_op jit(solution)/shard_map/ppermute | solution.py:274
  17.3 21.8 %copy-start.14 = (f32[4,1,2,16,128]{4,3,2,1,0:T(8,128)}, f32[4,1,2,16,128]{4,3,2,1,0:T(8,128)S(1)}, u32[]{:S(2)}) copy-start(f32[4,1,2,16,128]{4,3,2,1,0:T(8,128)S(1)} %collective-permute-done.5.load_xh) | copy-start | bytes 196612
  17.3 21.9 %collective-permute-start.6 = (f32[4,4,1,16,128]{4,3,2,1,0:T(8,128)S(1)}, f32[4,4,1,16,128]{4,3,2,1,0:T(8,128)S(1)}, u32[]{:S(2)}, u32[]{:S(2)}) collective-permute-start(f32[4,4,1,16,128]{4,3,2,1,0:T(8,128)S(1)} %get-tuple-element.11), channel_id=1, source_target_pairs={{0,1},{1,2},{2,3},{3,4},{4,5},{5,6},{6,7},{7,0},{8,9},{9,10},{10,1... | collective-permute-start | bytes 393224 | tf_op jit(solution)/shard_map/ppermute | solution.py:273
  39.2 0.6 copy-start.15
  39.2 0.7 copy-start.8
  39.2 0.7 copy-start.9
  39.3 0.7 copy-start.6
  40.0 0.6 copy-start.7
  49.3 1.0 copy-start.2
  50.3 27.7 %collective-permute-start.9 = (f32[3,1,2,16,128]{4,3,2,1,0:T(8,128)S(1)}, f32[3,1,2,16,128]{4,3,2,1,0:T(8,128)S(1)}, u32[]{:S(2)}, u32[]{:S(2)}) collective-permute-start(f32[3,1,2,16,128]{4,3,2,1,0:T(8,128)S(1)} %get-tuple-element.20), channel_id=1, source_target_pairs={{8,0},{16,8},{24,16},{0,24},{9,1},{17,9},{25,17},{1,25},{10,2},{18... | collective-permute-start | bytes 147464 | tf_op jit(solution)/shard_map/ppermute | solution.py:274
  53.9 24.2 %collective-permute-start.8 = (f32[3,1,2,16,128]{4,3,2,1,0:T(8,128)S(1)}, f32[3,1,2,16,128]{4,3,2,1,0:T(8,128)S(1)}, u32[]{:S(2)}, u32[]{:S(2)}) collective-permute-start(f32[3,1,2,16,128]{4,3,2,1,0:T(8,128)S(1)} %get-tuple-element.21), channel_id=1, source_target_pairs={{0,8},{8,16},{16,24},{24,0},{1,9},{9,17},{17,25},{25,1},{2,10},{10... | collective-permute-start | bytes 147464 | tf_op jit(solution)/shard_map/ppermute | solution.py:273
  53.9 24.2 %collective-permute-start.11 = (f32[3,4,1,16,128]{4,3,2,1,0:T(8,128)S(1)}, f32[3,4,1,16,128]{4,3,2,1,0:T(8,128)S(1)}, u32[]{:S(2)}, u32[]{:S(2)}) collective-permute-start(f32[3,4,1,16,128]{4,3,2,1,0:T(8,128)S(1)} %get-tuple-element.18), channel_id=1, source_target_pairs={{1,0},{2,1},{3,2},{4,3},{5,4},{6,5},{7,6},{0,7},{9,8},{10,9},{11,1... | collective-permute-start | bytes 294920 | tf_op jit(solution)/shard_map/ppermute | solution.py:274
  56.2 21.8 %collective-permute-start.10 = (f32[3,4,1,16,128]{4,3,2,1,0:T(8,128)S(1)}, f32[3,4,1,16,128]{4,3,2,1,0:T(8,128)S(1)}, u32[]{:S(2)}, u32[]{:S(2)}) collective-permute-start(f32[3,4,1,16,128]{4,3,2,1,0:T(8,128)S(1)} %get-tuple-element.19), channel_id=1, source_target_pairs={{0,1},{1,2},{2,3},{3,4},{4,5},{5,6},{6,7},{7,0},{8,9},{9,10},{10,1... | collective-permute-start | bytes 294920 | tf_op jit(solution)/shard_map/ppermute | solution.py:273
  78.0 0.6 copy-start.20
  78.1 0.6 copy-start.21
  78.1 0.7 copy-start.12
  78.7 0.6 copy-start.13
  88.1 1.0 copy-start.1
  89.1 27.8 %collective-permute-start.13 = (f32[3,1,2,16,128]{4,3,2,1,0:T(8,128)S(1)}, f32[3,1,2,16,128]{4,3,2,1,0:T(8,128)S(1)}, u32[]{:S(2)}, u32[]{:S(2)}) collective-permute-start(f32[3,1,2,16,128]{4,3,2,1,0:T(8,128)S(1)} %get-tuple-element.16), channel_id=1, source_target_pairs={{8,0},{16,8},{24,16},{0,24},{9,1},{17,9},{25,17},{1,25},{10,2},{18... | collective-permute-start | bytes 147464 | tf_op jit(solution)/shard_map/ppermute | solution.py:274
  92.7 24.2 %collective-permute-start.12 = (f32[3,1,2,16,128]{4,3,2,1,0:T(8,128)S(1)}, f32[3,1,2,16,128]{4,3,2,1,0:T(8,128)S(1)}, u32[]{:S(2)}, u32[]{:S(2)}) collective-permute-start(f32[3,1,2,16,128]{4,3,2,1,0:T(8,128)S(1)} %get-tuple-element.17), channel_id=1, source_target_pairs={{0,8},{8,16},{16,24},{24,0},{1,9},{9,17},{17,25},{25,1},{2,10},{10... | collective-permute-start | bytes 147464 | tf_op jit(solution)/shard_map/ppermute | solution.py:273
  92.7 24.2 %collective-permute-start.15 = (f32[3,4,1,16,128]{4,3,2,1,0:T(8,128)S(1)}, f32[3,4,1,16,128]{4,3,2,1,0:T(8,128)S(1)}, u32[]{:S(2)}, u32[]{:S(2)}) collective-permute-start(f32[3,4,1,16,128]{4,3,2,1,0:T(8,128)S(1)} %get-tuple-element.14), channel_id=1, source_target_pairs={{1,0},{2,1},{3,2},{4,3},{5,4},{6,5},{7,6},{0,7},{9,8},{10,9},{11,1... | collective-permute-start | bytes 294920 | tf_op jit(solution)/shard_map/ppermute | solution.py:274
  95.0 21.9 %collective-permute-start.14 = (f32[3,4,1,16,128]{4,3,2,1,0:T(8,128)S(1)}, f32[3,4,1,16,128]{4,3,2,1,0:T(8,128)S(1)}, u32[]{:S(2)}, u32[]{:S(2)}) collective-permute-start(f32[3,4,1,16,128]{4,3,2,1,0:T(8,128)S(1)} %get-tuple-element.15), channel_id=1, source_target_pairs={{0,1},{1,2},{2,3},{3,4},{4,5},{5,6},{6,7},{7,0},{8,9},{9,10},{10,1... | collective-permute-start | bytes 294920 | tf_op jit(solution)/shard_map/ppermute | solution.py:273
  116.8 0.6 copy-start.18
  116.9 0.6 copy-start.19
  116.9 0.6 copy-start.10
  117.5 0.6 copy-start.11

commit v5 on v4

--- a/solution.py
+++ b/solution.py
@@ -33,26 +33,31 @@
     return high, (value - high.astype(jnp.float32)).astype(jnp.bfloat16)
 
 
+def fill_rows(rows, base, count, values):
+    for row, value in enumerate(values):
+        rows[pl.ds(base + row, count, stride=8), :] = value
+
+
+def centred(places):
+    xyz = [place - 0.5 * CELL for place in places]
+    return xyz, -RATE * (xyz[0] * xyz[0] + xyz[1] * xyz[1] + xyz[2] * xyz[2])
+
+
 def fill_source(places, loads, base, count, source_rows, load_rows):
-    xyz = [place - 0.5 * CELL for place in places]
+    xyz, square = centred(places)
+    scaled = [2.0 * RATE * value for value in xyz]
     torque = loads[:3]
-    square = -RATE * (xyz[0] * xyz[0] + xyz[1] * xyz[1] + xyz[2] * xyz[2])
-    zero = jnp.zeros_like(square)
     moment = [torque[1] * xyz[2] - torque[2] * xyz[1],
               torque[2] * xyz[0] - torque[0] * xyz[2],
               torque[0] * xyz[1] - torque[1] * xyz[0]]
-    for row, value in enumerate(xyz + [jnp.ones_like(square), square, zero, zero, zero]):
-        source_rows[pl.ds(base + row, count, stride=8), :] = value
-    for row, value in enumerate(torque + moment + [loads[3], zero]):
-        load_rows[pl.ds(base + row, count, stride=8), :] = value
+    fill_rows(source_rows, base, count, scaled + [jnp.ones_like(square), square] + scaled)
+    fill_rows(load_rows, base, count, torque + moment + [loads[3], jnp.zeros_like(square)])
 
 
 def fill_target(places, base, count, target_rows):
-    xyz = [place - 0.5 * CELL for place in places]
-    square = -RATE * (xyz[0] * xyz[0] + xyz[1] * xyz[1] + xyz[2] * xyz[2])
+    xyz, square = centred(places)
     zero = jnp.zeros_like(square)
-    for row, value in enumerate([2.0 * RATE * d for d in xyz] + [square, jnp.ones_like(square), zero, zero, zero]):
-        target_rows[pl.ds(base + row, count, stride=8), :] = value
+    fill_rows(target_rows, base, count, xyz + [square, jnp.ones_like(square), zero, zero, zero])
 
 
 def rows_of(entries, slots):
@@ -66,126 +71,137 @@
 def source_side(source_rows, starts):
     blocks = []
     for start in starts:
-        high, middle, low = split_three(source_rows[pl.ds(start, 8), :])
-        blocks += [high, middle, low, high, middle, high, jnp.zeros((16, high.shape[1]), jnp.float32)]
+        value = source_rows[pl.ds(start, 8), :]
+        slots = value.shape[1]
+        high, middle, low = split_three(value)
+        row_id = lax.broadcasted_iota(jnp.int32, (8, slots), 0)
+        one = rows_of([(5, 1.0)], slots)
+        blocks += [high, middle, low] + [jnp.where(row_id < 5, part, one) for part in (high, middle, high)]
+    blocks.append(jnp.zeros((slots - 8 * len(blocks), slots), jnp.float32))
     return jnp.transpose(jnp.concatenate(blocks, 0)).astype(jnp.bfloat16)
 
 
-def target_block(target_rows, start, face):
-    value = target_rows[pl.ds(start, 8), :]
-    slots = value.shape[1]
-    if face is not None:
+def load_block(load_rows, start):
+    value = load_rows[pl.ds(start, 8), :]
+    high = value.astype(jnp.bfloat16).astype(jnp.float32)
+    return jnp.concatenate([high, value - high], 0).astype(jnp.bfloat16)
+
+
+def target_parts(target_rows, start):
+    return split_three(target_rows[pl.ds(start, 8), :])
+
+
+def target_block(target_rows, start, parts, face):
+    high, middle, low = parts
+    slots = high.shape[1]
+    if face is None:
+        groups = [high, high, high, middle, middle, low]
+    else:
         axis, sign = face
         along = target_rows[pl.ds(start + axis, 1), :]
-        value = value + rows_of([(axis, -2.0 * RATE * CELL * sign), (3, -RATE * CELL * CELL)], slots)
-        value = value + rows_of([(3, CELL * sign)], slots) * along
-    high, middle, low = split_three(value)
-    pad = jnp.zeros((16, slots), jnp.float32)
-    return jnp.concatenate([high, high, high, middle, middle, low, pad], 0).astype(jnp.bfloat16)
-
-
-def load_block(load_rows, start, face, gate):
-    value = load_rows[pl.ds(start, 8), :]
-    slots = value.shape[1]
-    if face is not None:
-        axis, sign = face
-        after, before = (axis + 1) % 3, (axis + 2) % 3
-        value = value + rows_of([(3 + after, CELL * sign)], slots) * load_rows[pl.ds(start + before, 1), :]
-        value = value - rows_of([(3 + before, CELL * sign)], slots) * load_rows[pl.ds(start + after, 1), :]
-        value = value * gate
-    high = value.astype(jnp.bfloat16).astype(jnp.float32)
-    block = jnp.concatenate([high, value - high], 0)
-    return jnp.concatenate([block, block], 1).astype(jnp.bfloat16)
-
-
-def act(side, source_starts, target_starts, face_id, flags, cells, target_rows, load_rows, sums):
+        own = rows_of([(5, 2.0 * RATE * CELL * sign)], slots) * along + rows_of([(5, -RATE * CELL * CELL)], slots)
+        own = split_three(own)
+        moved = high + rows_of([(5 + axis, -CELL * sign)], slots)
+        groups = [moved, moved, moved, middle + own[0], middle + own[1], low + own[2]]
+    return jnp.concatenate(groups, 0).astype(jnp.bfloat16)
+
+
+def act(side, loads, starts, parts, face_id, flags, cells, target_rows):
     face = FACES[face_id]
-    blocks = [target_block(target_rows, start, face) for start in target_starts]
+    blocks = [target_block(target_rows, start, part, face) for start, part in zip(starts, parts)]
     blank = jnp.zeros_like(blocks[0])
-    right = jnp.concatenate([jnp.concatenate([blocks[0], blank], 1), jnp.concatenate([blank, blocks[1]], 1)], 0)
+    slots = blank.shape[1]
+    rest = jnp.zeros((slots - 2 * blank.shape[0], 2 * slots), jnp.bfloat16)
+    right = jnp.concatenate([jnp.concatenate([blocks[0], blank], 1), jnp.concatenate([blank, blocks[1]], 1), rest], 0)
     high, low = split_two(jnp.exp2(jnp.dot(side, right, preferred_element_type=jnp.float32)))
-    slots = high.shape[0]
     totals = []
     for which in range(2):
-        gate = None
+        lanes = slice(which * slots, (which + 1) * slots)
+        total = jnp.dot(jnp.concatenate([loads[which], loads[which]], 1),
+                        jnp.concatenate([high[:, lanes], low[:, lanes]], 0), preferred_element_type=jnp.float32)
+        total = total[:8] + total[8:]
         if face is not None:
-            gate = flags[(face_id - 1) * cells + target_starts[which] // 8].astype(jnp.float32)
-        block = load_block(load_rows, source_starts[which], face, gate)
-        lanes = slice(which * slots, (which + 1) * slots)
-        total = jnp.dot(block, jnp.concatenate([high[:, lanes], low[:, lanes]], 0), preferred_element_type=jnp.float32)
-        totals.append(total[:8] + total[8:])
+            total = total * flags[(face_id - 1) * cells + starts[which] // 8].astype(jnp.float32)
+        totals.append(total)
     return totals
+
+
+class Gain:
+    def __init__(self):
+        self.total, self.along = None, {}
+
+    def add(self, totals, face):
+        self.total = totals if self.total is None else [a + b for a, b in zip(self.total, totals)]
+        if face is not None:
+            axis, sign = face
+            signed = totals if sign > 0 else [-value for value in totals]
+            held = self.along.get(axis)
+            self.along[axis] = signed if held is None else [a + b for a, b in zip(held, signed)]
+
+    def folded(self, which):
+        value = self.total[which]
+        slots = value.shape[1]
+        for axis, pair in self.along.items():
+            after, before = (axis + 1) % 3, (axis + 2) % 3
+            value = value + rows_of([(3 + after, CELL)], slots) * pltpu.roll(pair[which], (3 + after - before) % 8, 0)
+            value = value - rows_of([(3 + before, CELL)], slots) * pltpu.roll(pair[which], (3 + before - after) % 8, 0)
+        return value
 
 
 def aligned(start):
     return start if isinstance(start, int) else pl.multiple_of(start, 8)
 
 
-def local_kernel(dims, flags, place, load, sums, source_rows, load_rows, target_rows, sides):
+def local_kernel(dims, flags, place, load, sums, source_rows, load_rows, target_rows, sides, blocks):
     nx, ny, nz, slots = dims
     half = nz // 2
     cells = nx * ny * nz
-    for ix in range(nx):
-        for iy in range(ny):
-            base = (ix * ny + iy) * nz * 8
-            places = [place[d, ix, iy] for d in range(3)]
-            fill_source(places, [load[d, ix, iy] for d in range(4)], base, nz, source_rows, load_rows)
-            fill_target(places, base, nz, target_rows)
-
-    def starts_of(ix, iy, level):
-        base = (ix * ny + iy) * nz
-        return [aligned((base + (level + which * half + nz) % nz) * 8) for which in range(2)]
-
-    def column(index, carry):
-        iy = index // half
-        level = index % half
-        lines = [starts_of(ix, iy, level) for ix in range(nx)]
-        turned = [source_side(source_rows, starts) for starts in lines]
-        for ix in range(nx):
-            sides[(ix * ny + iy) * half + level] = turned[ix]
-        args = (flags, cells, target_rows, load_rows, sums)
-        for ix in range(nx):
-            total = act(turned[ix], lines[ix], lines[ix], 0, *args)
-            for near, step in ((1, 1), (2, -1)):
-                other = ix + step
-                if 0 <= other < nx:
-                    more = act(turned[other], lines[other], lines[ix], near, *args)
-                    total = [a + b for a, b in zip(total, more)]
-            for near, step in ((5, 1), (6, -1)):
-                shifted = starts_of(ix, iy, level + step)
-                side = source_side(source_rows, shifted)
-                more = act(side, shifted, lines[ix], near, *args)
-                total = [a + b for a, b in zip(total, more)]
+    columns = [(ix, iy) for ix in range(nx) for iy in range(ny)]
+    for column, (ix, iy) in enumerate(columns):
+        places = [place[d, ix, iy] for d in range(3)]
+        fill_source(places, [load[3 + d, ix, iy] for d in range(4)], column * nz * 8, nz, source_rows, load_rows)
+        fill_target(places, column * nz * 8, nz, target_rows)
+
+    def cells_of(column, level):
+        return [column * nz + (level + which * half + nz) % nz for which in range(2)]
+
+    def turn_level(index, carry):
+        for column in range(len(columns)):
+            members = cells_of(column, index - 1)
+            sides[column * (half + 2) + index] = source_side(source_rows, [aligned(cell * 8) for cell in members])
+            for cell in members:
+                blocks[cell] = load_block(load_rows, aligned(cell * 8))
+        return carry
+
+    lax.fori_loop(0, half + 2, turn_level, 0)
+
+    def level_of(level, carry):
+        for column, (ix, iy) in enumerate(columns):
+            members = cells_of(column, level)
+            starts = [aligned(cell * 8) for cell in members]
+            parts = [target_parts(target_rows, start) for start in starts]
+            gain = Gain()
+            for face_id, face in enumerate(FACES):
+                at = [ix, iy, 0]
+                if face is not None:
+                    at[face[0]] += face[1]
+                if not (0 <= at[0] < nx and 0 <= at[1] < ny):
+                    continue
+                other = at[0] * ny + at[1]
+                loads = [blocks[cell] for cell in cells_of(other, level + at[2])]
+                side = sides[other * (half + 2) + level + 1 + at[2]]
+                gain.add(act(side, loads, starts, parts, face_id, flags, cells, target_rows), face)
             for which in range(2):
-                sums[pl.ds(lines[ix][which], 8), :] = total[which]
+                sums[pl.ds(starts[which], 8), :] = gain.folded(which)
         return carry
 
-    lax.fori_loop(0, ny * half, column, 0)
-
-    def across(level, carry):
-        args = (flags, cells, target_rows, load_rows, sums)
-        for ix in range(nx):
-            for iy in range(ny):
-                target = starts_of(ix, iy, level)
-                total = None
-                for near, step in ((3, 1), (4, -1)):
-                    other = iy + step
-                    if 0 <= other < ny:
-                        source = starts_of(ix, other, level)
-                        more = act(sides[(ix * ny + other) * half + level], source, target, near, *args)
-                        total = more if total is None else [a + b for a, b in zip(total, more)]
-                for which in range(2):
-                    sums[pl.ds(target[which], 8), :] = sums[pl.ds(target[which], 8), :] + total[which]
-        return carry
-
-    if ny > 1:
-        lax.fori_loop(0, half, across, 0)
-
-
-def rim_kernel(dims, flags, place, load, part, place_xl, place_xh, place_yl, place_yh,
-               load_xl, load_xh, load_yl, load_yh, place_out, spin_out,
-               source_rows, load_rows, target_rows, sums):
+    lax.fori_loop(0, half, level_of, 0)
+
+
+def rim_kernel(dims, edges, flags, place, load, part, place_xl, place_xh, place_yl, place_yh,
+               load_xl, load_xh, load_yl, load_yh, place_out, spin_out, *rest):
     nx, ny, nz, slots = dims
+    source_rows, load_rows, target_rows, sums = rest[-4:]
     half = nz // 2
     cells = nx * ny * nz
     for ix in range(nx):
@@ -200,22 +216,24 @@
         links.append((ix, 0, 4, place_yl, load_yl, (ix, 0)))
         links.append((ix, ny - 1, 3, place_yh, load_yh, (ix, 0)))
     for slot, (_, _, _, places, loads, at) in enumerate(links):
-        fill_source([places[d, *at] for d in range(3)], [loads[d, *at] for d in range(4)],
+        fill_source([places[d, *at] for d in range(3)], [loads[3 + d, *at] for d in range(4)],
                     slot * nz * 8, nz, source_rows, load_rows)
 
     def level_of(level, carry):
-        gained = {}
-        for slot, (ix, iy, face_id, _, _, _) in enumerate(links):
-            source = [aligned((slot * nz + level + which * half) * 8) for which in range(2)]
-            target = [aligned(((ix * ny + iy) * nz + level + which * half) * 8) for which in range(2)]
-            side = source_side(source_rows, source)
-            more = act(side, source, target, face_id, flags, cells, target_rows, load_rows, sums)
-            if (ix, iy) in gained:
-                more = [a + b for a, b in zip(gained[ix, iy][1], more)]
-            gained[ix, iy] = (target, more)
-        for target, more in gained.values():
-            for which in range(2):
-                sums[pl.ds(target[which], 8), :] = sums[pl.ds(target[which], 8), :] + more[which]
+        for ix in range(nx):
+            for iy in range(ny):
+                mine = [(slot, link[2]) for slot, link in enumerate(links) if link[:2] == (ix, iy)]
+                if not mine:
+                    continue
+                starts = [aligned(((ix * ny + iy) * nz + level + which * half) * 8) for which in range(2)]
+                parts = [target_parts(target_rows, start) for start in starts]
+                gain = Gain()
+                for slot, face_id in mine:
+                    source = [aligned((slot * nz + level + which * half) * 8) for which in range(2)]
+                    gain.add(act(source_side(source_rows, source), [load_block(load_rows, start) for start in source],
+                                 starts, parts, face_id, flags, cells, target_rows), FACES[face_id])
+                for which in range(2):
+                    sums[pl.ds(starts[which], 8), :] = sums[pl.ds(starts[which], 8), :] + gain.folded(which)
         return carry
 
     lax.fori_loop(0, half, level_of, 0)
@@ -224,15 +242,23 @@
         for iy in range(ny):
             base = (ix * ny + iy) * nz * 8
             rows = [sums[pl.ds(base + row, nz, stride=8), :] for row in range(7)]
-            filled = load[3, ix, iy]
+            filled = load[6, ix, iy]
             xyz = [place[d, ix, iy] - 0.5 * CELL for d in range(3)]
             for d in range(3):
                 after, before = (d + 1) % 3, (d + 2) % 3
                 drive = rows[after] * xyz[before] - rows[before] * xyz[after] - rows[3 + d]
                 velocity = drift_gain / slots * drive * filled
-                place_out[d, ix, iy] = place[d, ix, iy] + step_pace * CELL * velocity
-                torque = load[d, ix, iy]
+                moved = place[d, ix, iy] + step_pace * CELL * velocity
+                place_out[d, ix, iy] = moved
+                torque = load[3 + d, ix, iy]
                 spin_out[d, ix, iy] = torque + couple_gain / slots * (filled * rows[d] - rows[6] * torque)
+                if edges:
+                    for out, here in zip(rest[:2], (nx - 1, 0)):
+                        if ix == here:
+                            out[d, 0, iy] = moved
+                    for out, here in zip(rest[2:4], (ny - 1, 0)):
+                        if iy == here:
+                            out[d, ix, 0] = moved
 
 
 def pair_cost(tiles, slots):
@@ -240,7 +266,7 @@
                            transcendentals=tiles * slots * slots)
 
 
-def near_step(places, loads, flags, load_rim):
+def near_step(places, packed, flags, place_rim, load_rim, edges):
     _, nx, ny, nz, slots = places.shape
     cells = nx * ny * nz
     vmem = pl.BlockSpec(memory_space=pltpu.VMEM)
@@ -249,29 +275,39 @@
     faces = nx * ny * 7 - 2 * (nx + ny)
     rows = pltpu.VMEM((cells * 8, slots), jnp.float32)
     params = pltpu.CompilerParams(vmem_limit_bytes=VMEM_LIMIT)
-    place_rim = rim(places)
     part = pl.pallas_call(
         functools.partial(local_kernel, dims), out_shape=jax.ShapeDtypeStruct((cells * 8, slots), jnp.float32),
         in_specs=[smem, vmem, vmem], out_specs=vmem,
-        scratch_shapes=[rows, rows, rows, pltpu.VMEM((cells // 2, slots, 128), jnp.bfloat16)],
+        scratch_shapes=[rows, rows, rows, pltpu.VMEM((nx * ny * (nz // 2 + 2), slots, slots), jnp.bfloat16),
+                        pltpu.VMEM((cells, 16, slots), jnp.bfloat16)],
         compiler_params=params, cost_estimate=pair_cost(faces * nz, slots), name="near_local",
-    )(flags, places, loads)
+    )(flags, places, packed)
     rim_rows = pltpu.VMEM((2 * (nx + ny) * nz * 8, slots), jnp.float32)
-    return pl.pallas_call(
-        functools.partial(rim_kernel, dims), out_shape=[jax.ShapeDtypeStruct(places.shape, jnp.float32)] * 2,
-        in_specs=[smem] + [vmem] * 11, out_specs=[vmem] * 2, scratch_shapes=[rim_rows, rim_rows, rows, rows],
+    shapes = [places.shape] * 2
+    if edges:
+        shapes += [(3, 1, ny, nz, slots)] * 2 + [(3, nx, 1, nz, slots)] * 2
+    out = pl.pallas_call(
+        functools.partial(rim_kernel, dims, edges), out_shape=[jax.ShapeDtypeStruct(s, jnp.float32) for s in shapes],
+        in_specs=[smem] + [vmem] * 11, out_specs=[vmem] * len(shapes), scratch_shapes=[rim_rows, rim_rows, rows, rows],
         compiler_params=params, cost_estimate=pair_cost(2 * (nx + ny) * nz, slots), name="near_rim",
-    )(flags, places, loads, part, *place_rim, *load_rim)
-
-
-def rim(block):
+    )(flags, places, packed, part, *place_rim, *load_rim)
+    return out[0], out[1], out[2:]
+
+
+def edges_of(block):
     out = []
-    for axis, dim in (("row", 1), ("col", 2)):
+    for dim in (1, 2):
+        out.append(lax.slice_in_dim(block, block.shape[dim] - 1, None, axis=dim))
+        out.append(lax.slice_in_dim(block, 0, 1, axis=dim))
+    return out
+
+
+def rim(edges):
+    out = []
+    for index, axis in enumerate(("row", "row", "col", "col")):
         count = lax.axis_size(axis)
-        forward = [(i, (i + 1) % count) for i in range(count)]
-        backward = [(target, source) for source, target in forward]
-        out.append(lax.ppermute(lax.slice_in_dim(block, block.shape[dim] - 1, None, axis=dim), axis, forward))
-        out.append(lax.ppermute(lax.slice_in_dim(block, 0, 1, axis=dim), axis, backward))
+        step = 1 if index % 2 == 0 else count - 1
+        out.append(lax.ppermute(edges[index], axis, [(i, (i + step) % count) for i in range(count)]))
     return out
 
 
@@ -396,7 +432,7 @@
             def cell(cz, carry, xp=xp, iy=iy):
                 high, low, thirds = planar_pair(place, 2 * xp, iy, cz)
                 lifted = jnp.concatenate(
-                    [jnp.concatenate([load[q, 2 * xp + which, iy, pl.ds(cz, 1), :] * thirds[which]
+                    [jnp.concatenate([load[3 + q, 2 * xp + which, iy, pl.ds(cz, 1), :] * thirds[which]
                                       for q in range(3)], 0) for which in range(2)], 1)
                 total = lax.dot_general(paired(lifted), jnp.concatenate([high, low], 1), (((1,), (1,)), ((), ())),
                                         preferred_element_type=jnp.float32)
@@ -443,7 +479,7 @@
                 total = total[:3 * CELL] + total[3 * CELL:]
                 for which in range(2):
                     at = (2 * xp + which, iy, pl.ds(cz, 1))
-                    filled = load[3, *at, :]
+                    filled = load[6, *at, :]
                     for q in range(3):
                         part = total[q * CELL:(q + 1) * CELL, which * slots:(which + 1) * slots] * thirds[which]
                         out[q, *at, :] = near[q, *at, :] + filled * jnp.sum(part, axis=0, keepdims=True)
@@ -692,14 +728,17 @@
 def shards(positions, torques, counts, neighbour_flags):
     slot_count = positions.shape[4]
     filled = (jnp.arange(slot_count, dtype=jnp.int32) < counts[..., None]).astype(jnp.float32)
-    places = positions
-    loads = jnp.concatenate([torques * filled, filled[None]], 0)
-    load_rim = rim(loads)
+    packed = jnp.concatenate([positions, torques * filled, filled[None]], 0)
+    load_rim = rim(edges_of(packed))
     flags = neighbour_flags.reshape(-1)
+    places, place_rim = positions, load_rim
     spin_near = None
     for step_id in range(STEPS):
-        places, spin_near = near_step(places, loads, flags, load_rim)
-    return (places, far_field(places, loads, spin_near))
+        more = step_id < STEPS - 1
+        places, spin_near, edges = near_step(places, packed, flags, place_rim, load_rim, more)
+        if more:
+            place_rim = rim(edges)
+    return (places, far_field(places, packed, spin_near))
 
 
 def solution(mesh):

time: 201 us -> 179 us (0.89)
  Pallas kernels: 114 us -> 103 us
  starting transfers between devices: 24.5 us -> 19.7 us
  local copies, waits for them, and re-layouts: 8.16 us -> 4.8 us
  blocking collectives: 51.1 us -> 48.2 us
    pallas_call x3, Pallas kernels: 65.4 us -> 54 us  [near_step(): pl.pallas_call(functools.partial(local_kernel, dims), out_shape=jax.Shape...]
    ppermute x16 -> x12, starting transfers between devices: 24.5 us -> 19.7 us  [rim(): lax.ppermute(edges[index], axis, [(i, (i + step) % count) for i in range(...]
    all_to_all x2, blocking collectives: 51.1 us -> 48.2 us  [turn(): return lax.all_to_all(lines, axis, split_axis=0, concat_axis=0, tiled=True)]
    slice x6 -> x2, local copies, waits for them, and re-layouts: 2.67 us -> 0.05 us  [edges_of(): out.append(lax.slice_in_dim(block, 0, 1, axis=dim))]
    unnamed x44 -> x32, local copies, waits for them, and re-layouts: 4.82 us -> 4.05 us
  transfers between devices with their start and end apart: 16 -> 12, of which waited for: 0 -> 0; matrix products, arithmetic and copies ran while one was open for 1% -> 0% of each run, Pallas kernels for 33% -> 30%
where the time goes in v5:
time: 179 us
  Pallas kernels  103 us (58%)
  blocking collectives  48.2 us (27%)
  starting transfers between devices  19.7 us (11%)
  local copies, waits for them, and re-layouts  4.8 us (3%)
  other arithmetic  1.93 us (1%)
    pallas_call x3, Pallas kernels, near_step(): pl.pallas_call(functools.partial(local_kernel, dims), out_shape=jax.Shape...  54 us
    all_to_all x2, blocking collectives, turn(): return lax.all_to_all(lines, axis, split_axis=0, concat_axis=0, tiled=True)  48.2 us
    pallas_call x3, Pallas kernels, near_step(): pl.pallas_call(functools.partial(rim_kernel, dims, edges), out_shape=[jax...  26.8 us
    pallas_call x3, Pallas kernels, local_call(): pl.pallas_call(kernel, out_shape=jax.ShapeDtypeStruct(shape, jnp.float32)...  22.3 us
    ppermute x12, starting transfers between devices, rim(): lax.ppermute(edges[index], axis, [(i, (i + step) % count) for i in range(...  19.7 us
    unnamed x32, local copies, waits for them, and re-layouts  4.05 us
  transfers between devices with their start and end apart: 12, of which 0 were waited for; matrix products, arithmetic and copies ran while one was open for 0% of the time, Pallas kernels for 30%

profile of v5, /device:TPU:0, one launch (start us, length us, event | category | flops | bytes accessed | tf_op | source)
XLA Modules:
  0.0 178.7 jit_solution(16284574494790090068)
XLA Ops:
  0.6 0.8 fusion.1
  1.5 0.1 fusion
  1.6 0.0 copy-start.1
  1.6 1.0 broadcast_multiply_fusion
  2.6 0.0 copy-done.1
  2.7 5.1 %collective-permute-start.1 = (f32[7,1,2,16,128]{4,3,2,1,0:T(8,128)S(1)}, f32[7,1,2,16,128]{4,3,2,1,0:T(8,128)S(1)}, u32[]{:S(2)}, u32[]{:S(2)}) collective-permute-start(f32[7,1,2,16,128]{4,3,2,1,0:T(8,128)S(1)} %get-tuple-element.28), channel_id=1, source_target_pairs={{0,24},{8,0},{16,8},{24,16},{1,25},{9,1},{17,9},{25,17},{2,26},{10... | collective-permute-start | bytes 344072 | tf_op jit(solution)/shard_map/ppermute | solution.py:310
  7.8 0.0 collective-permute-start
  7.8 1.7 collective-permute-start.3
  9.5 0.0 collective-permute-start.2
  9.5 0.7 reshape.24.flags
  10.2 18.0 %near_local.3.part = f32[1024,128]{1,0:T(8,128)} custom-call(s32[768]{0:T(1024)} %reshape.24.flags, f32[3,4,2,16,128]{4,3,2,1,0:T(8,128)} %place.3, f32[7,4,2,16,128]{4,3,2,1,0:T(8,128)} %copy-done), custom_call_target="tpu_custom_call" | custom-call | flops 2952790016 | bytes 4194304 | tf_op jit(solution)/shard_map/near_local/pallas_call | solution.py:278
  28.2 0.0 collective-permute-done.1.place_xh.load_xh
  28.2 0.0 collective-permute-done.place_xl.load_xl
  28.2 0.0 collective-permute-done.3.place_yh.load_yh
  28.2 0.0 collective-permute-done.2.place_yl.load_yl
  28.2 0.6 copy-done.6
  28.8 0.1 copy-done.7
  28.9 0.1 copy-done.4
  29.0 0.7 copy-done.5
  29.7 9.0 %near_rim.3 = (f32[3,4,2,16,128]{4,3,2,1,0:T(8,128)}, f32[3,4,2,16,128]{4,3,2,1,0:T(8,128)}, f32[3,1,2,16,128]{4,3,2,1,0:T(8,128)}, f32[3,1,2,16,128]{4,3,2,1,0:...) custom-call(s32[768]{0:T(1024)} %reshape.24.flags, f32[3,4,2,16,128]{4,3,2,1,0:T(8,128)} %place.3, ...), custom_call_target="tpu_custom_call" | custom-call | flops 805306368 | bytes 4194304 | tf_op jit(solution)/shard_map/near_rim/pallas_call | solution.py:289
  38.7 0.0 collective-permute-start.4
  38.7 3.8 %collective-permute-start.5 = (f32[3,1,2,16,128]{4,3,2,1,0:T(8,128)}, f32[3,1,2,16,128]{4,3,2,1,0:T(8,128)S(1)}, u32[]{:S(2)}, u32[]{:S(2)}) collective-permute-start(f32[3,1,2,16,128]{4,3,2,1,0:T(8,128)} %get-tuple-element.16), channel_id=1, source_target_pairs={{0,24},{8,0},{16,8},{24,16},{1,25},{9,1},{17,9},{25,17},{2,26},{10... | collective-permute-start | bytes 147464 | tf_op jit(solution)/shard_map/ppermute | solution.py:310
  42.5 0.0 collective-permute-start.6
  42.6 2.6 %collective-permute-start.7 = (f32[3,4,1,16,128]{4,3,2,1,0:T(8,128)}, f32[3,4,1,16,128]{4,3,2,1,0:T(8,128)S(1)}, u32[]{:S(2)}, u32[]{:S(2)}) collective-permute-start(f32[3,4,1,16,128]{4,3,2,1,0:T(8,128)} %get-tuple-element.18), channel_id=1, source_target_pairs={{0,7},{1,0},{2,1},{3,2},{4,3},{5,4},{6,5},{7,6},{8,15},{9,8},{10,9... | collective-permute-start | bytes 294920 | tf_op jit(solution)/shard_map/ppermute | solution.py:310
  45.2 18.0 %near_local.4.part = f32[1024,128]{1,0:T(8,128)} custom-call(s32[768]{0:T(1024)} %reshape.24.flags, f32[3,4,2,16,128]{4,3,2,1,0:T(8,128)} %get-tuple-element.14.place, f32[7,4,2,16,128]{4,3,2,1,0:T(8,128)} %copy-done), custom_call_target="tpu_custom_call" | custom-call | flops 2952790016 | bytes 4194304 | tf_op jit(solution)/shard_map/near_local/pallas_call | solution.py:278
  63.2 0.0 collective-permute-done.6.place_yl
  63.2 0.6 copy-done.13
  63.8 0.0 copy-done.15
  63.8 0.1 copy-done.9
  63.9 0.6 copy-done.11
  64.5 8.9 %near_rim.4 = (f32[3,4,2,16,128]{4,3,2,1,0:T(8,128)}, f32[3,4,2,16,128]{4,3,2,1,0:T(8,128)}, f32[3,1,2,16,128]{4,3,2,1,0:T(8,128)}, f32[3,1,2,16,128]{4,3,2,1,0:...) custom-call(s32[768]{0:T(1024)} %reshape.24.flags, ...), custom_call_target="tpu_custom_call" | custom-call | flops 805306368 | bytes 4194304 | tf_op jit(solution)/shard_map/near_rim/pallas_call | solution.py:289
  73.4 0.0 collective-permute-start.8
  73.5 3.8 %collective-permute-start.9 = (f32[3,1,2,16,128]{4,3,2,1,0:T(8,128)}, f32[3,1,2,16,128]{4,3,2,1,0:T(8,128)S(1)}, u32[]{:S(2)}, u32[]{:S(2)}) collective-permute-start(f32[3,1,2,16,128]{4,3,2,1,0:T(8,128)} %get-tuple-element.21), channel_id=1, source_target_pairs={{0,24},{8,0},{16,8},{24,16},{1,25},{9,1},{17,9},{25,17},{2,26},{10... | collective-permute-start | bytes 147464 | tf_op jit(solution)/shard_map/ppermute | solution.py:310
  77.3 2.6 %collective-permute-start.11 = (f32[3,4,1,16,128]{4,3,2,1,0:T(8,128)}, f32[3,4,1,16,128]{4,3,2,1,0:T(8,128)S(1)}, u32[]{:S(2)}, u32[]{:S(2)}) collective-permute-start(f32[3,4,1,16,128]{4,3,2,1,0:T(8,128)} %get-tuple-element.23), channel_id=1, source_target_pairs={{0,7},{1,0},{2,1},{3,2},{4,3},{5,4},{6,5},{7,6},{8,15},{9,8},{10,9... | collective-permute-start | bytes 294920 | tf_op jit(solution)/shard_map/ppermute | solution.py:310
  79.9 18.0 %near_local.5.part = f32[1024,128]{1,0:T(8,128)} custom-call(s32[768]{0:T(1024)} %reshape.24.flags, f32[3,4,2,16,128]{4,3,2,1,0:T(8,128)} %get-tuple-element.19.place, f32[7,4,2,16,128]{4,3,2,1,0:T(8,128)} %copy-done), custom_call_target="tpu_custom_call" | custom-call | flops 2952790016 | bytes 4194304 | tf_op jit(solution)/shard_map/near_local/pallas_call | solution.py:278
  97.9 0.0 collective-permute-done.8.place_xl
  98.0 0.0 collective-permute-done.10.place_yl
  98.0 0.0 copy-start.8
  98.0 0.6 copy-done.12
  98.6 0.0 copy-done.14
  98.6 0.0 copy-done.8
  98.6 0.6 copy-done.10
  99.3 8.8 %near_rim.5 = (f32[3,4,2,16,128]{4,3,2,1,0:T(8,128)}, f32[3,4,2,16,128]{4,3,2,1,0:T(8,128)}) custom-call(s32[768]{0:T(1024)} %reshape.24.flags, f32[3,4,2,16,128]{4,3,2,1,0:T(8,128)} %get-tuple-element.19.place, f32[7,4,2,16,128]{4,3,2,1,0:T(8,128)} %copy-done, f32[1024,128]{1,0:T(8,128)} %near_local.5.part, f32[3,1,2,16,128]{4,3,2,1,0:T(8,128)} %copy-done.12, ...), custom_call_target="tpu_custom_call" | custom-call | flops 805306368 | bytes 4194304 | tf_op jit(solution)/shard_map/near_rim/pallas_call | solution.py:289
  108.1 9.3 %spread_third.1 = f32[32,3,1,16,128]{4,3,2,1,0:T(8,128)} custom-call(f32[3,4,2,16,128]{4,3,2,1,0:T(8,128)} %get-tuple-element.12.place, f32[7,4,2,16,128]{4,3,2,1,0:T(8,128)} %copy-done, bf16[2,128,128]{2,1,0:T(8,128)(2,1)} %constant.16.clone.table), custom_call_target="tpu_custom_call" | custom-call | tf_op jit(solution)/shard_map/spread_third/pallas_call | solution.py:682
  117.4 23.9 %all_to_all.10.lines_in = f32[32,3,16,128]{3,2,1,0:T(8,128)} all-to-all(f32[32,3,16,128]{3,2,1,0:T(8,128)} %bitcast.2), channel_id=1, replica_groups=mesh['row'=4,'col'=8] {'row','col'}, dimensions={0} | all-to-all | bytes 1572864 | tf_op jit(solution)/shard_map/all_to_all | solution.py:705
  141.3 5.0 %planes_stokes.1 = f32[32,3,16,128]{3,2,1,0:T(8,128)} custom-call(bf16[2,128,128]{2,1,0:T(8,128)(2,1)} %constant.12.clone.table, bf16[2,128,128]{2,1,0:T(8,128)(2,1)} %constant.14.clone.table_turned, bf16[2,128,128]{2,1,0:T(8,128)(2,1)} %constant.13.clone.back, bf16[2,128,128]{2,1,0:T(8,128)(2,1)} %constant.15.clone.back_turned, ...), custom_call_target="tpu_custom_call" | custom-call | tf_op jit(solution)/shard_map/planes_stokes/pallas_call | solution.py:682
  146.3 24.3 %all_to_all.11 = f32[32,3,16,128]{3,2,1,0:T(8,128)} all-to-all(f32[32,3,16,128]{3,2,1,0:T(8,128)} %planes_stokes.1), channel_id=1, replica_groups=mesh['row'=4,'col'=8] {'row','col'}, dimensions={0} | all-to-all | bytes 1572864 | tf_op jit(solution)/shard_map/all_to_all | solution.py:705
  170.6 8.0 %third_gather.1 = f32[3,4,2,16,128]{4,3,2,1,0:T(8,128)} custom-call(f32[3,4,2,16,128]{4,3,2,1,0:T(8,128)} %get-tuple-element.12.place, f32[7,4,2,16,128]{4,3,2,1,0:T(8,128)} %copy-done, f32[3,4,2,16,128]{4,3,2,1,0:T(8,128)} %get-tuple-element.25.near, bf16[2,128,128]{2,1,0:T(8,128)(2,1)} %constant.17.clone.table, f32[32,3,1,16,128]{4,3,2,1,0:T(8,128)} %bitcast.3), custom_call_target="tpu_custom_call" | custom-call | tf_op jit(solution)/shard_map/third_gather/pallas_call | solution.py:682
  (26 shorter events, 0.1 us)
Async XLA Ops:
  0.6 0.9 copy-start.3
  1.6 1.0 copy-start.1
  2.6 5.2 %copy-start = (f32[7,4,2,16,128]{4,3,2,1,0:T(8,128)}, f32[7,4,2,16,128]{4,3,2,1,0:T(8,128)S(1)}, u32[]{:S(2)}) copy-start(f32[7,4,2,16,128]{4,3,2,1,0:T(8,128)S(1)} %pad_maximum_fusion.load) | copy-start | bytes 1376260
  2.7 25.5 %collective-permute-start.1 = (f32[7,1,2,16,128]{4,3,2,1,0:T(8,128)S(1)}, f32[7,1,2,16,128]{4,3,2,1,0:T(8,128)S(1)}, u32[]{:S(2)}, u32[]{:S(2)}) collective-permute-start(f32[7,1,2,16,128]{4,3,2,1,0:T(8,128)S(1)} %get-tuple-element.28), channel_id=1, source_target_pairs={{0,24},{8,0},{16,8},{24,16},{1,25},{9,1},{17,9},{25,17},{2,26},{10... | collective-permute-start | bytes 344072 | tf_op jit(solution)/shard_map/ppermute | solution.py:310
  7.8 1.7 copy-start.2
  7.8 20.4 %collective-permute-start = (f32[7,1,2,16,128]{4,3,2,1,0:T(8,128)S(1)}, f32[7,1,2,16,128]{4,3,2,1,0:T(8,128)S(1)}, u32[]{:S(2)}, u32[]{:S(2)}) collective-permute-start(f32[7,1,2,16,128]{4,3,2,1,0:T(8,128)S(1)} %get-tuple-element.29), channel_id=1, source_target_pairs={{0,8},{8,16},{16,24},{24,0},{1,9},{9,17},{17,25},{25,1},{2,10},{10... | collective-permute-start | bytes 344072 | tf_op jit(solution)/shard_map/ppermute | solution.py:310
  7.8 20.4 %collective-permute-start.3 = (f32[7,4,1,16,128]{4,3,2,1,0:T(8,128)S(1)}, f32[7,4,1,16,128]{4,3,2,1,0:T(8,128)S(1)}, u32[]{:S(2)}, u32[]{:S(2)}) collective-permute-start(f32[7,4,1,16,128]{4,3,2,1,0:T(8,128)S(1)} %get-tuple-element.26), channel_id=1, source_target_pairs={{0,7},{1,0},{2,1},{3,2},{4,3},{5,4},{6,5},{7,6},{8,15},{9,8},{10,9... | collective-permute-start | bytes 688136 | tf_op jit(solution)/shard_map/ppermute | solution.py:310
  9.5 18.7 %collective-permute-start.2 = (f32[7,4,1,16,128]{4,3,2,1,0:T(8,128)S(1)}, f32[7,4,1,16,128]{4,3,2,1,0:T(8,128)S(1)}, u32[]{:S(2)}, u32[]{:S(2)}) collective-permute-start(f32[7,4,1,16,128]{4,3,2,1,0:T(8,128)S(1)} %get-tuple-element.27), channel_id=1, source_target_pairs={{0,1},{1,2},{2,3},{3,4},{4,5},{5,6},{6,7},{7,0},{8,9},{9,10},{10,1... | collective-permute-start | bytes 688136 | tf_op jit(solution)/shard_map/ppermute | solution.py:310
  28.2 0.6 copy-start.6
  28.2 0.7 copy-start.7
  28.2 0.8 copy-start.4
  29.0 0.7 copy-start.5
  38.7 24.5 %collective-permute-start.4 = (f32[3,1,2,16,128]{4,3,2,1,0:T(8,128)}, f32[3,1,2,16,128]{4,3,2,1,0:T(8,128)S(1)}, u32[]{:S(2)}, u32[]{:S(2)}) collective-permute-start(f32[3,1,2,16,128]{4,3,2,1,0:T(8,128)} %get-tuple-element.15), channel_id=1, source_target_pairs={{0,8},{8,16},{16,24},{24,0},{1,9},{9,17},{17,25},{25,1},{2,10},{10... | collective-permute-start | bytes 147464 | tf_op jit(solution)/shard_map/ppermute | solution.py:310
  38.7 24.5 %collective-permute-start.5 = (f32[3,1,2,16,128]{4,3,2,1,0:T(8,128)}, f32[3,1,2,16,128]{4,3,2,1,0:T(8,128)S(1)}, u32[]{:S(2)}, u32[]{:S(2)}) collective-permute-start(f32[3,1,2,16,128]{4,3,2,1,0:T(8,128)} %get-tuple-element.16), channel_id=1, source_target_pairs={{0,24},{8,0},{16,8},{24,16},{1,25},{9,1},{17,9},{25,17},{2,26},{10... | collective-permute-start | bytes 147464 | tf_op jit(solution)/shard_map/ppermute | solution.py:310
  42.5 20.7 %collective-permute-start.6 = (f32[3,4,1,16,128]{4,3,2,1,0:T(8,128)}, f32[3,4,1,16,128]{4,3,2,1,0:T(8,128)S(1)}, u32[]{:S(2)}, u32[]{:S(2)}) collective-permute-start(f32[3,4,1,16,128]{4,3,2,1,0:T(8,128)} %get-tuple-element.17), channel_id=1, source_target_pairs={{0,1},{1,2},{2,3},{3,4},{4,5},{5,6},{6,7},{7,0},{8,9},{9,10},{10,1... | collective-permute-start | bytes 294920 | tf_op jit(solution)/shard_map/ppermute | solution.py:310
  42.6 20.7 %collective-permute-start.7 = (f32[3,4,1,16,128]{4,3,2,1,0:T(8,128)}, f32[3,4,1,16,128]{4,3,2,1,0:T(8,128)S(1)}, u32[]{:S(2)}, u32[]{:S(2)}) collective-permute-start(f32[3,4,1,16,128]{4,3,2,1,0:T(8,128)} %get-tuple-element.18), channel_id=1, source_target_pairs={{0,7},{1,0},{2,1},{3,2},{4,3},{5,4},{6,5},{7,6},{8,15},{9,8},{10,9... | collective-permute-start | bytes 294920 | tf_op jit(solution)/shard_map/ppermute | solution.py:310
  63.2 0.6 copy-start.13
  63.2 0.6 copy-start.15
  63.2 0.7 copy-start.9
  63.9 0.6 copy-start.11
  73.4 24.5 %collective-permute-start.8 = (f32[3,1,2,16,128]{4,3,2,1,0:T(8,128)}, f32[3,1,2,16,128]{4,3,2,1,0:T(8,128)S(1)}, u32[]{:S(2)}, u32[]{:S(2)}) collective-permute-start(f32[3,1,2,16,128]{4,3,2,1,0:T(8,128)} %get-tuple-element.20), channel_id=1, source_target_pairs={{0,8},{8,16},{16,24},{24,0},{1,9},{9,17},{17,25},{25,1},{2,10},{10... | collective-permute-start | bytes 147464 | tf_op jit(solution)/shard_map/ppermute | solution.py:310
  73.5 24.5 %collective-permute-start.9 = (f32[3,1,2,16,128]{4,3,2,1,0:T(8,128)}, f32[3,1,2,16,128]{4,3,2,1,0:T(8,128)S(1)}, u32[]{:S(2)}, u32[]{:S(2)}) collective-permute-start(f32[3,1,2,16,128]{4,3,2,1,0:T(8,128)} %get-tuple-element.21), channel_id=1, source_target_pairs={{0,24},{8,0},{16,8},{24,16},{1,25},{9,1},{17,9},{25,17},{2,26},{10... | collective-permute-start | bytes 147464 | tf_op jit(solution)/shard_map/ppermute | solution.py:310
  77.3 20.7 %collective-permute-start.10 = (f32[3,4,1,16,128]{4,3,2,1,0:T(8,128)}, f32[3,4,1,16,128]{4,3,2,1,0:T(8,128)S(1)}, u32[]{:S(2)}, u32[]{:S(2)}) collective-permute-start(f32[3,4,1,16,128]{4,3,2,1,0:T(8,128)} %get-tuple-element.22), channel_id=1, source_target_pairs={{0,1},{1,2},{2,3},{3,4},{4,5},{5,6},{6,7},{7,0},{8,9},{9,10},{10,1... | collective-permute-start | bytes 294920 | tf_op jit(solution)/shard_map/ppermute | solution.py:310
  77.3 20.7 %collective-permute-start.11 = (f32[3,4,1,16,128]{4,3,2,1,0:T(8,128)}, f32[3,4,1,16,128]{4,3,2,1,0:T(8,128)S(1)}, u32[]{:S(2)}, u32[]{:S(2)}) collective-permute-start(f32[3,4,1,16,128]{4,3,2,1,0:T(8,128)} %get-tuple-element.23), channel_id=1, source_target_pairs={{0,7},{1,0},{2,1},{3,2},{4,3},{5,4},{6,5},{7,6},{8,15},{9,8},{10,9... | collective-permute-start | bytes 294920 | tf_op jit(solution)/shard_map/ppermute | solution.py:310
  97.9 0.6 copy-start.12
  97.9 0.6 copy-start.14
  98.0 0.6 copy-start.8
  98.6 0.6 copy-start.10

commit v6 on v5

--- a/solution.py
+++ b/solution.py
@@ -18,7 +18,7 @@
 bin_rate = 1.0
 RATE = 2.0 / (CELL * CELL) * math.log2(math.e)
 FACES = (None, (0, 1), (0, -1), (1, 1), (1, -1), (2, 1), (2, -1))
-VMEM_LIMIT = 56 * 1024 * 1024
+VMEM_LIMIT = 24 * 1024 * 1024
 
 
 def split_three(value):
@@ -173,7 +173,7 @@
                 blocks[cell] = load_block(load_rows, aligned(cell * 8))
         return carry
 
-    lax.fori_loop(0, half + 2, turn_level, 0)
+    lax.fori_loop(0, half + 2, turn_level, 0, unroll=5)
 
     def level_of(level, carry):
         for column, (ix, iy) in enumerate(columns):
@@ -195,7 +195,7 @@
                 sums[pl.ds(starts[which], 8), :] = gain.folded(which)
         return carry
 
-    lax.fori_loop(0, half, level_of, 0)
+    lax.fori_loop(0, half, level_of, 0, unroll=2)
 
 
 def rim_kernel(dims, edges, flags, place, load, part, place_xl, place_xh, place_yl, place_yh,
@@ -236,7 +236,7 @@
                     sums[pl.ds(starts[which], 8), :] = sums[pl.ds(starts[which], 8), :] + gain.folded(which)
         return carry
 
-    lax.fori_loop(0, half, level_of, 0)
+    lax.fori_loop(0, half, level_of, 0, unroll=2)
 
     for ix in range(nx):
         for iy in range(ny):
@@ -441,7 +441,7 @@
                     cubes[q, xp, iy, pl.ds(pl.multiple_of(cz * CELL, CELL), CELL), :] = total[q * CELL:(q + 1) * CELL]
                 return carry
 
-            lax.fori_loop(0, nz, cell, 0, unroll=4)
+            lax.fori_loop(0, nz, cell, 0, unroll=True)
     span = max(cols // (2 * CELL), 1)
     for q in range(3):
         for iy in range(ny):
@@ -485,7 +485,7 @@
                         out[q, *at, :] = near[q, *at, :] + filled * jnp.sum(part, axis=0, keepdims=True)
                 return carry
 
-            lax.fori_loop(0, nz, cell, 0, unroll=4)
+            lax.fori_loop(0, nz, cell, 0, unroll=True)
 
 
 def second_kernel(rows, cols, table, lines_in, out):

time: 179 us -> 146 us (0.82)
  Pallas kernels: 103 us -> 75.6 us
  local copies, waits for them, and re-layouts: 4.8 us -> 1.15 us
  blocking collectives: 48.2 us -> 46.4 us
    pallas_call x3, Pallas kernels: 22.3 us -> 11.7 us  [local_call(): pl.pallas_call(kernel, out_shape=jax.ShapeDtypeStruct(shape, jnp.float32)...]
    pallas_call x3, Pallas kernels: 54 us -> 44.6 us  [near_step(): pl.pallas_call(functools.partial(local_kernel, dims), out_shape=jax.Shape...]
    pallas_call x3, Pallas kernels: 26.8 us -> 19.3 us  [near_step(): pl.pallas_call(functools.partial(rim_kernel, dims, edges), out_shape=[jax...]
    unnamed x32 -> x22, local copies, waits for them, and re-layouts: 4.05 us -> 1.01 us
  transfers between devices with their start and end apart: 12 -> 12, of which waited for: 0 -> 0; matrix products, arithmetic and copies ran while one was open for 0% -> 0% of each run, Pallas kernels for 30% -> 31%
where the time goes in v6:
time: 146 us
  Pallas kernels  75.6 us (52%)
  blocking collectives  46.4 us (32%)
  starting transfers between devices  19.7 us (13%)
  other arithmetic  1.93 us (1%)
    all_to_all x2, blocking collectives, turn(): return lax.all_to_all(lines, axis, split_axis=0, concat_axis=0, tiled=True)  46.4 us
    pallas_call x3, Pallas kernels, near_step(): pl.pallas_call(functools.partial(local_kernel, dims), out_shape=jax.Shape...  44.6 us
    ppermute x12, starting transfers between devices, rim(): lax.ppermute(edges[index], axis, [(i, (i + step) % count) for i in range(...  19.7 us
    pallas_call x3, Pallas kernels, near_step(): pl.pallas_call(functools.partial(rim_kernel, dims, edges), out_shape=[jax...  19.3 us
    pallas_call x3, Pallas kernels, local_call(): pl.pallas_call(kernel, out_shape=jax.ShapeDtypeStruct(shape, jnp.float32)...  11.7 us
  transfers between devices with their start and end apart: 12, of which 0 were waited for; matrix products, arithmetic and copies ran while one was open for 0% of the time, Pallas kernels for 31%

profile of v6, /device:TPU:0, one launch (start us, length us, event | category | flops | bytes accessed | tf_op | source)
XLA Modules:
  0.0 145.8 jit_solution(7139349252490276572)
XLA Ops:
  0.6 0.8 fusion.1
  1.5 0.1 fusion
  1.6 0.0 copy-start.2
  1.6 1.0 broadcast_multiply_fusion
  2.6 0.0 copy-done.2
  2.7 5.1 %collective-permute-start.1 = (f32[7,1,2,16,128]{4,3,2,1,0:T(8,128)S(1)}, f32[7,1,2,16,128]{4,3,2,1,0:T(8,128)S(1)}, u32[]{:S(2)}, u32[]{:S(2)}) collective-permute-start(f32[7,1,2,16,128]{4,3,2,1,0:T(8,128)S(1)} %get-tuple-element.28), channel_id=1, source_target_pairs={{0,24},{8,0},{16,8},{24,16},{1,25},{9,1},{17,9},{25,17},{2,26},{10... | collective-permute-start | bytes 344072 | tf_op jit(solution)/shard_map/ppermute | solution.py:310
  7.8 0.0 collective-permute-start
  7.8 1.7 %collective-permute-start.3 = (f32[7,4,1,16,128]{4,3,2,1,0:T(8,128)S(1)}, f32[7,4,1,16,128]{4,3,2,1,0:T(8,128)S(1)}, u32[]{:S(2)}, u32[]{:S(2)}) collective-permute-start(f32[7,4,1,16,128]{4,3,2,1,0:T(8,128)S(1)} %get-tuple-element.26), channel_id=1, source_target_pairs={{0,7},{1,0},{2,1},{3,2},{4,3},{5,4},{6,5},{7,6},{8,15},{9,8},{10,9... | collective-permute-start | bytes 688136 | tf_op jit(solution)/shard_map/ppermute | solution.py:310
  9.5 0.0 collective-permute-start.2
  9.5 0.1 reshape.24.flags
  9.6 14.9 %near_local.3.part = f32[1024,128]{1,0:T(8,128)S(1)} custom-call(s32[768]{0:T(1024)S(1)} %reshape.24.flags, f32[3,4,2,16,128]{4,3,2,1,0:T(8,128)S(1)} %copy-done.2, f32[7,4,2,16,128]{4,3,2,1,0:T(8,128)S(1)} %pad_maximum_fusion.load), custom_call_target="tpu_custom_call" | custom-call | flops 2952790016 | bytes 4194304 | tf_op jit(solution)/shard_map/near_local/pallas_call | solution.py:278
  24.4 0.0 collective-permute-done.1.place_xh.load_xh
  24.5 0.0 collective-permute-done.place_xl.load_xl
  24.5 0.0 collective-permute-done.3.place_yh.load_yh
  24.5 0.0 collective-permute-done.2.place_yl.load_yl
  24.5 6.4 %near_rim.3 = (f32[3,4,2,16,128]{4,3,2,1,0:T(8,128)S(1)}, f32[3,4,2,16,128]{4,3,2,1,0:T(8,128)}, f32[3,1,2,16,128]{4,3,2,1,0:T(8,128)S(1)}, f32[3,1,2,16,128]{4,...) custom-call(s32[768]{0:T(1024)S(1)} %reshape.24.flags, ...), custom_call_target="tpu_custom_call" | custom-call | flops 805306368 | bytes 4194304 | tf_op jit(solution)/shard_map/near_rim/pallas_call | solution.py:289
  30.9 0.0 collective-permute-start.4
  30.9 3.8 %collective-permute-start.5 = (f32[3,1,2,16,128]{4,3,2,1,0:T(8,128)S(1)}, f32[3,1,2,16,128]{4,3,2,1,0:T(8,128)S(1)}, u32[]{:S(2)}, u32[]{:S(2)}) collective-permute-start(f32[3,1,2,16,128]{4,3,2,1,0:T(8,128)S(1)} %get-tuple-element.16), channel_id=1, source_target_pairs={{0,24},{8,0},{16,8},{24,16},{1,25},{9,1},{17,9},{25,17},{2,26},{10... | collective-permute-start | bytes 147464 | tf_op jit(solution)/shard_map/ppermute | solution.py:310
  34.7 0.0 collective-permute-start.6
  34.7 2.6 %collective-permute-start.7 = (f32[3,4,1,16,128]{4,3,2,1,0:T(8,128)S(1)}, f32[3,4,1,16,128]{4,3,2,1,0:T(8,128)S(1)}, u32[]{:S(2)}, u32[]{:S(2)}) collective-permute-start(f32[3,4,1,16,128]{4,3,2,1,0:T(8,128)S(1)} %get-tuple-element.18), channel_id=1, source_target_pairs={{0,7},{1,0},{2,1},{3,2},{4,3},{5,4},{6,5},{7,6},{8,15},{9,8},{10,9... | collective-permute-start | bytes 294920 | tf_op jit(solution)/shard_map/ppermute | solution.py:310
  37.4 14.9 %near_local.4.part = f32[1024,128]{1,0:T(8,128)S(1)} custom-call(s32[768]{0:T(1024)S(1)} %reshape.24.flags, f32[3,4,2,16,128]{4,3,2,1,0:T(8,128)S(1)} %get-tuple-element.14.place, f32[7,4,2,16,128]{4,3,2,1,0:T(8,128)S(1)} %pad_maximum_fusion.load), custom_call_target="tpu_custom_call" | custom-call | flops 2952790016 | bytes 4194304 | tf_op jit(solution)/shard_map/near_local/pallas_call | solution.py:278
  52.3 0.0 collective-permute-done.4.place_xl
  52.3 0.0 collective-permute-done.5.place_xh
  52.3 0.0 collective-permute-done.6.place_yl
  52.3 0.0 collective-permute-done.7.place_yh
  52.3 6.4 %near_rim.4 = (f32[3,4,2,16,128]{4,3,2,1,0:T(8,128)S(1)}, f32[3,4,2,16,128]{4,3,2,1,0:T(8,128)}, f32[3,1,2,16,128]{4,3,2,1,0:T(8,128)S(1)}, f32[3,1,2,16,128]{4,...) custom-call(s32[768]{0:T(1024)S(1)} %reshape.24.flags, ...), custom_call_target="tpu_custom_call" | custom-call | flops 805306368 | bytes 4194304 | tf_op jit(solution)/shard_map/near_rim/pallas_call | solution.py:289
  58.7 0.0 collective-permute-start.8
  58.7 3.8 %collective-permute-start.9 = (f32[3,1,2,16,128]{4,3,2,1,0:T(8,128)S(1)}, f32[3,1,2,16,128]{4,3,2,1,0:T(8,128)S(1)}, u32[]{:S(2)}, u32[]{:S(2)}) collective-permute-start(f32[3,1,2,16,128]{4,3,2,1,0:T(8,128)S(1)} %get-tuple-element.21), channel_id=1, source_target_pairs={{0,24},{8,0},{16,8},{24,16},{1,25},{9,1},{17,9},{25,17},{2,26},{10... | collective-permute-start | bytes 147464 | tf_op jit(solution)/shard_map/ppermute | solution.py:310
  62.6 0.0 collective-permute-start.10
  62.6 2.6 %collective-permute-start.11 = (f32[3,4,1,16,128]{4,3,2,1,0:T(8,128)S(1)}, f32[3,4,1,16,128]{4,3,2,1,0:T(8,128)S(1)}, u32[]{:S(2)}, u32[]{:S(2)}) collective-permute-start(f32[3,4,1,16,128]{4,3,2,1,0:T(8,128)S(1)} %get-tuple-element.23), channel_id=1, source_target_pairs={{0,7},{1,0},{2,1},{3,2},{4,3},{5,4},{6,5},{7,6},{8,15},{9,8},{10,9... | collective-permute-start | bytes 294920 | tf_op jit(solution)/shard_map/ppermute | solution.py:310
  65.2 14.9 %near_local.5.part = f32[1024,128]{1,0:T(8,128)S(1)} custom-call(s32[768]{0:T(1024)S(1)} %reshape.24.flags, f32[3,4,2,16,128]{4,3,2,1,0:T(8,128)S(1)} %get-tuple-element.19.place, f32[7,4,2,16,128]{4,3,2,1,0:T(8,128)S(1)} %pad_maximum_fusion.load), custom_call_target="tpu_custom_call" | custom-call | flops 2952790016 | bytes 4194304 | tf_op jit(solution)/shard_map/near_local/pallas_call | solution.py:278
  80.1 0.0 copy-start.3
  80.1 0.0 collective-permute-done.8.place_xl
  80.1 0.0 collective-permute-done.10.place_yl
  80.1 0.0 collective-permute-done.11.place_yh
  80.1 6.4 %near_rim.5 = (f32[3,4,2,16,128]{4,3,2,1,0:T(8,128)}, f32[3,4,2,16,128]{4,3,2,1,0:T(8,128)S(1)}) custom-call(s32[768]{0:T(1024)S(1)} %reshape.24.flags, f32[3,4,2,16,128]{4,3,2,1,0:T(8,128)S(1)} %get-tuple-element.19.place, f32[7,4,2,16,128]{4,3,2,1,0:T(8,128)S(1)} %pad_maximum_fusion.load, f32[1024,128]{1,0:T(8,128)S(1)} %near_local.5.part, ...), custom_call_target="tpu_custom_call" | custom-call | flops 805306368 | bytes 4194304 | tf_op jit(solution)/shard_map/near_rim/pallas_call | solution.py:289
  86.6 0.9 copy-done
  87.5 4.7 %spread_third.1 = f32[32,3,1,16,128]{4,3,2,1,0:T(8,128)S(1)} custom-call(f32[3,4,2,16,128]{4,3,2,1,0:T(8,128)S(1)} %copy-done, f32[7,4,2,16,128]{4,3,2,1,0:T(8,128)S(1)} %pad_maximum_fusion.load, bf16[2,128,128]{2,1,0:T(8,128)(2,1)S(1)} %copy-done.3), custom_call_target="tpu_custom_call" | custom-call | tf_op jit(solution)/shard_map/spread_third/pallas_call | solution.py:682
  92.2 0.0 copy-start.4
  92.3 0.0 copy-start.5
  92.3 0.0 copy-start.6
  92.3 0.0 copy-start.7
  92.3 22.5 %all_to_all.10.lines_in = f32[32,3,16,128]{3,2,1,0:T(8,128)S(1)} all-to-all(f32[32,3,16,128]{3,2,1,0:T(8,128)S(1)} %bitcast.2), channel_id=1, replica_groups=mesh['row'=4,'col'=8] {'row','col'}, dimensions={0} | all-to-all | bytes 1572864 | tf_op jit(solution)/shard_map/all_to_all | solution.py:705
  114.8 2.8 %planes_stokes.1 = f32[32,3,16,128]{3,2,1,0:T(8,128)S(1)} custom-call(bf16[2,128,128]{2,1,0:T(8,128)(2,1)S(1)} %copy-done.7, bf16[2,128,128]{2,1,0:T(8,128)(2,1)S(1)} %copy-done.5, bf16[2,128,128]{2,1,0:T(8,128)(2,1)S(1)} %copy-done.6, bf16[2,128,128]{2,1,0:T(8,128)(2,1)S(1)} %copy-done.4, f32[32,3,16,128]{3,2,1,0:T(8,128)S(1)} %all_to_all.10.lines_in), custom_call_target="tpu_custom_call" | custom-call | tf_op jit(solution)/shard_map/planes_stokes/pallas_call | solution.py:682
  117.6 0.0 copy-start.1
  117.6 0.0 copy-start.8
  117.6 24.0 %all_to_all.11 = f32[32,3,16,128]{3,2,1,0:T(8,128)S(1)} all-to-all(f32[32,3,16,128]{3,2,1,0:T(8,128)S(1)} %planes_stokes.1), channel_id=1, replica_groups=mesh['row'=4,'col'=8] {'row','col'}, dimensions={0} | all-to-all | bytes 1572864 | tf_op jit(solution)/shard_map/all_to_all | solution.py:705
  141.6 4.2 %third_gather.1 = f32[3,4,2,16,128]{4,3,2,1,0:T(8,128)} custom-call(f32[3,4,2,16,128]{4,3,2,1,0:T(8,128)S(1)} %copy-done.1, f32[7,4,2,16,128]{4,3,2,1,0:T(8,128)S(1)} %pad_maximum_fusion.load, f32[3,4,2,16,128]{4,3,2,1,0:T(8,128)S(1)} %get-tuple-element.25.near, bf16[2,128,128]{2,1,0:T(8,128)(2,1)S(1)} %copy-done.8, f32[32,3,1,16,128]{4,3,2,1,0:T(8,128)S(1)} %bitcast.3), custom_call_target="tpu_custom_call" | custom-call | tf_op jit(solution)/shard_map/third_gather/pallas_call | solution.py:682
  (16 shorter events, 0.1 us)
Async XLA Ops:
  0.6 0.9 copy-start.10
  1.6 1.0 copy-start.2
  2.7 21.8 %collective-permute-start.1 = (f32[7,1,2,16,128]{4,3,2,1,0:T(8,128)S(1)}, f32[7,1,2,16,128]{4,3,2,1,0:T(8,128)S(1)}, u32[]{:S(2)}, u32[]{:S(2)}) collective-permute-start(f32[7,1,2,16,128]{4,3,2,1,0:T(8,128)S(1)} %get-tuple-element.28), channel_id=1, source_target_pairs={{0,24},{8,0},{16,8},{24,16},{1,25},{9,1},{17,9},{25,17},{2,26},{10... | collective-permute-start | bytes 344072 | tf_op jit(solution)/shard_map/ppermute | solution.py:310
  7.8 1.7 %copy-start.9 = (s32[6,4,2,16]{3,2,1,0:T(2,128)S(1)}, s32[6,4,2,16]{3,2,1,0:T(2,128)}, u32[]{:S(2)}) copy-start(s32[6,4,2,16]{3,2,1,0:T(2,128)} %param.13) | copy-start | bytes 9220
  7.8 16.7 %collective-permute-start = (f32[7,1,2,16,128]{4,3,2,1,0:T(8,128)S(1)}, f32[7,1,2,16,128]{4,3,2,1,0:T(8,128)S(1)}, u32[]{:S(2)}, u32[]{:S(2)}) collective-permute-start(f32[7,1,2,16,128]{4,3,2,1,0:T(8,128)S(1)} %get-tuple-element.29), channel_id=1, source_target_pairs={{0,8},{8,16},{16,24},{24,0},{1,9},{9,17},{17,25},{25,1},{2,10},{10... | collective-permute-start | bytes 344072 | tf_op jit(solution)/shard_map/ppermute | solution.py:310
  7.8 16.7 %collective-permute-start.3 = (f32[7,4,1,16,128]{4,3,2,1,0:T(8,128)S(1)}, f32[7,4,1,16,128]{4,3,2,1,0:T(8,128)S(1)}, u32[]{:S(2)}, u32[]{:S(2)}) collective-permute-start(f32[7,4,1,16,128]{4,3,2,1,0:T(8,128)S(1)} %get-tuple-element.26), channel_id=1, source_target_pairs={{0,7},{1,0},{2,1},{3,2},{4,3},{5,4},{6,5},{7,6},{8,15},{9,8},{10,9... | collective-permute-start | bytes 688136 | tf_op jit(solution)/shard_map/ppermute | solution.py:310
  9.5 15.0 %collective-permute-start.2 = (f32[7,4,1,16,128]{4,3,2,1,0:T(8,128)S(1)}, f32[7,4,1,16,128]{4,3,2,1,0:T(8,128)S(1)}, u32[]{:S(2)}, u32[]{:S(2)}) collective-permute-start(f32[7,4,1,16,128]{4,3,2,1,0:T(8,128)S(1)} %get-tuple-element.27), channel_id=1, source_target_pairs={{0,1},{1,2},{2,3},{3,4},{4,5},{5,6},{6,7},{7,0},{8,9},{9,10},{10,1... | collective-permute-start | bytes 688136 | tf_op jit(solution)/shard_map/ppermute | solution.py:310
  30.9 21.3 %collective-permute-start.4 = (f32[3,1,2,16,128]{4,3,2,1,0:T(8,128)S(1)}, f32[3,1,2,16,128]{4,3,2,1,0:T(8,128)S(1)}, u32[]{:S(2)}, u32[]{:S(2)}) collective-permute-start(f32[3,1,2,16,128]{4,3,2,1,0:T(8,128)S(1)} %get-tuple-element.15), channel_id=1, source_target_pairs={{0,8},{8,16},{16,24},{24,0},{1,9},{9,17},{17,25},{25,1},{2,10},{10... | collective-permute-start | bytes 147464 | tf_op jit(solution)/shard_map/ppermute | solution.py:310
  30.9 21.4 %collective-permute-start.5 = (f32[3,1,2,16,128]{4,3,2,1,0:T(8,128)S(1)}, f32[3,1,2,16,128]{4,3,2,1,0:T(8,128)S(1)}, u32[]{:S(2)}, u32[]{:S(2)}) collective-permute-start(f32[3,1,2,16,128]{4,3,2,1,0:T(8,128)S(1)} %get-tuple-element.16), channel_id=1, source_target_pairs={{0,24},{8,0},{16,8},{24,16},{1,25},{9,1},{17,9},{25,17},{2,26},{10... | collective-permute-start | bytes 147464 | tf_op jit(solution)/shard_map/ppermute | solution.py:310
  34.7 17.5 %collective-permute-start.6 = (f32[3,4,1,16,128]{4,3,2,1,0:T(8,128)S(1)}, f32[3,4,1,16,128]{4,3,2,1,0:T(8,128)S(1)}, u32[]{:S(2)}, u32[]{:S(2)}) collective-permute-start(f32[3,4,1,16,128]{4,3,2,1,0:T(8,128)S(1)} %get-tuple-element.17), channel_id=1, source_target_pairs={{0,1},{1,2},{2,3},{3,4},{4,5},{5,6},{6,7},{7,0},{8,9},{9,10},{10,1... | collective-permute-start | bytes 294920 | tf_op jit(solution)/shard_map/ppermute | solution.py:310
  34.7 17.6 %collective-permute-start.7 = (f32[3,4,1,16,128]{4,3,2,1,0:T(8,128)S(1)}, f32[3,4,1,16,128]{4,3,2,1,0:T(8,128)S(1)}, u32[]{:S(2)}, u32[]{:S(2)}) collective-permute-start(f32[3,4,1,16,128]{4,3,2,1,0:T(8,128)S(1)} %get-tuple-element.18), channel_id=1, source_target_pairs={{0,7},{1,0},{2,1},{3,2},{4,3},{5,4},{6,5},{7,6},{8,15},{9,8},{10,9... | collective-permute-start | bytes 294920 | tf_op jit(solution)/shard_map/ppermute | solution.py:310
  58.7 21.4 %collective-permute-start.8 = (f32[3,1,2,16,128]{4,3,2,1,0:T(8,128)S(1)}, f32[3,1,2,16,128]{4,3,2,1,0:T(8,128)S(1)}, u32[]{:S(2)}, u32[]{:S(2)}) collective-permute-start(f32[3,1,2,16,128]{4,3,2,1,0:T(8,128)S(1)} %get-tuple-element.20), channel_id=1, source_target_pairs={{0,8},{8,16},{16,24},{24,0},{1,9},{9,17},{17,25},{25,1},{2,10},{10... | collective-permute-start | bytes 147464 | tf_op jit(solution)/shard_map/ppermute | solution.py:310
  58.7 21.4 %collective-permute-start.9 = (f32[3,1,2,16,128]{4,3,2,1,0:T(8,128)S(1)}, f32[3,1,2,16,128]{4,3,2,1,0:T(8,128)S(1)}, u32[]{:S(2)}, u32[]{:S(2)}) collective-permute-start(f32[3,1,2,16,128]{4,3,2,1,0:T(8,128)S(1)} %get-tuple-element.21), channel_id=1, source_target_pairs={{0,24},{8,0},{16,8},{24,16},{1,25},{9,1},{17,9},{25,17},{2,26},{10... | collective-permute-start | bytes 147464 | tf_op jit(solution)/shard_map/ppermute | solution.py:310
  62.6 17.6 %collective-permute-start.10 = (f32[3,4,1,16,128]{4,3,2,1,0:T(8,128)S(1)}, f32[3,4,1,16,128]{4,3,2,1,0:T(8,128)S(1)}, u32[]{:S(2)}, u32[]{:S(2)}) collective-permute-start(f32[3,4,1,16,128]{4,3,2,1,0:T(8,128)S(1)} %get-tuple-element.22), channel_id=1, source_target_pairs={{0,1},{1,2},{2,3},{3,4},{4,5},{5,6},{6,7},{7,0},{8,9},{9,10},{10,1... | collective-permute-start | bytes 294920 | tf_op jit(solution)/shard_map/ppermute | solution.py:310
  62.6 17.6 %collective-permute-start.11 = (f32[3,4,1,16,128]{4,3,2,1,0:T(8,128)S(1)}, f32[3,4,1,16,128]{4,3,2,1,0:T(8,128)S(1)}, u32[]{:S(2)}, u32[]{:S(2)}) collective-permute-start(f32[3,4,1,16,128]{4,3,2,1,0:T(8,128)S(1)} %get-tuple-element.23), channel_id=1, source_target_pairs={{0,7},{1,0},{2,1},{3,2},{4,3},{5,4},{6,5},{7,6},{8,15},{9,8},{10,9... | collective-permute-start | bytes 294920 | tf_op jit(solution)/shard_map/ppermute | solution.py:310
  80.1 6.5 %copy-start.3 = (bf16[2,128,128]{2,1,0:T(8,128)(2,1)S(1)}, bf16[2,128,128]{2,1,0:T(8,128)(2,1)}, u32[]{:S(2)}) copy-start(bf16[2,128,128]{2,1,0:T(8,128)(2,1)} %constant.16.clone.table) | copy-start | bytes 196612
  86.6 0.9 copy-start
  92.2 22.5 %copy-start.4 = (bf16[2,128,128]{2,1,0:T(8,128)(2,1)S(1)}, bf16[2,128,128]{2,1,0:T(8,128)(2,1)}, u32[]{:S(2)}) copy-start(bf16[2,128,128]{2,1,0:T(8,128)(2,1)} %constant.15.clone.back_turned) | copy-start | bytes 196612
  92.3 22.5 %copy-start.5 = (bf16[2,128,128]{2,1,0:T(8,128)(2,1)S(1)}, bf16[2,128,128]{2,1,0:T(8,128)(2,1)}, u32[]{:S(2)}) copy-start(bf16[2,128,128]{2,1,0:T(8,128)(2,1)} %constant.14.clone.table_turned) | copy-start | bytes 196612
  92.3 22.5 %copy-start.6 = (bf16[2,128,128]{2,1,0:T(8,128)(2,1)S(1)}, bf16[2,128,128]{2,1,0:T(8,128)(2,1)}, u32[]{:S(2)}) copy-start(bf16[2,128,128]{2,1,0:T(8,128)(2,1)} %constant.13.clone.back) | copy-start | bytes 196612
  92.3 22.5 %copy-start.7 = (bf16[2,128,128]{2,1,0:T(8,128)(2,1)S(1)}, bf16[2,128,128]{2,1,0:T(8,128)(2,1)}, u32[]{:S(2)}) copy-start(bf16[2,128,128]{2,1,0:T(8,128)(2,1)} %constant.12.clone.table) | copy-start | bytes 196612
  117.6 24.0 %copy-start.1 = (f32[3,4,2,16,128]{4,3,2,1,0:T(8,128)S(1)}, f32[3,4,2,16,128]{4,3,2,1,0:T(8,128)}, u32[]{:S(2)}) copy-start(f32[3,4,2,16,128]{4,3,2,1,0:T(8,128)} %get-tuple-element.12.place) | copy-start | bytes 589828
  117.6 24.0 %copy-start.8 = (bf16[2,128,128]{2,1,0:T(8,128)(2,1)S(1)}, bf16[2,128,128]{2,1,0:T(8,128)(2,1)}, u32[]{:S(2)}) copy-start(bf16[2,128,128]{2,1,0:T(8,128)(2,1)} %constant.17.clone.table) | copy-start | bytes 196612

commit v7 on v6

--- a/solution.py
+++ b/solution.py
@@ -113,13 +113,13 @@
     slots = blank.shape[1]
     rest = jnp.zeros((slots - 2 * blank.shape[0], 2 * slots), jnp.bfloat16)
     right = jnp.concatenate([jnp.concatenate([blocks[0], blank], 1), jnp.concatenate([blank, blocks[1]], 1), rest], 0)
-    high, low = split_two(jnp.exp2(jnp.dot(side, right, preferred_element_type=jnp.float32)))
+    weights = jnp.concatenate(split_two(jnp.exp2(jnp.dot(side, right, preferred_element_type=jnp.float32))), 0)
+    both = jnp.concatenate(loads, 0)
+    sums = jnp.dot(jnp.concatenate([both, both], 1), weights, preferred_element_type=jnp.float32)
     totals = []
     for which in range(2):
-        lanes = slice(which * slots, (which + 1) * slots)
-        total = jnp.dot(jnp.concatenate([loads[which], loads[which]], 1),
-                        jnp.concatenate([high[:, lanes], low[:, lanes]], 0), preferred_element_type=jnp.float32)
-        total = total[:8] + total[8:]
+        part = sums[which * 16:(which + 1) * 16, which * slots:(which + 1) * slots]
+        total = part[:8] + part[8:]
         if face is not None:
             total = total * flags[(face_id - 1) * cells + starts[which] // 8].astype(jnp.float32)
         totals.append(total)
@@ -236,7 +236,7 @@
                     sums[pl.ds(starts[which], 8), :] = sums[pl.ds(starts[which], 8), :] + gain.folded(which)
         return carry
 
-    lax.fori_loop(0, half, level_of, 0, unroll=2)
+    lax.fori_loop(0, half, level_of, 0, unroll=4)
 
     for ix in range(nx):
         for iy in range(ny):

time: 146 us -> 144 us (0.986)
  Pallas kernels: 75.6 us -> 73.6 us
    pallas_call x3, Pallas kernels: 19.3 us -> 17.2 us  [near_step(): pl.pallas_call(functools.partial(rim_kernel, dims, edges), out_shape=[jax...]
where the time goes in v7:
time: 144 us
  Pallas kernels  73.6 us (51%)
  blocking collectives  46.4 us (32%)
  starting transfers between devices  19.7 us (14%)
  other arithmetic  1.93 us (1%)
    all_to_all x2, blocking collectives, turn(): return lax.all_to_all(lines, axis, split_axis=0, concat_axis=0, tiled=True)  46.4 us
    pallas_call x3, Pallas kernels, near_step(): pl.pallas_call(functools.partial(local_kernel, dims), out_shape=jax.Shape...  44.7 us
    ppermute x12, starting transfers between devices, rim(): lax.ppermute(edges[index], axis, [(i, (i + step) % count) for i in range(...  19.7 us
    pallas_call x3, Pallas kernels, near_step(): pl.pallas_call(functools.partial(rim_kernel, dims, edges), out_shape=[jax...  17.2 us
    pallas_call x3, Pallas kernels, local_call(): pl.pallas_call(kernel, out_shape=jax.ShapeDtypeStruct(shape, jnp.float32)...  11.7 us
  transfers between devices with their start and end apart: 12, of which 0 were waited for; matrix products, arithmetic and copies ran while one was open for 0% of the time, Pallas kernels for 31%

profile of v7, /device:TPU:0, one launch (start us, length us, event | category | flops | bytes accessed | tf_op | source)
XLA Modules:
  0.0 143.8 jit_solution(9655754100953045155)
XLA Ops:
  0.6 0.8 fusion.1
  1.5 0.1 fusion
  1.6 0.0 copy-start.2
  1.6 1.0 broadcast_multiply_fusion
  2.6 0.0 copy-done.2
  2.7 5.1 %collective-permute-start.1 = (f32[7,1,2,16,128]{4,3,2,1,0:T(8,128)S(1)}, f32[7,1,2,16,128]{4,3,2,1,0:T(8,128)S(1)}, u32[]{:S(2)}, u32[]{:S(2)}) collective-permute-start(f32[7,1,2,16,128]{4,3,2,1,0:T(8,128)S(1)} %get-tuple-element.28), channel_id=1, source_target_pairs={{0,24},{8,0},{16,8},{24,16},{1,25},{9,1},{17,9},{25,17},{2,26},{10... | collective-permute-start | bytes 344072 | tf_op jit(solution)/shard_map/ppermute | solution.py:310
  7.8 0.0 collective-permute-start
  7.8 1.7 %collective-permute-start.3 = (f32[7,4,1,16,128]{4,3,2,1,0:T(8,128)S(1)}, f32[7,4,1,16,128]{4,3,2,1,0:T(8,128)S(1)}, u32[]{:S(2)}, u32[]{:S(2)}) collective-permute-start(f32[7,4,1,16,128]{4,3,2,1,0:T(8,128)S(1)} %get-tuple-element.26), channel_id=1, source_target_pairs={{0,7},{1,0},{2,1},{3,2},{4,3},{5,4},{6,5},{7,6},{8,15},{9,8},{10,9... | collective-permute-start | bytes 688136 | tf_op jit(solution)/shard_map/ppermute | solution.py:310
  9.5 0.0 collective-permute-start.2
  9.5 0.1 reshape.24.flags
  9.6 14.9 %near_local.3.part = f32[1024,128]{1,0:T(8,128)S(1)} custom-call(s32[768]{0:T(1024)S(1)} %reshape.24.flags, f32[3,4,2,16,128]{4,3,2,1,0:T(8,128)S(1)} %copy-done.2, f32[7,4,2,16,128]{4,3,2,1,0:T(8,128)S(1)} %pad_maximum_fusion.load), custom_call_target="tpu_custom_call" | custom-call | flops 2952790016 | bytes 4194304 | tf_op jit(solution)/shard_map/near_local/pallas_call | solution.py:278
  24.5 0.0 collective-permute-done.1.place_xh.load_xh
  24.5 0.0 collective-permute-done.place_xl.load_xl
  24.5 0.0 collective-permute-done.3.place_yh.load_yh
  24.5 0.0 collective-permute-done.2.place_yl.load_yl
  24.5 5.7 %near_rim.3 = (f32[3,4,2,16,128]{4,3,2,1,0:T(8,128)S(1)}, f32[3,4,2,16,128]{4,3,2,1,0:T(8,128)}, f32[3,1,2,16,128]{4,3,2,1,0:T(8,128)S(1)}, f32[3,1,2,16,128]{4,...) custom-call(s32[768]{0:T(1024)S(1)} %reshape.24.flags, ...), custom_call_target="tpu_custom_call" | custom-call | flops 805306368 | bytes 4194304 | tf_op jit(solution)/shard_map/near_rim/pallas_call | solution.py:289
  30.2 0.0 collective-permute-start.4
  30.2 3.8 %collective-permute-start.5 = (f32[3,1,2,16,128]{4,3,2,1,0:T(8,128)S(1)}, f32[3,1,2,16,128]{4,3,2,1,0:T(8,128)S(1)}, u32[]{:S(2)}, u32[]{:S(2)}) collective-permute-start(f32[3,1,2,16,128]{4,3,2,1,0:T(8,128)S(1)} %get-tuple-element.16), channel_id=1, source_target_pairs={{0,24},{8,0},{16,8},{24,16},{1,25},{9,1},{17,9},{25,17},{2,26},{10... | collective-permute-start | bytes 147464 | tf_op jit(solution)/shard_map/ppermute | solution.py:310
  34.1 0.0 collective-permute-start.6
  34.1 2.6 %collective-permute-start.7 = (f32[3,4,1,16,128]{4,3,2,1,0:T(8,128)S(1)}, f32[3,4,1,16,128]{4,3,2,1,0:T(8,128)S(1)}, u32[]{:S(2)}, u32[]{:S(2)}) collective-permute-start(f32[3,4,1,16,128]{4,3,2,1,0:T(8,128)S(1)} %get-tuple-element.18), channel_id=1, source_target_pairs={{0,7},{1,0},{2,1},{3,2},{4,3},{5,4},{6,5},{7,6},{8,15},{9,8},{10,9... | collective-permute-start | bytes 294920 | tf_op jit(solution)/shard_map/ppermute | solution.py:310
  36.7 14.9 %near_local.4.part = f32[1024,128]{1,0:T(8,128)S(1)} custom-call(s32[768]{0:T(1024)S(1)} %reshape.24.flags, f32[3,4,2,16,128]{4,3,2,1,0:T(8,128)S(1)} %get-tuple-element.14.place, f32[7,4,2,16,128]{4,3,2,1,0:T(8,128)S(1)} %pad_maximum_fusion.load), custom_call_target="tpu_custom_call" | custom-call | flops 2952790016 | bytes 4194304 | tf_op jit(solution)/shard_map/near_local/pallas_call | solution.py:278
  51.6 0.0 collective-permute-done.4.place_xl
  51.6 0.0 collective-permute-done.5.place_xh
  51.6 0.0 collective-permute-done.6.place_yl
  51.6 0.0 collective-permute-done.7.place_yh
  51.6 5.7 %near_rim.4 = (f32[3,4,2,16,128]{4,3,2,1,0:T(8,128)S(1)}, f32[3,4,2,16,128]{4,3,2,1,0:T(8,128)}, f32[3,1,2,16,128]{4,3,2,1,0:T(8,128)S(1)}, f32[3,1,2,16,128]{4,...) custom-call(s32[768]{0:T(1024)S(1)} %reshape.24.flags, ...), custom_call_target="tpu_custom_call" | custom-call | flops 805306368 | bytes 4194304 | tf_op jit(solution)/shard_map/near_rim/pallas_call | solution.py:289
  57.4 0.0 collective-permute-start.8
  57.4 3.8 %collective-permute-start.9 = (f32[3,1,2,16,128]{4,3,2,1,0:T(8,128)S(1)}, f32[3,1,2,16,128]{4,3,2,1,0:T(8,128)S(1)}, u32[]{:S(2)}, u32[]{:S(2)}) collective-permute-start(f32[3,1,2,16,128]{4,3,2,1,0:T(8,128)S(1)} %get-tuple-element.21), channel_id=1, source_target_pairs={{0,24},{8,0},{16,8},{24,16},{1,25},{9,1},{17,9},{25,17},{2,26},{10... | collective-permute-start | bytes 147464 | tf_op jit(solution)/shard_map/ppermute | solution.py:310
  61.2 0.0 collective-permute-start.10
  61.2 2.6 %collective-permute-start.11 = (f32[3,4,1,16,128]{4,3,2,1,0:T(8,128)S(1)}, f32[3,4,1,16,128]{4,3,2,1,0:T(8,128)S(1)}, u32[]{:S(2)}, u32[]{:S(2)}) collective-permute-start(f32[3,4,1,16,128]{4,3,2,1,0:T(8,128)S(1)} %get-tuple-element.23), channel_id=1, source_target_pairs={{0,7},{1,0},{2,1},{3,2},{4,3},{5,4},{6,5},{7,6},{8,15},{9,8},{10,9... | collective-permute-start | bytes 294920 | tf_op jit(solution)/shard_map/ppermute | solution.py:310
  63.9 14.9 %near_local.5.part = f32[1024,128]{1,0:T(8,128)S(1)} custom-call(s32[768]{0:T(1024)S(1)} %reshape.24.flags, f32[3,4,2,16,128]{4,3,2,1,0:T(8,128)S(1)} %get-tuple-element.19.place, f32[7,4,2,16,128]{4,3,2,1,0:T(8,128)S(1)} %pad_maximum_fusion.load), custom_call_target="tpu_custom_call" | custom-call | flops 2952790016 | bytes 4194304 | tf_op jit(solution)/shard_map/near_local/pallas_call | solution.py:278
  78.8 0.0 copy-start.3
  78.8 0.0 collective-permute-done.8.place_xl
  78.8 0.0 collective-permute-done.9.place_xh
  78.8 0.0 collective-permute-done.10.place_yl
  78.8 5.7 %near_rim.5 = (f32[3,4,2,16,128]{4,3,2,1,0:T(8,128)}, f32[3,4,2,16,128]{4,3,2,1,0:T(8,128)S(1)}) custom-call(s32[768]{0:T(1024)S(1)} %reshape.24.flags, f32[3,4,2,16,128]{4,3,2,1,0:T(8,128)S(1)} %get-tuple-element.19.place, f32[7,4,2,16,128]{4,3,2,1,0:T(8,128)S(1)} %pad_maximum_fusion.load, f32[1024,128]{1,0:T(8,128)S(1)} %near_local.5.part, ...), custom_call_target="tpu_custom_call" | custom-call | flops 805306368 | bytes 4194304 | tf_op jit(solution)/shard_map/near_rim/pallas_call | solution.py:289
  84.6 0.9 copy-done
  85.5 4.8 %spread_third.1 = f32[32,3,1,16,128]{4,3,2,1,0:T(8,128)S(1)} custom-call(f32[3,4,2,16,128]{4,3,2,1,0:T(8,128)S(1)} %copy-done, f32[7,4,2,16,128]{4,3,2,1,0:T(8,128)S(1)} %pad_maximum_fusion.load, bf16[2,128,128]{2,1,0:T(8,128)(2,1)S(1)} %copy-done.3), custom_call_target="tpu_custom_call" | custom-call | tf_op jit(solution)/shard_map/spread_third/pallas_call | solution.py:682
  90.2 0.0 copy-start.4
  90.2 0.0 copy-start.5
  90.3 0.0 copy-start.6
  90.3 0.0 copy-start.7
  90.3 22.5 %all_to_all.10.lines_in = f32[32,3,16,128]{3,2,1,0:T(8,128)S(1)} all-to-all(f32[32,3,16,128]{3,2,1,0:T(8,128)S(1)} %bitcast.2), channel_id=1, replica_groups=mesh['row'=4,'col'=8] {'row','col'}, dimensions={0} | all-to-all | bytes 1572864 | tf_op jit(solution)/shard_map/all_to_all | solution.py:705
  112.8 2.8 %planes_stokes.1 = f32[32,3,16,128]{3,2,1,0:T(8,128)S(1)} custom-call(bf16[2,128,128]{2,1,0:T(8,128)(2,1)S(1)} %copy-done.7, bf16[2,128,128]{2,1,0:T(8,128)(2,1)S(1)} %copy-done.5, bf16[2,128,128]{2,1,0:T(8,128)(2,1)S(1)} %copy-done.6, bf16[2,128,128]{2,1,0:T(8,128)(2,1)S(1)} %copy-done.4, f32[32,3,16,128]{3,2,1,0:T(8,128)S(1)} %all_to_all.10.lines_in), custom_call_target="tpu_custom_call" | custom-call | tf_op jit(solution)/shard_map/planes_stokes/pallas_call | solution.py:682
  115.6 0.0 copy-start.1
  115.6 0.0 copy-start.8
  115.6 24.0 %all_to_all.11 = f32[32,3,16,128]{3,2,1,0:T(8,128)S(1)} all-to-all(f32[32,3,16,128]{3,2,1,0:T(8,128)S(1)} %planes_stokes.1), channel_id=1, replica_groups=mesh['row'=4,'col'=8] {'row','col'}, dimensions={0} | all-to-all | bytes 1572864 | tf_op jit(solution)/shard_map/all_to_all | solution.py:705
  139.6 4.2 %third_gather.1 = f32[3,4,2,16,128]{4,3,2,1,0:T(8,128)} custom-call(f32[3,4,2,16,128]{4,3,2,1,0:T(8,128)S(1)} %copy-done.1, f32[7,4,2,16,128]{4,3,2,1,0:T(8,128)S(1)} %pad_maximum_fusion.load, f32[3,4,2,16,128]{4,3,2,1,0:T(8,128)S(1)} %get-tuple-element.25.near, bf16[2,128,128]{2,1,0:T(8,128)(2,1)S(1)} %copy-done.8, f32[32,3,1,16,128]{4,3,2,1,0:T(8,128)S(1)} %bitcast.3), custom_call_target="tpu_custom_call" | custom-call | tf_op jit(solution)/shard_map/third_gather/pallas_call | solution.py:682
  (16 shorter events, 0.1 us)
Async XLA Ops:
  0.6 0.9 copy-start.10
  1.6 1.0 copy-start.2
  2.7 21.8 %collective-permute-start.1 = (f32[7,1,2,16,128]{4,3,2,1,0:T(8,128)S(1)}, f32[7,1,2,16,128]{4,3,2,1,0:T(8,128)S(1)}, u32[]{:S(2)}, u32[]{:S(2)}) collective-permute-start(f32[7,1,2,16,128]{4,3,2,1,0:T(8,128)S(1)} %get-tuple-element.28), channel_id=1, source_target_pairs={{0,24},{8,0},{16,8},{24,16},{1,25},{9,1},{17,9},{25,17},{2,26},{10... | collective-permute-start | bytes 344072 | tf_op jit(solution)/shard_map/ppermute | solution.py:310
  7.8 1.7 %copy-start.9 = (s32[6,4,2,16]{3,2,1,0:T(2,128)S(1)}, s32[6,4,2,16]{3,2,1,0:T(2,128)}, u32[]{:S(2)}) copy-start(s32[6,4,2,16]{3,2,1,0:T(2,128)} %param.13) | copy-start | bytes 9220
  7.8 16.7 %collective-permute-start = (f32[7,1,2,16,128]{4,3,2,1,0:T(8,128)S(1)}, f32[7,1,2,16,128]{4,3,2,1,0:T(8,128)S(1)}, u32[]{:S(2)}, u32[]{:S(2)}) collective-permute-start(f32[7,1,2,16,128]{4,3,2,1,0:T(8,128)S(1)} %get-tuple-element.29), channel_id=1, source_target_pairs={{0,8},{8,16},{16,24},{24,0},{1,9},{9,17},{17,25},{25,1},{2,10},{10... | collective-permute-start | bytes 344072 | tf_op jit(solution)/shard_map/ppermute | solution.py:310
  7.8 16.7 %collective-permute-start.3 = (f32[7,4,1,16,128]{4,3,2,1,0:T(8,128)S(1)}, f32[7,4,1,16,128]{4,3,2,1,0:T(8,128)S(1)}, u32[]{:S(2)}, u32[]{:S(2)}) collective-permute-start(f32[7,4,1,16,128]{4,3,2,1,0:T(8,128)S(1)} %get-tuple-element.26), channel_id=1, source_target_pairs={{0,7},{1,0},{2,1},{3,2},{4,3},{5,4},{6,5},{7,6},{8,15},{9,8},{10,9... | collective-permute-start | bytes 688136 | tf_op jit(solution)/shard_map/ppermute | solution.py:310
  9.5 15.0 %collective-permute-start.2 = (f32[7,4,1,16,128]{4,3,2,1,0:T(8,128)S(1)}, f32[7,4,1,16,128]{4,3,2,1,0:T(8,128)S(1)}, u32[]{:S(2)}, u32[]{:S(2)}) collective-permute-start(f32[7,4,1,16,128]{4,3,2,1,0:T(8,128)S(1)} %get-tuple-element.27), channel_id=1, source_target_pairs={{0,1},{1,2},{2,3},{3,4},{4,5},{5,6},{6,7},{7,0},{8,9},{9,10},{10,1... | collective-permute-start | bytes 688136 | tf_op jit(solution)/shard_map/ppermute | solution.py:310
  30.2 21.4 %collective-permute-start.4 = (f32[3,1,2,16,128]{4,3,2,1,0:T(8,128)S(1)}, f32[3,1,2,16,128]{4,3,2,1,0:T(8,128)S(1)}, u32[]{:S(2)}, u32[]{:S(2)}) collective-permute-start(f32[3,1,2,16,128]{4,3,2,1,0:T(8,128)S(1)} %get-tuple-element.15), channel_id=1, source_target_pairs={{0,8},{8,16},{16,24},{24,0},{1,9},{9,17},{17,25},{25,1},{2,10},{10... | collective-permute-start | bytes 147464 | tf_op jit(solution)/shard_map/ppermute | solution.py:310
  30.2 21.4 %collective-permute-start.5 = (f32[3,1,2,16,128]{4,3,2,1,0:T(8,128)S(1)}, f32[3,1,2,16,128]{4,3,2,1,0:T(8,128)S(1)}, u32[]{:S(2)}, u32[]{:S(2)}) collective-permute-start(f32[3,1,2,16,128]{4,3,2,1,0:T(8,128)S(1)} %get-tuple-element.16), channel_id=1, source_target_pairs={{0,24},{8,0},{16,8},{24,16},{1,25},{9,1},{17,9},{25,17},{2,26},{10... | collective-permute-start | bytes 147464 | tf_op jit(solution)/shard_map/ppermute | solution.py:310
  34.1 17.6 %collective-permute-start.6 = (f32[3,4,1,16,128]{4,3,2,1,0:T(8,128)S(1)}, f32[3,4,1,16,128]{4,3,2,1,0:T(8,128)S(1)}, u32[]{:S(2)}, u32[]{:S(2)}) collective-permute-start(f32[3,4,1,16,128]{4,3,2,1,0:T(8,128)S(1)} %get-tuple-element.17), channel_id=1, source_target_pairs={{0,1},{1,2},{2,3},{3,4},{4,5},{5,6},{6,7},{7,0},{8,9},{9,10},{10,1... | collective-permute-start | bytes 294920 | tf_op jit(solution)/shard_map/ppermute | solution.py:310
  34.1 17.6 %collective-permute-start.7 = (f32[3,4,1,16,128]{4,3,2,1,0:T(8,128)S(1)}, f32[3,4,1,16,128]{4,3,2,1,0:T(8,128)S(1)}, u32[]{:S(2)}, u32[]{:S(2)}) collective-permute-start(f32[3,4,1,16,128]{4,3,2,1,0:T(8,128)S(1)} %get-tuple-element.18), channel_id=1, source_target_pairs={{0,7},{1,0},{2,1},{3,2},{4,3},{5,4},{6,5},{7,6},{8,15},{9,8},{10,9... | collective-permute-start | bytes 294920 | tf_op jit(solution)/shard_map/ppermute | solution.py:310
  57.4 21.4 %collective-permute-start.8 = (f32[3,1,2,16,128]{4,3,2,1,0:T(8,128)S(1)}, f32[3,1,2,16,128]{4,3,2,1,0:T(8,128)S(1)}, u32[]{:S(2)}, u32[]{:S(2)}) collective-permute-start(f32[3,1,2,16,128]{4,3,2,1,0:T(8,128)S(1)} %get-tuple-element.20), channel_id=1, source_target_pairs={{0,8},{8,16},{16,24},{24,0},{1,9},{9,17},{17,25},{25,1},{2,10},{10... | collective-permute-start | bytes 147464 | tf_op jit(solution)/shard_map/ppermute | solution.py:310
  57.4 21.4 %collective-permute-start.9 = (f32[3,1,2,16,128]{4,3,2,1,0:T(8,128)S(1)}, f32[3,1,2,16,128]{4,3,2,1,0:T(8,128)S(1)}, u32[]{:S(2)}, u32[]{:S(2)}) collective-permute-start(f32[3,1,2,16,128]{4,3,2,1,0:T(8,128)S(1)} %get-tuple-element.21), channel_id=1, source_target_pairs={{0,24},{8,0},{16,8},{24,16},{1,25},{9,1},{17,9},{25,17},{2,26},{10... | collective-permute-start | bytes 147464 | tf_op jit(solution)/shard_map/ppermute | solution.py:310
  61.2 17.6 %collective-permute-start.10 = (f32[3,4,1,16,128]{4,3,2,1,0:T(8,128)S(1)}, f32[3,4,1,16,128]{4,3,2,1,0:T(8,128)S(1)}, u32[]{:S(2)}, u32[]{:S(2)}) collective-permute-start(f32[3,4,1,16,128]{4,3,2,1,0:T(8,128)S(1)} %get-tuple-element.22), channel_id=1, source_target_pairs={{0,1},{1,2},{2,3},{3,4},{4,5},{5,6},{6,7},{7,0},{8,9},{9,10},{10,1... | collective-permute-start | bytes 294920 | tf_op jit(solution)/shard_map/ppermute | solution.py:310
  61.2 17.6 %collective-permute-start.11 = (f32[3,4,1,16,128]{4,3,2,1,0:T(8,128)S(1)}, f32[3,4,1,16,128]{4,3,2,1,0:T(8,128)S(1)}, u32[]{:S(2)}, u32[]{:S(2)}) collective-permute-start(f32[3,4,1,16,128]{4,3,2,1,0:T(8,128)S(1)} %get-tuple-element.23), channel_id=1, source_target_pairs={{0,7},{1,0},{2,1},{3,2},{4,3},{5,4},{6,5},{7,6},{8,15},{9,8},{10,9... | collective-permute-start | bytes 294920 | tf_op jit(solution)/shard_map/ppermute | solution.py:310
  78.8 5.8 %copy-start.3 = (bf16[2,128,128]{2,1,0:T(8,128)(2,1)S(1)}, bf16[2,128,128]{2,1,0:T(8,128)(2,1)}, u32[]{:S(2)}) copy-start(bf16[2,128,128]{2,1,0:T(8,128)(2,1)} %constant.16.clone.table) | copy-start | bytes 196612
  84.6 0.9 copy-start
  90.2 22.5 %copy-start.4 = (bf16[2,128,128]{2,1,0:T(8,128)(2,1)S(1)}, bf16[2,128,128]{2,1,0:T(8,128)(2,1)}, u32[]{:S(2)}) copy-start(bf16[2,128,128]{2,1,0:T(8,128)(2,1)} %constant.15.clone.back_turned) | copy-start | bytes 196612
  90.2 22.5 %copy-start.5 = (bf16[2,128,128]{2,1,0:T(8,128)(2,1)S(1)}, bf16[2,128,128]{2,1,0:T(8,128)(2,1)}, u32[]{:S(2)}) copy-start(bf16[2,128,128]{2,1,0:T(8,128)(2,1)} %constant.14.clone.table_turned) | copy-start | bytes 196612
  90.3 22.5 %copy-start.6 = (bf16[2,128,128]{2,1,0:T(8,128)(2,1)S(1)}, bf16[2,128,128]{2,1,0:T(8,128)(2,1)}, u32[]{:S(2)}) copy-start(bf16[2,128,128]{2,1,0:T(8,128)(2,1)} %constant.13.clone.back) | copy-start | bytes 196612
  90.3 22.5 %copy-start.7 = (bf16[2,128,128]{2,1,0:T(8,128)(2,1)S(1)}, bf16[2,128,128]{2,1,0:T(8,128)(2,1)}, u32[]{:S(2)}) copy-start(bf16[2,128,128]{2,1,0:T(8,128)(2,1)} %constant.12.clone.table) | copy-start | bytes 196612
  115.6 24.0 %copy-start.1 = (f32[3,4,2,16,128]{4,3,2,1,0:T(8,128)S(1)}, f32[3,4,2,16,128]{4,3,2,1,0:T(8,128)}, u32[]{:S(2)}) copy-start(f32[3,4,2,16,128]{4,3,2,1,0:T(8,128)} %get-tuple-element.12.place) | copy-start | bytes 589828
  115.6 24.0 %copy-start.8 = (bf16[2,128,128]{2,1,0:T(8,128)(2,1)S(1)}, bf16[2,128,128]{2,1,0:T(8,128)(2,1)}, u32[]{:S(2)}) copy-start(bf16[2,128,128]{2,1,0:T(8,128)(2,1)} %constant.17.clone.table) | copy-start | bytes 196612

commit v8 on v7

--- a/solution.py
+++ b/solution.py
@@ -106,24 +106,45 @@
     return jnp.concatenate(groups, 0).astype(jnp.bfloat16)
 
 
-def act(side, loads, starts, parts, face_id, flags, cells, target_rows):
-    face = FACES[face_id]
+def pair_weights(side, starts, parts, face, target_rows):
     blocks = [target_block(target_rows, start, part, face) for start, part in zip(starts, parts)]
     blank = jnp.zeros_like(blocks[0])
     slots = blank.shape[1]
     rest = jnp.zeros((slots - 2 * blank.shape[0], 2 * slots), jnp.bfloat16)
     right = jnp.concatenate([jnp.concatenate([blocks[0], blank], 1), jnp.concatenate([blank, blocks[1]], 1), rest], 0)
-    weights = jnp.concatenate(split_two(jnp.exp2(jnp.dot(side, right, preferred_element_type=jnp.float32))), 0)
+    return split_two(jnp.exp2(jnp.dot(side, right, preferred_element_type=jnp.float32)))
+
+
+def gated(total, face_id, flags, cells, start):
+    total = total[:8] + total[8:]
+    if face_id > 0:
+        total = total * flags[(face_id - 1) * cells + start // 8].astype(jnp.float32)
+    return total
+
+
+def ahead(weights, loads, face_id, flags, cells, starts):
+    slots = weights[0].shape[0]
     both = jnp.concatenate(loads, 0)
-    sums = jnp.dot(jnp.concatenate([both, both], 1), weights, preferred_element_type=jnp.float32)
+    sums = jnp.dot(jnp.concatenate([both, both], 1), jnp.concatenate(weights, 0), preferred_element_type=jnp.float32)
+    return [gated(sums[which * 16:(which + 1) * 16, which * slots:(which + 1) * slots], face_id, flags, cells,
+                  starts[which]) for which in range(2)]
+
+
+def behind(weights, loads, face_id, flags, cells, starts):
+    slots = weights[0].shape[0]
     totals = []
     for which in range(2):
-        part = sums[which * 16:(which + 1) * 16, which * slots:(which + 1) * slots]
-        total = part[:8] + part[8:]
-        if face is not None:
-            total = total * flags[(face_id - 1) * cells + starts[which] // 8].astype(jnp.float32)
-        totals.append(total)
+        lanes = slice(which * slots, (which + 1) * slots)
+        sums = lax.dot_general(jnp.concatenate([loads[which]] * 2, 1),
+                               jnp.concatenate([part[:, lanes] for part in weights], 1), (((1,), (1,)), ((), ())),
+                               preferred_element_type=jnp.float32)
+        totals.append(gated(sums, face_id, flags, cells, starts[which]))
     return totals
+
+
+def act(side, loads, starts, parts, face_id, flags, cells, target_rows):
+    weights = pair_weights(side, starts, parts, FACES[face_id], target_rows)
+    return ahead(weights, loads, face_id, flags, cells, starts)
 
 
 class Gain:
@@ -176,25 +197,41 @@
     lax.fori_loop(0, half + 2, turn_level, 0, unroll=5)
 
     def level_of(level, carry):
+        gains = [Gain() for _ in columns]
+        above = []
+        members = [cells_of(column, level) for column in range(len(columns))]
+        starts = [[aligned(cell * 8) for cell in pair] for pair in members]
         for column, (ix, iy) in enumerate(columns):
-            members = cells_of(column, level)
-            starts = [aligned(cell * 8) for cell in members]
-            parts = [target_parts(target_rows, start) for start in starts]
-            gain = Gain()
-            for face_id, face in enumerate(FACES):
+            parts = [target_parts(target_rows, start) for start in starts[column]]
+            mine = [blocks[cell] for cell in members[column]]
+            for face_id in (0, 1, 3, 5):
+                face = FACES[face_id]
                 at = [ix, iy, 0]
                 if face is not None:
-                    at[face[0]] += face[1]
-                if not (0 <= at[0] < nx and 0 <= at[1] < ny):
+                    at[face[0]] += 1
+                if not (at[0] < nx and at[1] < ny):
                     continue
                 other = at[0] * ny + at[1]
-                loads = [blocks[cell] for cell in cells_of(other, level + at[2])]
+                source = cells_of(other, level + at[2])
                 side = sides[other * (half + 2) + level + 1 + at[2]]
-                gain.add(act(side, loads, starts, parts, face_id, flags, cells, target_rows), face)
+                weights = pair_weights(side, starts[column], parts, face, target_rows)
+                gains[column].add(ahead(weights, [blocks[cell] for cell in source], face_id, flags, cells,
+                                        starts[column]), face)
+                if face is None:
+                    continue
+                places = [aligned(cell * 8) for cell in source]
+                back = behind(weights, mine, face_id + 1, flags, cells, places)
+                gain = gains[other]
+                if at[2]:
+                    gain = Gain()
+                    above.append((places, gain))
+                gain.add(back, FACES[face_id + 1])
+        for places, gain in list(zip(starts, gains)) + above:
             for which in range(2):
-                sums[pl.ds(starts[which], 8), :] = gain.folded(which)
+                sums[pl.ds(places[which], 8), :] = sums[pl.ds(places[which], 8), :] + gain.folded(which)
         return carry
 
+    sums[...] = jnp.zeros_like(sums)
     lax.fori_loop(0, half, level_of, 0, unroll=2)
 
 

time: 144 us -> 195 us (1.35)
  Pallas kernels: 73.6 us -> 124 us
    pallas_call x3, Pallas kernels: 44.7 us -> 95.2 us  [near_step(): pl.pallas_call(functools.partial(local_kernel, dims), out_shape=jax.Shape...]
  transfers between devices with their start and end apart: 12 -> 12, of which waited for: 0 -> 0; matrix products, arithmetic and copies ran while one was open for 0% -> 0% of each run, Pallas kernels for 31% -> 49%
where the time goes in v8:
time: 195 us; the launch traced here: 194 us
  Pallas kernels  124 us (64%)
  blocking collectives  46.4 us (24%)
  starting transfers between devices  19.7 us (10%)
    pallas_call x3, Pallas kernels, near_step(): pl.pallas_call(functools.partial(local_kernel, dims), out_shape=jax.Shape...  95.2 us
    all_to_all x2, blocking collectives, turn(): return lax.all_to_all(lines, axis, split_axis=0, concat_axis=0, tiled=True)  46.4 us
    ppermute x12, starting transfers between devices, rim(): lax.ppermute(edges[index], axis, [(i, (i + step) % count) for i in range(...  19.7 us
    pallas_call x3, Pallas kernels, near_step(): pl.pallas_call(functools.partial(rim_kernel, dims, edges), out_shape=[jax...  17.2 us
    pallas_call x3, Pallas kernels, local_call(): pl.pallas_call(kernel, out_shape=jax.ShapeDtypeStruct(shape, jnp.float32)...  11.7 us
  transfers between devices with their start and end apart: 12, of which 0 were waited for; matrix products, arithmetic and copies ran while one was open for 0% of the time, Pallas kernels for 49%

profile of v8, /device:TPU:0, one launch (start us, length us, event | category | flops | bytes accessed | tf_op | source)
XLA Modules:
  0.0 194.3 jit_solution(1976197144930365832)
XLA Ops:
  0.6 0.8 fusion.1
  1.5 0.1 fusion
  1.6 0.0 copy-start.2
  1.6 1.0 broadcast_multiply_fusion
  2.6 0.0 copy-done.2
  2.7 5.1 %collective-permute-start.1 = (f32[7,1,2,16,128]{4,3,2,1,0:T(8,128)S(1)}, f32[7,1,2,16,128]{4,3,2,1,0:T(8,128)S(1)}, u32[]{:S(2)}, u32[]{:S(2)}) collective-permute-start(f32[7,1,2,16,128]{4,3,2,1,0:T(8,128)S(1)} %get-tuple-element.28), channel_id=1, source_target_pairs={{0,24},{8,0},{16,8},{24,16},{1,25},{9,1},{17,9},{25,17},{2,26},{10... | collective-permute-start | bytes 344072 | tf_op jit(solution)/shard_map/ppermute | solution.py:347
  7.8 0.0 collective-permute-start
  7.8 1.7 collective-permute-start.3
  9.5 0.0 collective-permute-start.2
  9.5 0.1 reshape.24.flags
  9.6 31.7 %near_local.3.part = f32[1024,128]{1,0:T(8,128)S(1)} custom-call(s32[768]{0:T(1024)S(1)} %reshape.24.flags, f32[3,4,2,16,128]{4,3,2,1,0:T(8,128)S(1)} %copy-done.2, f32[7,4,2,16,128]{4,3,2,1,0:T(8,128)S(1)} %pad_maximum_fusion.load), custom_call_target="tpu_custom_call" | custom-call | flops 2952790016 | bytes 4194304 | tf_op jit(solution)/shard_map/near_local/pallas_call | solution.py:315
  41.3 0.0 collective-permute-done.1.place_xh.load_xh
  41.3 0.0 collective-permute-done.place_xl.load_xl
  41.3 0.0 collective-permute-done.3.place_yh.load_yh
  41.3 0.0 collective-permute-done.2.place_yl.load_yl
  41.4 5.7 %near_rim.3 = (f32[3,4,2,16,128]{4,3,2,1,0:T(8,128)S(1)}, f32[3,4,2,16,128]{4,3,2,1,0:T(8,128)}, f32[3,1,2,16,128]{4,3,2,1,0:T(8,128)S(1)}, f32[3,1,2,16,128]{4,...) custom-call(s32[768]{0:T(1024)S(1)} %reshape.24.flags, ...), custom_call_target="tpu_custom_call" | custom-call | flops 805306368 | bytes 4194304 | tf_op jit(solution)/shard_map/near_rim/pallas_call | solution.py:326
  47.1 0.0 collective-permute-start.4
  47.1 3.8 %collective-permute-start.5 = (f32[3,1,2,16,128]{4,3,2,1,0:T(8,128)S(1)}, f32[3,1,2,16,128]{4,3,2,1,0:T(8,128)S(1)}, u32[]{:S(2)}, u32[]{:S(2)}) collective-permute-start(f32[3,1,2,16,128]{4,3,2,1,0:T(8,128)S(1)} %get-tuple-element.16), channel_id=1, source_target_pairs={{0,24},{8,0},{16,8},{24,16},{1,25},{9,1},{17,9},{25,17},{2,26},{10... | collective-permute-start | bytes 147464 | tf_op jit(solution)/shard_map/ppermute | solution.py:347
  50.9 0.0 collective-permute-start.6
  50.9 2.6 %collective-permute-start.7 = (f32[3,4,1,16,128]{4,3,2,1,0:T(8,128)S(1)}, f32[3,4,1,16,128]{4,3,2,1,0:T(8,128)S(1)}, u32[]{:S(2)}, u32[]{:S(2)}) collective-permute-start(f32[3,4,1,16,128]{4,3,2,1,0:T(8,128)S(1)} %get-tuple-element.18), channel_id=1, source_target_pairs={{0,7},{1,0},{2,1},{3,2},{4,3},{5,4},{6,5},{7,6},{8,15},{9,8},{10,9... | collective-permute-start | bytes 294920 | tf_op jit(solution)/shard_map/ppermute | solution.py:347
  53.6 31.7 %near_local.4.part = f32[1024,128]{1,0:T(8,128)S(1)} custom-call(s32[768]{0:T(1024)S(1)} %reshape.24.flags, f32[3,4,2,16,128]{4,3,2,1,0:T(8,128)S(1)} %get-tuple-element.14.place, f32[7,4,2,16,128]{4,3,2,1,0:T(8,128)S(1)} %pad_maximum_fusion.load), custom_call_target="tpu_custom_call" | custom-call | flops 2952790016 | bytes 4194304 | tf_op jit(solution)/shard_map/near_local/pallas_call | solution.py:315
  85.3 0.0 collective-permute-done.4.place_xl
  85.3 0.0 collective-permute-done.5.place_xh
  85.3 0.0 collective-permute-done.6.place_yl
  85.3 0.0 collective-permute-done.7.place_yh
  85.4 5.7 %near_rim.4 = (f32[3,4,2,16,128]{4,3,2,1,0:T(8,128)S(1)}, f32[3,4,2,16,128]{4,3,2,1,0:T(8,128)}, f32[3,1,2,16,128]{4,3,2,1,0:T(8,128)S(1)}, f32[3,1,2,16,128]{4,...) custom-call(s32[768]{0:T(1024)S(1)} %reshape.24.flags, ...), custom_call_target="tpu_custom_call" | custom-call | flops 805306368 | bytes 4194304 | tf_op jit(solution)/shard_map/near_rim/pallas_call | solution.py:326
  91.1 0.0 collective-permute-start.8
  91.1 3.8 %collective-permute-start.9 = (f32[3,1,2,16,128]{4,3,2,1,0:T(8,128)S(1)}, f32[3,1,2,16,128]{4,3,2,1,0:T(8,128)S(1)}, u32[]{:S(2)}, u32[]{:S(2)}) collective-permute-start(f32[3,1,2,16,128]{4,3,2,1,0:T(8,128)S(1)} %get-tuple-element.21), channel_id=1, source_target_pairs={{0,24},{8,0},{16,8},{24,16},{1,25},{9,1},{17,9},{25,17},{2,26},{10... | collective-permute-start | bytes 147464 | tf_op jit(solution)/shard_map/ppermute | solution.py:347
  94.9 0.0 collective-permute-start.10
  94.9 2.6 %collective-permute-start.11 = (f32[3,4,1,16,128]{4,3,2,1,0:T(8,128)S(1)}, f32[3,4,1,16,128]{4,3,2,1,0:T(8,128)S(1)}, u32[]{:S(2)}, u32[]{:S(2)}) collective-permute-start(f32[3,4,1,16,128]{4,3,2,1,0:T(8,128)S(1)} %get-tuple-element.23), channel_id=1, source_target_pairs={{0,7},{1,0},{2,1},{3,2},{4,3},{5,4},{6,5},{7,6},{8,15},{9,8},{10,9... | collective-permute-start | bytes 294920 | tf_op jit(solution)/shard_map/ppermute | solution.py:347
  97.6 31.7 %near_local.5.part = f32[1024,128]{1,0:T(8,128)S(1)} custom-call(s32[768]{0:T(1024)S(1)} %reshape.24.flags, f32[3,4,2,16,128]{4,3,2,1,0:T(8,128)S(1)} %get-tuple-element.19.place, f32[7,4,2,16,128]{4,3,2,1,0:T(8,128)S(1)} %pad_maximum_fusion.load), custom_call_target="tpu_custom_call" | custom-call | flops 2952790016 | bytes 4194304 | tf_op jit(solution)/shard_map/near_local/pallas_call | solution.py:315
  129.3 0.0 copy-start.3
  129.3 0.0 collective-permute-done.8.place_xl
  129.3 0.0 collective-permute-done.9.place_xh
  129.4 0.0 collective-permute-done.11.place_yh
  129.4 5.7 %near_rim.5 = (f32[3,4,2,16,128]{4,3,2,1,0:T(8,128)}, f32[3,4,2,16,128]{4,3,2,1,0:T(8,128)S(1)}) custom-call(s32[768]{0:T(1024)S(1)} %reshape.24.flags, f32[3,4,2,16,128]{4,3,2,1,0:T(8,128)S(1)} %get-tuple-element.19.place, f32[7,4,2,16,128]{4,3,2,1,0:T(8,128)S(1)} %pad_maximum_fusion.load, f32[1024,128]{1,0:T(8,128)S(1)} %near_local.5.part, ...), custom_call_target="tpu_custom_call" | custom-call | flops 805306368 | bytes 4194304 | tf_op jit(solution)/shard_map/near_rim/pallas_call | solution.py:326
  135.1 0.9 copy-done
  136.0 4.8 %spread_third.1 = f32[32,3,1,16,128]{4,3,2,1,0:T(8,128)S(1)} custom-call(f32[3,4,2,16,128]{4,3,2,1,0:T(8,128)S(1)} %copy-done, f32[7,4,2,16,128]{4,3,2,1,0:T(8,128)S(1)} %pad_maximum_fusion.load, bf16[2,128,128]{2,1,0:T(8,128)(2,1)S(1)} %copy-done.3), custom_call_target="tpu_custom_call" | custom-call | tf_op jit(solution)/shard_map/spread_third/pallas_call | solution.py:719
  140.8 0.0 copy-start.4
  140.8 0.0 copy-start.5
  140.8 0.0 copy-start.6
  140.8 0.0 copy-start.7
  140.8 22.5 %all_to_all.10.lines_in = f32[32,3,16,128]{3,2,1,0:T(8,128)S(1)} all-to-all(f32[32,3,16,128]{3,2,1,0:T(8,128)S(1)} %bitcast.2), channel_id=1, replica_groups=mesh['row'=4,'col'=8] {'row','col'}, dimensions={0} | all-to-all | bytes 1572864 | tf_op jit(solution)/shard_map/all_to_all | solution.py:742
  163.3 2.8 %planes_stokes.1 = f32[32,3,16,128]{3,2,1,0:T(8,128)S(1)} custom-call(bf16[2,128,128]{2,1,0:T(8,128)(2,1)S(1)} %copy-done.7, bf16[2,128,128]{2,1,0:T(8,128)(2,1)S(1)} %copy-done.5, bf16[2,128,128]{2,1,0:T(8,128)(2,1)S(1)} %copy-done.6, bf16[2,128,128]{2,1,0:T(8,128)(2,1)S(1)} %copy-done.4, f32[32,3,16,128]{3,2,1,0:T(8,128)S(1)} %all_to_all.10.lines_in), custom_call_target="tpu_custom_call" | custom-call | tf_op jit(solution)/shard_map/planes_stokes/pallas_call | solution.py:719
  166.1 0.0 copy-start.1
  166.2 0.0 copy-start.8
  166.2 24.0 %all_to_all.11 = f32[32,3,16,128]{3,2,1,0:T(8,128)S(1)} all-to-all(f32[32,3,16,128]{3,2,1,0:T(8,128)S(1)} %planes_stokes.1), channel_id=1, replica_groups=mesh['row'=4,'col'=8] {'row','col'}, dimensions={0} | all-to-all | bytes 1572864 | tf_op jit(solution)/shard_map/all_to_all | solution.py:742
  190.1 4.2 %third_gather.1 = f32[3,4,2,16,128]{4,3,2,1,0:T(8,128)} custom-call(f32[3,4,2,16,128]{4,3,2,1,0:T(8,128)S(1)} %copy-done.1, f32[7,4,2,16,128]{4,3,2,1,0:T(8,128)S(1)} %pad_maximum_fusion.load, f32[3,4,2,16,128]{4,3,2,1,0:T(8,128)S(1)} %get-tuple-element.25.near, bf16[2,128,128]{2,1,0:T(8,128)(2,1)S(1)} %copy-done.8, f32[32,3,1,16,128]{4,3,2,1,0:T(8,128)S(1)} %bitcast.3), custom_call_target="tpu_custom_call" | custom-call | tf_op jit(solution)/shard_map/third_gather/pallas_call | solution.py:719
  (16 shorter events, 0.1 us)
Async XLA Ops:
  0.6 0.9 copy-start.10
  1.6 1.0 copy-start.2
  2.7 38.7 %collective-permute-start.1 = (f32[7,1,2,16,128]{4,3,2,1,0:T(8,128)S(1)}, f32[7,1,2,16,128]{4,3,2,1,0:T(8,128)S(1)}, u32[]{:S(2)}, u32[]{:S(2)}) collective-permute-start(f32[7,1,2,16,128]{4,3,2,1,0:T(8,128)S(1)} %get-tuple-element.28), channel_id=1, source_target_pairs={{0,24},{8,0},{16,8},{24,16},{1,25},{9,1},{17,9},{25,17},{2,26},{10... | collective-permute-start | bytes 344072 | tf_op jit(solution)/shard_map/ppermute | solution.py:347
  7.8 1.7 copy-start.9
  7.8 33.6 %collective-permute-start = (f32[7,1,2,16,128]{4,3,2,1,0:T(8,128)S(1)}, f32[7,1,2,16,128]{4,3,2,1,0:T(8,128)S(1)}, u32[]{:S(2)}, u32[]{:S(2)}) collective-permute-start(f32[7,1,2,16,128]{4,3,2,1,0:T(8,128)S(1)} %get-tuple-element.29), channel_id=1, source_target_pairs={{0,8},{8,16},{16,24},{24,0},{1,9},{9,17},{17,25},{25,1},{2,10},{10... | collective-permute-start | bytes 344072 | tf_op jit(solution)/shard_map/ppermute | solution.py:347
  7.8 33.5 %collective-permute-start.3 = (f32[7,4,1,16,128]{4,3,2,1,0:T(8,128)S(1)}, f32[7,4,1,16,128]{4,3,2,1,0:T(8,128)S(1)}, u32[]{:S(2)}, u32[]{:S(2)}) collective-permute-start(f32[7,4,1,16,128]{4,3,2,1,0:T(8,128)S(1)} %get-tuple-element.26), channel_id=1, source_target_pairs={{0,7},{1,0},{2,1},{3,2},{4,3},{5,4},{6,5},{7,6},{8,15},{9,8},{10,9... | collective-permute-start | bytes 688136 | tf_op jit(solution)/shard_map/ppermute | solution.py:347
  9.5 31.9 %collective-permute-start.2 = (f32[7,4,1,16,128]{4,3,2,1,0:T(8,128)S(1)}, f32[7,4,1,16,128]{4,3,2,1,0:T(8,128)S(1)}, u32[]{:S(2)}, u32[]{:S(2)}) collective-permute-start(f32[7,4,1,16,128]{4,3,2,1,0:T(8,128)S(1)} %get-tuple-element.27), channel_id=1, source_target_pairs={{0,1},{1,2},{2,3},{3,4},{4,5},{5,6},{6,7},{7,0},{8,9},{9,10},{10,1... | collective-permute-start | bytes 688136 | tf_op jit(solution)/shard_map/ppermute | solution.py:347
  47.1 38.2 %collective-permute-start.4 = (f32[3,1,2,16,128]{4,3,2,1,0:T(8,128)S(1)}, f32[3,1,2,16,128]{4,3,2,1,0:T(8,128)S(1)}, u32[]{:S(2)}, u32[]{:S(2)}) collective-permute-start(f32[3,1,2,16,128]{4,3,2,1,0:T(8,128)S(1)} %get-tuple-element.15), channel_id=1, source_target_pairs={{0,8},{8,16},{16,24},{24,0},{1,9},{9,17},{17,25},{25,1},{2,10},{10... | collective-permute-start | bytes 147464 | tf_op jit(solution)/shard_map/ppermute | solution.py:347
  47.1 38.2 %collective-permute-start.5 = (f32[3,1,2,16,128]{4,3,2,1,0:T(8,128)S(1)}, f32[3,1,2,16,128]{4,3,2,1,0:T(8,128)S(1)}, u32[]{:S(2)}, u32[]{:S(2)}) collective-permute-start(f32[3,1,2,16,128]{4,3,2,1,0:T(8,128)S(1)} %get-tuple-element.16), channel_id=1, source_target_pairs={{0,24},{8,0},{16,8},{24,16},{1,25},{9,1},{17,9},{25,17},{2,26},{10... | collective-permute-start | bytes 147464 | tf_op jit(solution)/shard_map/ppermute | solution.py:347
  50.9 34.4 %collective-permute-start.6 = (f32[3,4,1,16,128]{4,3,2,1,0:T(8,128)S(1)}, f32[3,4,1,16,128]{4,3,2,1,0:T(8,128)S(1)}, u32[]{:S(2)}, u32[]{:S(2)}) collective-permute-start(f32[3,4,1,16,128]{4,3,2,1,0:T(8,128)S(1)} %get-tuple-element.17), channel_id=1, source_target_pairs={{0,1},{1,2},{2,3},{3,4},{4,5},{5,6},{6,7},{7,0},{8,9},{9,10},{10,1... | collective-permute-start | bytes 294920 | tf_op jit(solution)/shard_map/ppermute | solution.py:347
  50.9 34.4 %collective-permute-start.7 = (f32[3,4,1,16,128]{4,3,2,1,0:T(8,128)S(1)}, f32[3,4,1,16,128]{4,3,2,1,0:T(8,128)S(1)}, u32[]{:S(2)}, u32[]{:S(2)}) collective-permute-start(f32[3,4,1,16,128]{4,3,2,1,0:T(8,128)S(1)} %get-tuple-element.18), channel_id=1, source_target_pairs={{0,7},{1,0},{2,1},{3,2},{4,3},{5,4},{6,5},{7,6},{8,15},{9,8},{10,9... | collective-permute-start | bytes 294920 | tf_op jit(solution)/shard_map/ppermute | solution.py:347
  91.1 38.2 %collective-permute-start.8 = (f32[3,1,2,16,128]{4,3,2,1,0:T(8,128)S(1)}, f32[3,1,2,16,128]{4,3,2,1,0:T(8,128)S(1)}, u32[]{:S(2)}, u32[]{:S(2)}) collective-permute-start(f32[3,1,2,16,128]{4,3,2,1,0:T(8,128)S(1)} %get-tuple-element.20), channel_id=1, source_target_pairs={{0,8},{8,16},{16,24},{24,0},{1,9},{9,17},{17,25},{25,1},{2,10},{10... | collective-permute-start | bytes 147464 | tf_op jit(solution)/shard_map/ppermute | solution.py:347
  91.1 38.2 %collective-permute-start.9 = (f32[3,1,2,16,128]{4,3,2,1,0:T(8,128)S(1)}, f32[3,1,2,16,128]{4,3,2,1,0:T(8,128)S(1)}, u32[]{:S(2)}, u32[]{:S(2)}) collective-permute-start(f32[3,1,2,16,128]{4,3,2,1,0:T(8,128)S(1)} %get-tuple-element.21), channel_id=1, source_target_pairs={{0,24},{8,0},{16,8},{24,16},{1,25},{9,1},{17,9},{25,17},{2,26},{10... | collective-permute-start | bytes 147464 | tf_op jit(solution)/shard_map/ppermute | solution.py:347
  94.9 34.4 %collective-permute-start.10 = (f32[3,4,1,16,128]{4,3,2,1,0:T(8,128)S(1)}, f32[3,4,1,16,128]{4,3,2,1,0:T(8,128)S(1)}, u32[]{:S(2)}, u32[]{:S(2)}) collective-permute-start(f32[3,4,1,16,128]{4,3,2,1,0:T(8,128)S(1)} %get-tuple-element.22), channel_id=1, source_target_pairs={{0,1},{1,2},{2,3},{3,4},{4,5},{5,6},{6,7},{7,0},{8,9},{9,10},{10,1... | collective-permute-start | bytes 294920 | tf_op jit(solution)/shard_map/ppermute | solution.py:347
  94.9 34.4 %collective-permute-start.11 = (f32[3,4,1,16,128]{4,3,2,1,0:T(8,128)S(1)}, f32[3,4,1,16,128]{4,3,2,1,0:T(8,128)S(1)}, u32[]{:S(2)}, u32[]{:S(2)}) collective-permute-start(f32[3,4,1,16,128]{4,3,2,1,0:T(8,128)S(1)} %get-tuple-element.23), channel_id=1, source_target_pairs={{0,7},{1,0},{2,1},{3,2},{4,3},{5,4},{6,5},{7,6},{8,15},{9,8},{10,9... | collective-permute-start | bytes 294920 | tf_op jit(solution)/shard_map/ppermute | solution.py:347
  129.3 5.8 %copy-start.3 = (bf16[2,128,128]{2,1,0:T(8,128)(2,1)S(1)}, bf16[2,128,128]{2,1,0:T(8,128)(2,1)}, u32[]{:S(2)}) copy-start(bf16[2,128,128]{2,1,0:T(8,128)(2,1)} %constant.16.clone.table) | copy-start | bytes 196612
  135.1 0.9 copy-start
  140.8 22.5 %copy-start.4 = (bf16[2,128,128]{2,1,0:T(8,128)(2,1)S(1)}, bf16[2,128,128]{2,1,0:T(8,128)(2,1)}, u32[]{:S(2)}) copy-start(bf16[2,128,128]{2,1,0:T(8,128)(2,1)} %constant.15.clone.back_turned) | copy-start | bytes 196612
  140.8 22.5 %copy-start.5 = (bf16[2,128,128]{2,1,0:T(8,128)(2,1)S(1)}, bf16[2,128,128]{2,1,0:T(8,128)(2,1)}, u32[]{:S(2)}) copy-start(bf16[2,128,128]{2,1,0:T(8,128)(2,1)} %constant.14.clone.table_turned) | copy-start | bytes 196612
  140.8 22.5 %copy-start.6 = (bf16[2,128,128]{2,1,0:T(8,128)(2,1)S(1)}, bf16[2,128,128]{2,1,0:T(8,128)(2,1)}, u32[]{:S(2)}) copy-start(bf16[2,128,128]{2,1,0:T(8,128)(2,1)} %constant.13.clone.back) | copy-start | bytes 196612
  140.8 22.5 %copy-start.7 = (bf16[2,128,128]{2,1,0:T(8,128)(2,1)S(1)}, bf16[2,128,128]{2,1,0:T(8,128)(2,1)}, u32[]{:S(2)}) copy-start(bf16[2,128,128]{2,1,0:T(8,128)(2,1)} %constant.12.clone.table) | copy-start | bytes 196612
  166.1 24.0 %copy-start.1 = (f32[3,4,2,16,128]{4,3,2,1,0:T(8,128)S(1)}, f32[3,4,2,16,128]{4,3,2,1,0:T(8,128)}, u32[]{:S(2)}) copy-start(f32[3,4,2,16,128]{4,3,2,1,0:T(8,128)} %get-tuple-element.12.place) | copy-start | bytes 589828
  166.2 24.0 %copy-start.8 = (bf16[2,128,128]{2,1,0:T(8,128)(2,1)S(1)}, bf16[2,128,128]{2,1,0:T(8,128)(2,1)}, u32[]{:S(2)}) copy-start(bf16[2,128,128]{2,1,0:T(8,128)(2,1)} %constant.17.clone.table) | copy-start | bytes 196612
